TPU v7x, 1024 devices: a whole 4x8x16 slice. The times are simulated.
1024 devices in a mesh: level: 8 (over y_hi, core), block: 128 (over y_lo, x, z).
Axes of the slice: x: 4, y: 8 (y_hi: 4, y_lo: 2; y = y_hi * 2 + y_lo), z: 16, core: 2. Of those that a mesh axis runs over, the one named last changes fastest.
Arguments:
- flow_state: float32 [8, 5, 1024, 16, 128], P('level', None, 'block'), as said below
Outputs:
- updated: float32 [8, 5, 1024, 16, 128], P('level', None, 'block')
Inputs may be any that keep to these rules, and one draw needn't show every extreme that they name: `flow_state`: every cell has density between 0.5 and 2.6 and pressure between 0.35 and 1.4, and the velocity along the cells' first dimension lies between 7 and 9.
All inputs are finite; a program needn't handle non-finite values.
Results may differ from a plain program's by a relative error of at most 0.0001.
Values sent between devices are 32-bit elements; how exact they have to be, the bound alone decides.
No kernel may reach another device: no remote copies, remote signals or barrier semaphores. Data moves between devices by JAX's collectives and lax.ppermute only.
A program may use at most 32 MiB of HBM per device.

v0:
```python
import jax
import jax.numpy as jnp
from jax import lax
from jax.sharding import PartitionSpec as P

SWEEPS = 8


GAMMA = 1.4
COURANT = 0.8
SMOOTHING = 2.0


def padded_2(shard, sides, width):
    for axis, dim in sides:
        size, length = (lax.axis_size(axis), shard.shape[dim])
        up = [(i, (i + 1) % size) for i in range(size - 1)]
        down = [(j, i) for i, j in up]
        last = lax.slice_in_dim(shard, length - width, length, axis=dim)
        first = lax.slice_in_dim(shard, 0, width, axis=dim)
        before = lax.ppermute(last, axis, up)
        after = lax.ppermute(first, axis, down)
        shard = jnp.concatenate([before, shard, after], axis=dim)
    return shard


def passed_along(value, axis, steps):
    count = lax.axis_size(axis)
    first, last = (max(0, -steps), min(count, count - steps))
    return lax.ppermute(value, axis, [(source, source + steps) for source in range(first, last)])


def flux_parts(cells, direction):
    density = cells[0]
    velocity = cells[1:4] / density
    pressure = (GAMMA - 1.0) * (cells[4] - 0.5 * density * jnp.sum(velocity * velocity, axis=0))
    sound_speed = jnp.sqrt(GAMMA * pressure / density)
    normal = velocity[direction]
    momentum = cells[1:4] * normal
    momentum = momentum.at[direction].add(pressure)
    flux_vector = jnp.concatenate(
        [cells[1 + direction][None], momentum, ((cells[4] + pressure) * normal)[None]], axis=0
    )
    return (flux_vector, jnp.abs(normal) + sound_speed)


def face_flux(left_state, right_state, direction):
    flux_left, speed_left = flux_parts(left_state, direction)
    flux_right, speed_right = flux_parts(right_state, direction)
    wave_speed = jnp.maximum(speed_left, speed_right)
    return 0.5 * (flux_left + flux_right) - 0.5 * wave_speed * (right_state - left_state)


def trim_others(extended, direction):
    for axis_index in range(1, 4):
        if axis_index != 1 + direction:
            extended = lax.slice_in_dim(
                extended, 1, extended.shape[axis_index] - 1, axis=axis_index
            )
    return extended


def scaled_residual(extended, refinement):
    interior = extended[:, 1:-1, 1:-1, 1:-1]
    divergence = jnp.zeros_like(interior)
    for direction in range(3):
        strip_cells = trim_others(extended, direction)
        length = strip_cells.shape[1 + direction]
        face_values = face_flux(
            lax.slice_in_dim(strip_cells, 0, length - 1, axis=1 + direction),
            lax.slice_in_dim(strip_cells, 1, length, axis=1 + direction),
            direction,
        )
        difference = lax.slice_in_dim(
            face_values, 1, length - 1, axis=1 + direction
        ) - lax.slice_in_dim(face_values, 0, length - 2, axis=1 + direction)
        if direction == 2:
            difference = difference * refinement
        divergence = divergence - difference
    density = interior[0]
    velocity = interior[1:4] / density
    pressure = (GAMMA - 1.0) * (interior[4] - 0.5 * density * jnp.sum(velocity * velocity, axis=0))
    sound_speed = jnp.sqrt(GAMMA * pressure / density)
    wave_rate = (
        jnp.abs(velocity[0])
        + sound_speed
        + (jnp.abs(velocity[1]) + sound_speed)
        + (jnp.abs(velocity[2]) + sound_speed) * refinement
    )
    return COURANT * divergence / wave_rate


def transverse_sum(field):
    padded = jnp.pad(field, ((0, 0), (0, 0), (1, 1), (1, 1)))
    return (
        padded[:, :, 2:, 1:-1]
        + padded[:, :, :-2, 1:-1]
        + padded[:, :, 1:-1, 2:]
        + padded[:, :, 1:-1, :-2]
    )


def shards(flow_state):
    fields = flow_state[0]
    level_index = lax.axis_index("level")
    level_count = lax.axis_size("level")
    block_index = lax.axis_index("block")
    block_count = lax.axis_size("block")
    quarter = fields.shape[3] // 4
    refinement = jnp.left_shift(jnp.int32(1), level_index).astype(jnp.float32)
    halo_state = padded_2(fields, (("block", 1),), 1)
    lower_ghost = jnp.where(block_index == 0, fields[:, :1], halo_state[:, :1])
    upper_ghost = jnp.where(block_index == block_count - 1, fields[:, -1:], halo_state[:, -1:])
    widened = jnp.concatenate([lower_ghost, fields, upper_ghost], axis=1)
    widened = jnp.pad(widened, ((0, 0), (0, 0), (1, 1), (0, 0)), mode="edge")
    planes = jnp.stack([fields[:, :, :, quarter - 1], fields[:, :, :, 3 * quarter]], axis=-1)
    from_coarser = passed_along(planes, "level", 1)
    own_planes = jnp.stack([fields[:, :, :, 0], fields[:, :, :, -1]], axis=-1)
    ghosts = jnp.where(level_index == 0, own_planes, from_coarser)
    ghosts = jnp.pad(ghosts, ((0, 0), (1, 1), (1, 1), (0, 0)), mode="edge")
    extended = jnp.concatenate([ghosts[..., :1], widened, ghosts[..., 1:]], axis=3)
    residual = scaled_residual(extended, refinement)
    averaged = (residual[..., 0::2] + residual[..., 1::2]) * 0.5
    received = passed_along(averaged, "level", -1)
    covered_part = jnp.where(
        level_index == level_count - 1, residual[..., quarter : 3 * quarter], received
    )
    target = jnp.concatenate(
        [residual[..., :quarter], covered_part, residual[..., 3 * quarter :]], axis=3
    )
    correction = jnp.zeros_like(target)
    for sweep_index in range(SWEEPS):
        wide_correction = padded_2(correction, (("block", 1),), 1)
        neighbours = wide_correction[:, 2:] + wide_correction[:, :-2] + transverse_sum(correction)
        correction = (target + SMOOTHING * neighbours) / (1.0 + 6.0 * SMOOTHING)
    covered = correction[..., quarter : 3 * quarter]
    from_parent = passed_along(covered, "level", 1)
    lifted = jnp.repeat(from_parent, 2, axis=3)
    result = fields + correction + lifted
    return result[None]


def solution(mesh):
    in_specs = (P("level", None, "block", None, None),)
    out_specs = P("level", None, "block", None, None)
    return jax.shard_map(shards, mesh=mesh, in_specs=in_specs, out_specs=out_specs, check_vma=False)
```

profile of v0, /device:TPU:40, one launch (start us, length us, event | category | flops | bytes accessed | tf_op | source)
XLA Modules:
  0.0 168.0 jit_solution(4294255398849590747)
XLA Ops:
  0.0 21.2 %collective-permute-start.4 = (f32[5,1,16,128]{3,2,1,0:T(8,128)S(1)}, f32[5,1,16,128]{3,2,1,0:T(8,128)S(1)}, u32[]{:S(2)}, u32[]{:S(2)}) collective-permute-start(f32[5,1,16,128]{3,2,1,0:T(8,128)S(1)} %broadcast.213), channel_id=1, source_target_pairs={{1,0},{2,1},{3,2},{4,3},{5,4},{6,5},{7,6},{8,7},{9,8},{10,9},{11,1... | collective-permute-start | bytes 122888 | tf_op jit(solution)/shard_map/ppermute | solution.py:22
  21.2 1.9 %collective-permute-start.5 = (f32[5,1,16,128]{3,2,1,0:T(8,128)S(1)}, f32[5,1,16,128]{3,2,1,0:T(8,128)S(1)}, u32[]{:S(2)}, u32[]{:S(2)}) collective-permute-start(f32[5,1,16,128]{3,2,1,0:T(8,128)S(1)} %broadcast.213), channel_id=1, source_target_pairs={{0,1},{1,2},{2,3},{3,4},{4,5},{5,6},{6,7},{7,8},{8,9},{9,10},{10,1... | collective-permute-start | bytes 122888 | tf_op jit(solution)/shard_map/ppermute | solution.py:21
  23.1 1.7 %fusion.147 = (f32[5,8,16,1]{3,2,1,0:T(8,128)S(1)}, f32[5,8,16,1]{3,2,1,0:T(8,128)S(1)}, f32[5,8,16,1]{3,2,1,0:T(8,128)S(1)}, f32[5,8,16,1]{3,2,1,0:T(8,128)S(1)}) fusion(f32[5,8,16,128]{3,2,1,0:T(8,128)} %bitcast.109), kind=kLoop, calls=%fused_computation.307 | loop fusion | bytes 20480 | tf_op jit(solution)/shard_map/slice | solution.py:118
  25.5 1.9 %collective-permute-start.2 = (f32[5,8,16,2]{2,1,3,0:T(8,128)S(1)}, f32[5,8,16,2]{2,1,3,0:T(8,128)S(1)}, u32[]{:S(2)}, u32[]{:S(2)}) collective-permute-start(f32[5,8,16,2]{2,1,3,0:T(8,128)S(1)} %pad_maximum_fusion.29), channel_id=1, source_target_pairs={{0,128},{128,256},{256,384},{384,512},{512,640},{640,768},{768,896... | collective-permute-start | bytes 15368 | tf_op jit(solution)/shard_map/ppermute | solution.py:30
  27.4 1.9 %collective-permute-start = (f32[5,1,16,128]{3,2,1,0:T(8,128)S(1)}, f32[5,1,16,128]{3,2,1,0:T(8,128)S(1)}, u32[]{:S(2)}, u32[]{:S(2)}) collective-permute-start(f32[5,1,16,128]{3,2,1,0:T(8,128)S(1)} %get-tuple-element.149), channel_id=1, source_target_pairs={{0,1},{1,2},{2,3},{3,4},{4,5},{5,6},{6,7},{7,8},{8,9},{9,10},{10,1... | collective-permute-start | bytes 122888 | tf_op jit(solution)/shard_map/ppermute | solution.py:21
  29.4 8.1 %collective-permute-start.1 = (f32[5,1,16,128]{3,2,1,0:T(8,128)S(1)}, f32[5,1,16,128]{3,2,1,0:T(8,128)S(1)}, u32[]{:S(2)}, u32[]{:S(2)}) collective-permute-start(f32[5,1,16,128]{3,2,1,0:T(8,128)S(1)} %get-tuple-element.150), channel_id=1, source_target_pairs={{1,0},{2,1},{3,2},{4,3},{5,4},{6,5},{7,6},{8,7},{9,8},{10,9},{11,1... | collective-permute-start | bytes 122888 | tf_op jit(solution)/shard_map/ppermute | solution.py:22
  42.9 5.8 %slice.727 = f32[5,8,16,64]{3,2,1,0:T(8,128)S(1)} slice(f32[5,8,16,128]{3,2,1,0:T(8,128)S(1)} %fusion.101), slice={[0:5:1], [0:8:1], [0:16:1], [0:128:2]} | slice | bytes 327680 | tf_op jit(solution)/shard_map/slice | solution.py:123
  48.7 5.9 %slice.728 = f32[5,8,16,64]{3,2,1,0:T(8,128)S(1)} slice(f32[5,8,16,128]{3,2,1,0:T(8,128)S(1)} %fusion.101), slice={[0:5:1], [0:8:1], [0:16:1], [1:128:2]} | slice | bytes 327680 | tf_op jit(solution)/shard_map/slice | solution.py:123
  54.6 5.5 %collective-permute-start.3 = (f32[5,8,16,64]{3,2,1,0:T(8,128)S(1)}, f32[5,8,16,64]{3,2,1,0:T(8,128)S(1)}, u32[]{:S(2)}, u32[]{:S(2)}) collective-permute-start(f32[5,8,16,64]{3,2,1,0:T(8,128)S(1)} %add_multiply_fusion), channel_id=1, source_target_pairs={{128,0},{256,128},{384,256},{512,384},{640,512},{768,640},{896,768... | collective-permute-start | bytes 491528 | tf_op jit(solution)/shard_map/ppermute | solution.py:30
  60.2 4.4 %collective-permute-done.3 = f32[5,8,16,64]{3,2,1,0:T(8,128)S(1)} collective-permute-done((f32[5,8,16,64]{3,2,1,0:T(8,128)S(1)}, f32[5,8,16,64]{3,2,1,0:T(8,128)S(1)}, u32[]{:S(2)}, u32[]{:S(2)}) %collective-permute-start.3) | collective-permute-done | bytes 163872 | tf_op jit(solution)/shard_map/ppermute | solution.py:30
  65.3 1.9 %collective-permute-start.7 = (f32[5,1,16,128]{3,2,1,0:T(8,128)S(1)}, f32[5,1,16,128]{3,2,1,0:T(8,128)S(1)}, u32[]{:S(2)}, u32[]{:S(2)}) collective-permute-start(f32[5,1,16,128]{3,2,1,0:T(8,128)S(1)} %get-tuple-element.133), channel_id=1, source_target_pairs={{0,1},{1,2},{2,3},{3,4},{4,5},{5,6},{6,7},{7,8},{8,9},{9,10},{10,1... | collective-permute-start | bytes 122888 | tf_op jit(solution)/shard_map/ppermute | solution.py:21
  67.2 8.1 %collective-permute-start.6 = (f32[5,1,16,128]{3,2,1,0:T(8,128)S(1)}, f32[5,1,16,128]{3,2,1,0:T(8,128)S(1)}, u32[]{:S(2)}, u32[]{:S(2)}) collective-permute-start(f32[5,1,16,128]{3,2,1,0:T(8,128)S(1)} %get-tuple-element.132), channel_id=1, source_target_pairs={{1,0},{2,1},{3,2},{4,3},{5,4},{6,5},{7,6},{8,7},{9,8},{10,9},{11,1... | collective-permute-start | bytes 122888 | tf_op jit(solution)/shard_map/ppermute | solution.py:22
  75.4 1.6 collective-permute-done.6
  77.3 1.9 %collective-permute-start.9 = (f32[5,1,16,128]{3,2,1,0:T(8,128)S(1)}, f32[5,1,16,128]{3,2,1,0:T(8,128)S(1)}, u32[]{:S(2)}, u32[]{:S(2)}) collective-permute-start(f32[5,1,16,128]{3,2,1,0:T(8,128)S(1)} %get-tuple-element.131), channel_id=1, source_target_pairs={{0,1},{1,2},{2,3},{3,4},{4,5},{5,6},{6,7},{7,8},{8,9},{9,10},{10,1... | collective-permute-start | bytes 122888 | tf_op jit(solution)/shard_map/ppermute | solution.py:21
  79.2 8.5 %collective-permute-start.8 = (f32[5,1,16,128]{3,2,1,0:T(8,128)S(1)}, f32[5,1,16,128]{3,2,1,0:T(8,128)S(1)}, u32[]{:S(2)}, u32[]{:S(2)}) collective-permute-start(f32[5,1,16,128]{3,2,1,0:T(8,128)S(1)} %get-tuple-element.130), channel_id=1, source_target_pairs={{1,0},{2,1},{3,2},{4,3},{5,4},{6,5},{7,6},{8,7},{9,8},{10,9},{11,1... | collective-permute-start | bytes 122888 | tf_op jit(solution)/shard_map/ppermute | solution.py:22
  87.7 1.6 collective-permute-done.8
  89.6 1.9 %collective-permute-start.11 = (f32[5,1,16,128]{3,2,1,0:T(8,128)S(1)}, f32[5,1,16,128]{3,2,1,0:T(8,128)S(1)}, u32[]{:S(2)}, u32[]{:S(2)}) collective-permute-start(f32[5,1,16,128]{3,2,1,0:T(8,128)S(1)} %get-tuple-element.129), channel_id=1, source_target_pairs={{0,1},{1,2},{2,3},{3,4},{4,5},{5,6},{6,7},{7,8},{8,9},{9,10},{10,1... | collective-permute-start | bytes 122888 | tf_op jit(solution)/shard_map/ppermute | solution.py:21
  91.5 8.5 %collective-permute-start.10 = (f32[5,1,16,128]{3,2,1,0:T(8,128)S(1)}, f32[5,1,16,128]{3,2,1,0:T(8,128)S(1)}, u32[]{:S(2)}, u32[]{:S(2)}) collective-permute-start(f32[5,1,16,128]{3,2,1,0:T(8,128)S(1)} %get-tuple-element.128), channel_id=1, source_target_pairs={{1,0},{2,1},{3,2},{4,3},{5,4},{6,5},{7,6},{8,7},{9,8},{10,9},{11,1... | collective-permute-start | bytes 122888 | tf_op jit(solution)/shard_map/ppermute | solution.py:22
  100.0 1.6 collective-permute-done.10
  101.9 1.9 %collective-permute-start.13 = (f32[5,1,16,128]{3,2,1,0:T(8,128)S(1)}, f32[5,1,16,128]{3,2,1,0:T(8,128)S(1)}, u32[]{:S(2)}, u32[]{:S(2)}) collective-permute-start(f32[5,1,16,128]{3,2,1,0:T(8,128)S(1)} %get-tuple-element.127), channel_id=1, source_target_pairs={{0,1},{1,2},{2,3},{3,4},{4,5},{5,6},{6,7},{7,8},{8,9},{9,10},{10,1... | collective-permute-start | bytes 122888 | tf_op jit(solution)/shard_map/ppermute | solution.py:21
  103.8 8.5 %collective-permute-start.12 = (f32[5,1,16,128]{3,2,1,0:T(8,128)S(1)}, f32[5,1,16,128]{3,2,1,0:T(8,128)S(1)}, u32[]{:S(2)}, u32[]{:S(2)}) collective-permute-start(f32[5,1,16,128]{3,2,1,0:T(8,128)S(1)} %get-tuple-element.126), channel_id=1, source_target_pairs={{1,0},{2,1},{3,2},{4,3},{5,4},{6,5},{7,6},{8,7},{9,8},{10,9},{11,1... | collective-permute-start | bytes 122888 | tf_op jit(solution)/shard_map/ppermute | solution.py:22
  112.3 1.6 collective-permute-done.12
  114.2 1.9 %collective-permute-start.15 = (f32[5,1,16,128]{3,2,1,0:T(8,128)S(1)}, f32[5,1,16,128]{3,2,1,0:T(8,128)S(1)}, u32[]{:S(2)}, u32[]{:S(2)}) collective-permute-start(f32[5,1,16,128]{3,2,1,0:T(8,128)S(1)} %get-tuple-element.125), channel_id=1, source_target_pairs={{0,1},{1,2},{2,3},{3,4},{4,5},{5,6},{6,7},{7,8},{8,9},{9,10},{10,1... | collective-permute-start | bytes 122888 | tf_op jit(solution)/shard_map/ppermute | solution.py:21
  116.1 8.5 %collective-permute-start.14 = (f32[5,1,16,128]{3,2,1,0:T(8,128)S(1)}, f32[5,1,16,128]{3,2,1,0:T(8,128)S(1)}, u32[]{:S(2)}, u32[]{:S(2)}) collective-permute-start(f32[5,1,16,128]{3,2,1,0:T(8,128)S(1)} %get-tuple-element.124), channel_id=1, source_target_pairs={{1,0},{2,1},{3,2},{4,3},{5,4},{6,5},{7,6},{8,7},{9,8},{10,9},{11,1... | collective-permute-start | bytes 122888 | tf_op jit(solution)/shard_map/ppermute | solution.py:22
  124.6 1.6 collective-permute-done.14
  126.5 1.9 %collective-permute-start.17 = (f32[5,1,16,128]{3,2,1,0:T(8,128)S(1)}, f32[5,1,16,128]{3,2,1,0:T(8,128)S(1)}, u32[]{:S(2)}, u32[]{:S(2)}) collective-permute-start(f32[5,1,16,128]{3,2,1,0:T(8,128)S(1)} %get-tuple-element.123), channel_id=1, source_target_pairs={{0,1},{1,2},{2,3},{3,4},{4,5},{5,6},{6,7},{7,8},{8,9},{9,10},{10,1... | collective-permute-start | bytes 122888 | tf_op jit(solution)/shard_map/ppermute | solution.py:21
  128.4 8.5 %collective-permute-start.16 = (f32[5,1,16,128]{3,2,1,0:T(8,128)S(1)}, f32[5,1,16,128]{3,2,1,0:T(8,128)S(1)}, u32[]{:S(2)}, u32[]{:S(2)}) collective-permute-start(f32[5,1,16,128]{3,2,1,0:T(8,128)S(1)} %get-tuple-element.122), channel_id=1, source_target_pairs={{1,0},{2,1},{3,2},{4,3},{5,4},{6,5},{7,6},{8,7},{9,8},{10,9},{11,1... | collective-permute-start | bytes 122888 | tf_op jit(solution)/shard_map/ppermute | solution.py:22
  138.8 1.9 %collective-permute-start.19 = (f32[5,1,16,128]{3,2,1,0:T(8,128)S(1)}, f32[5,1,16,128]{3,2,1,0:T(8,128)S(1)}, u32[]{:S(2)}, u32[]{:S(2)}) collective-permute-start(f32[5,1,16,128]{3,2,1,0:T(8,128)S(1)} %get-tuple-element.121), channel_id=1, source_target_pairs={{0,1},{1,2},{2,3},{3,4},{4,5},{5,6},{6,7},{7,8},{8,9},{9,10},{10,1... | collective-permute-start | bytes 122888 | tf_op jit(solution)/shard_map/ppermute | solution.py:21
  140.7 8.5 %collective-permute-start.18 = (f32[5,1,16,128]{3,2,1,0:T(8,128)S(1)}, f32[5,1,16,128]{3,2,1,0:T(8,128)S(1)}, u32[]{:S(2)}, u32[]{:S(2)}) collective-permute-start(f32[5,1,16,128]{3,2,1,0:T(8,128)S(1)} %get-tuple-element.120), channel_id=1, source_target_pairs={{1,0},{2,1},{3,2},{4,3},{5,4},{6,5},{7,6},{8,7},{9,8},{10,9},{11,1... | collective-permute-start | bytes 122888 | tf_op jit(solution)/shard_map/ppermute | solution.py:22
  151.2 1.9 %collective-permute-start.20 = (f32[5,8,16,64]{3,2,1,0:T(8,128)S(1)}, f32[5,8,16,64]{3,2,1,0:T(8,128)S(1)}, u32[]{:S(2)}, u32[]{:S(2)}) collective-permute-start(f32[5,8,16,64]{3,2,1,0:T(8,128)S(1)} %slice.867), channel_id=1, source_target_pairs={{0,128},{128,256},{256,384},{384,512},{512,640},{640,768},{768,896... | collective-permute-start | bytes 491528 | tf_op jit(solution)/shard_map/ppermute | solution.py:30
  153.2 8.6 %collective-permute-done.20 = f32[5,8,16,64]{3,2,1,0:T(8,128)S(1)} collective-permute-done((f32[5,8,16,64]{3,2,1,0:T(8,128)S(1)}, f32[5,8,16,64]{3,2,1,0:T(8,128)S(1)}, u32[]{:S(2)}, u32[]{:S(2)}) %collective-permute-start.20) | collective-permute-done | bytes 163872 | tf_op jit(solution)/shard_map/ppermute | solution.py:30
  166.2 1.8 %add_bitcast_fusion = f32[1,5,8,16,128]{4,3,2,1,0:T(8,128)} fusion(f32[5,8,16,128]{3,2,1,0:T(8,128)} %copy.257, f32[5,8,16,128]{3,2,1,0:T(8,128)S(1)} %fusion.87, f32[1,5,8,16,128]{4,3,2,1,0:T(8,128)S(1)} %copy-done), kind=kLoop, calls=%fused_computation.200 | loop fusion | flops 163840 | bytes 1310720 | tf_op jit(solution)/shard_map/broadcast_in_dim | solution.py:140
  (87 shorter events, 16.4 us)
Async XLA Ops:
  0.0 64.8 %collective-permute-start.4 = (f32[5,1,16,128]{3,2,1,0:T(8,128)S(1)}, f32[5,1,16,128]{3,2,1,0:T(8,128)S(1)}, u32[]{:S(2)}, u32[]{:S(2)}) collective-permute-start(f32[5,1,16,128]{3,2,1,0:T(8,128)S(1)} %broadcast.213), channel_id=1, source_target_pairs={{1,0},{2,1},{3,2},{4,3},{5,4},{6,5},{7,6},{8,7},{9,8},{10,9},{11,1... | collective-permute-start | bytes 122888 | tf_op jit(solution)/shard_map/ppermute | solution.py:22
  21.2 43.6 %collective-permute-start.5 = (f32[5,1,16,128]{3,2,1,0:T(8,128)S(1)}, f32[5,1,16,128]{3,2,1,0:T(8,128)S(1)}, u32[]{:S(2)}, u32[]{:S(2)}) collective-permute-start(f32[5,1,16,128]{3,2,1,0:T(8,128)S(1)} %broadcast.213), channel_id=1, source_target_pairs={{0,1},{1,2},{2,3},{3,4},{4,5},{5,6},{6,7},{7,8},{8,9},{9,10},{10,1... | collective-permute-start | bytes 122888 | tf_op jit(solution)/shard_map/ppermute | solution.py:21
  23.1 4.3 %copy-start = (f32[1,5,8,16,128]{4,3,2,1,0:T(8,128)S(1)}, f32[1,5,8,16,128]{4,3,2,1,0:T(8,128)}, u32[]{:S(2)}) copy-start(f32[1,5,8,16,128]{4,3,2,1,0:T(8,128)} %param.13) | copy-start | bytes 983044
  25.5 12.8 %collective-permute-start.2 = (f32[5,8,16,2]{2,1,3,0:T(8,128)S(1)}, f32[5,8,16,2]{2,1,3,0:T(8,128)S(1)}, u32[]{:S(2)}, u32[]{:S(2)}) collective-permute-start(f32[5,8,16,2]{2,1,3,0:T(8,128)S(1)} %pad_maximum_fusion.29), channel_id=1, source_target_pairs={{0,128},{128,256},{256,384},{384,512},{512,640},{640,768},{768,896... | collective-permute-start | bytes 15368 | tf_op jit(solution)/shard_map/ppermute | solution.py:30
  27.4 12.1 %collective-permute-start = (f32[5,1,16,128]{3,2,1,0:T(8,128)S(1)}, f32[5,1,16,128]{3,2,1,0:T(8,128)S(1)}, u32[]{:S(2)}, u32[]{:S(2)}) collective-permute-start(f32[5,1,16,128]{3,2,1,0:T(8,128)S(1)} %get-tuple-element.149), channel_id=1, source_target_pairs={{0,1},{1,2},{2,3},{3,4},{4,5},{5,6},{6,7},{7,8},{8,9},{9,10},{10,1... | collective-permute-start | bytes 122888 | tf_op jit(solution)/shard_map/ppermute | solution.py:21
  29.4 10.2 %collective-permute-start.1 = (f32[5,1,16,128]{3,2,1,0:T(8,128)S(1)}, f32[5,1,16,128]{3,2,1,0:T(8,128)S(1)}, u32[]{:S(2)}, u32[]{:S(2)}) collective-permute-start(f32[5,1,16,128]{3,2,1,0:T(8,128)S(1)} %get-tuple-element.150), channel_id=1, source_target_pairs={{1,0},{2,1},{3,2},{4,3},{5,4},{6,5},{7,6},{8,7},{9,8},{10,9},{11,1... | collective-permute-start | bytes 122888 | tf_op jit(solution)/shard_map/ppermute | solution.py:22
  54.6 10.1 %collective-permute-start.3 = (f32[5,8,16,64]{3,2,1,0:T(8,128)S(1)}, f32[5,8,16,64]{3,2,1,0:T(8,128)S(1)}, u32[]{:S(2)}, u32[]{:S(2)}) collective-permute-start(f32[5,8,16,64]{3,2,1,0:T(8,128)S(1)} %add_multiply_fusion), channel_id=1, source_target_pairs={{128,0},{256,128},{384,256},{512,384},{640,512},{768,640},{896,768... | collective-permute-start | bytes 491528 | tf_op jit(solution)/shard_map/ppermute | solution.py:30
  65.3 10.1 %collective-permute-start.7 = (f32[5,1,16,128]{3,2,1,0:T(8,128)S(1)}, f32[5,1,16,128]{3,2,1,0:T(8,128)S(1)}, u32[]{:S(2)}, u32[]{:S(2)}) collective-permute-start(f32[5,1,16,128]{3,2,1,0:T(8,128)S(1)} %get-tuple-element.133), channel_id=1, source_target_pairs={{0,1},{1,2},{2,3},{3,4},{4,5},{5,6},{6,7},{7,8},{8,9},{9,10},{10,1... | collective-permute-start | bytes 122888 | tf_op jit(solution)/shard_map/ppermute | solution.py:21
  67.2 9.8 %collective-permute-start.6 = (f32[5,1,16,128]{3,2,1,0:T(8,128)S(1)}, f32[5,1,16,128]{3,2,1,0:T(8,128)S(1)}, u32[]{:S(2)}, u32[]{:S(2)}) collective-permute-start(f32[5,1,16,128]{3,2,1,0:T(8,128)S(1)} %get-tuple-element.132), channel_id=1, source_target_pairs={{1,0},{2,1},{3,2},{4,3},{5,4},{6,5},{7,6},{8,7},{9,8},{10,9},{11,1... | collective-permute-start | bytes 122888 | tf_op jit(solution)/shard_map/ppermute | solution.py:22
  77.3 10.4 %collective-permute-start.9 = (f32[5,1,16,128]{3,2,1,0:T(8,128)S(1)}, f32[5,1,16,128]{3,2,1,0:T(8,128)S(1)}, u32[]{:S(2)}, u32[]{:S(2)}) collective-permute-start(f32[5,1,16,128]{3,2,1,0:T(8,128)S(1)} %get-tuple-element.131), channel_id=1, source_target_pairs={{0,1},{1,2},{2,3},{3,4},{4,5},{5,6},{6,7},{7,8},{8,9},{9,10},{10,1... | collective-permute-start | bytes 122888 | tf_op jit(solution)/shard_map/ppermute | solution.py:21
  79.2 10.1 %collective-permute-start.8 = (f32[5,1,16,128]{3,2,1,0:T(8,128)S(1)}, f32[5,1,16,128]{3,2,1,0:T(8,128)S(1)}, u32[]{:S(2)}, u32[]{:S(2)}) collective-permute-start(f32[5,1,16,128]{3,2,1,0:T(8,128)S(1)} %get-tuple-element.130), channel_id=1, source_target_pairs={{1,0},{2,1},{3,2},{4,3},{5,4},{6,5},{7,6},{8,7},{9,8},{10,9},{11,1... | collective-permute-start | bytes 122888 | tf_op jit(solution)/shard_map/ppermute | solution.py:22
  89.6 10.4 %collective-permute-start.11 = (f32[5,1,16,128]{3,2,1,0:T(8,128)S(1)}, f32[5,1,16,128]{3,2,1,0:T(8,128)S(1)}, u32[]{:S(2)}, u32[]{:S(2)}) collective-permute-start(f32[5,1,16,128]{3,2,1,0:T(8,128)S(1)} %get-tuple-element.129), channel_id=1, source_target_pairs={{0,1},{1,2},{2,3},{3,4},{4,5},{5,6},{6,7},{7,8},{8,9},{9,10},{10,1... | collective-permute-start | bytes 122888 | tf_op jit(solution)/shard_map/ppermute | solution.py:21
  91.5 10.1 %collective-permute-start.10 = (f32[5,1,16,128]{3,2,1,0:T(8,128)S(1)}, f32[5,1,16,128]{3,2,1,0:T(8,128)S(1)}, u32[]{:S(2)}, u32[]{:S(2)}) collective-permute-start(f32[5,1,16,128]{3,2,1,0:T(8,128)S(1)} %get-tuple-element.128), channel_id=1, source_target_pairs={{1,0},{2,1},{3,2},{4,3},{5,4},{6,5},{7,6},{8,7},{9,8},{10,9},{11,1... | collective-permute-start | bytes 122888 | tf_op jit(solution)/shard_map/ppermute | solution.py:22
  101.9 10.4 %collective-permute-start.13 = (f32[5,1,16,128]{3,2,1,0:T(8,128)S(1)}, f32[5,1,16,128]{3,2,1,0:T(8,128)S(1)}, u32[]{:S(2)}, u32[]{:S(2)}) collective-permute-start(f32[5,1,16,128]{3,2,1,0:T(8,128)S(1)} %get-tuple-element.127), channel_id=1, source_target_pairs={{0,1},{1,2},{2,3},{3,4},{4,5},{5,6},{6,7},{7,8},{8,9},{9,10},{10,1... | collective-permute-start | bytes 122888 | tf_op jit(solution)/shard_map/ppermute | solution.py:21
  103.8 10.1 %collective-permute-start.12 = (f32[5,1,16,128]{3,2,1,0:T(8,128)S(1)}, f32[5,1,16,128]{3,2,1,0:T(8,128)S(1)}, u32[]{:S(2)}, u32[]{:S(2)}) collective-permute-start(f32[5,1,16,128]{3,2,1,0:T(8,128)S(1)} %get-tuple-element.126), channel_id=1, source_target_pairs={{1,0},{2,1},{3,2},{4,3},{5,4},{6,5},{7,6},{8,7},{9,8},{10,9},{11,1... | collective-permute-start | bytes 122888 | tf_op jit(solution)/shard_map/ppermute | solution.py:22
  114.2 10.4 %collective-permute-start.15 = (f32[5,1,16,128]{3,2,1,0:T(8,128)S(1)}, f32[5,1,16,128]{3,2,1,0:T(8,128)S(1)}, u32[]{:S(2)}, u32[]{:S(2)}) collective-permute-start(f32[5,1,16,128]{3,2,1,0:T(8,128)S(1)} %get-tuple-element.125), channel_id=1, source_target_pairs={{0,1},{1,2},{2,3},{3,4},{4,5},{5,6},{6,7},{7,8},{8,9},{9,10},{10,1... | collective-permute-start | bytes 122888 | tf_op jit(solution)/shard_map/ppermute | solution.py:21
  116.1 10.1 %collective-permute-start.14 = (f32[5,1,16,128]{3,2,1,0:T(8,128)S(1)}, f32[5,1,16,128]{3,2,1,0:T(8,128)S(1)}, u32[]{:S(2)}, u32[]{:S(2)}) collective-permute-start(f32[5,1,16,128]{3,2,1,0:T(8,128)S(1)} %get-tuple-element.124), channel_id=1, source_target_pairs={{1,0},{2,1},{3,2},{4,3},{5,4},{6,5},{7,6},{8,7},{9,8},{10,9},{11,1... | collective-permute-start | bytes 122888 | tf_op jit(solution)/shard_map/ppermute | solution.py:22
  126.5 10.4 %collective-permute-start.17 = (f32[5,1,16,128]{3,2,1,0:T(8,128)S(1)}, f32[5,1,16,128]{3,2,1,0:T(8,128)S(1)}, u32[]{:S(2)}, u32[]{:S(2)}) collective-permute-start(f32[5,1,16,128]{3,2,1,0:T(8,128)S(1)} %get-tuple-element.123), channel_id=1, source_target_pairs={{0,1},{1,2},{2,3},{3,4},{4,5},{5,6},{6,7},{7,8},{8,9},{9,10},{10,1... | collective-permute-start | bytes 122888 | tf_op jit(solution)/shard_map/ppermute | solution.py:21
  128.4 10.1 %collective-permute-start.16 = (f32[5,1,16,128]{3,2,1,0:T(8,128)S(1)}, f32[5,1,16,128]{3,2,1,0:T(8,128)S(1)}, u32[]{:S(2)}, u32[]{:S(2)}) collective-permute-start(f32[5,1,16,128]{3,2,1,0:T(8,128)S(1)} %get-tuple-element.122), channel_id=1, source_target_pairs={{1,0},{2,1},{3,2},{4,3},{5,4},{6,5},{7,6},{8,7},{9,8},{10,9},{11,1... | collective-permute-start | bytes 122888 | tf_op jit(solution)/shard_map/ppermute | solution.py:22
  138.8 10.9 %collective-permute-start.19 = (f32[5,1,16,128]{3,2,1,0:T(8,128)S(1)}, f32[5,1,16,128]{3,2,1,0:T(8,128)S(1)}, u32[]{:S(2)}, u32[]{:S(2)}) collective-permute-start(f32[5,1,16,128]{3,2,1,0:T(8,128)S(1)} %get-tuple-element.121), channel_id=1, source_target_pairs={{0,1},{1,2},{2,3},{3,4},{4,5},{5,6},{6,7},{7,8},{8,9},{9,10},{10,1... | collective-permute-start | bytes 122888 | tf_op jit(solution)/shard_map/ppermute | solution.py:21
  140.7 10.1 %collective-permute-start.18 = (f32[5,1,16,128]{3,2,1,0:T(8,128)S(1)}, f32[5,1,16,128]{3,2,1,0:T(8,128)S(1)}, u32[]{:S(2)}, u32[]{:S(2)}) collective-permute-start(f32[5,1,16,128]{3,2,1,0:T(8,128)S(1)} %get-tuple-element.120), channel_id=1, source_target_pairs={{1,0},{2,1},{3,2},{4,3},{5,4},{6,5},{7,6},{8,7},{9,8},{10,9},{11,1... | collective-permute-start | bytes 122888 | tf_op jit(solution)/shard_map/ppermute | solution.py:22
  151.2 10.5 %collective-permute-start.20 = (f32[5,8,16,64]{3,2,1,0:T(8,128)S(1)}, f32[5,8,16,64]{3,2,1,0:T(8,128)S(1)}, u32[]{:S(2)}, u32[]{:S(2)}) collective-permute-start(f32[5,8,16,64]{3,2,1,0:T(8,128)S(1)} %slice.867), channel_id=1, source_target_pairs={{0,128},{128,256},{256,384},{384,512},{512,640},{640,768},{768,896... | collective-permute-start | bytes 491528 | tf_op jit(solution)/shard_map/ppermute | solution.py:30
where the time goes:
time: 169 us; the launch traced here: 168 us
  starting transfers between devices  115 us (68%)
  waiting for transfers between devices  24.6 us (15%)
  local copies, waits for them, and re-layouts  20.4 us (12%)
  other arithmetic  7.55 us (4%)
    ppermute x9, starting transfers between devices, padded_2(): after = lax.ppermute(first, axis, down)  88.2 us
    ppermute x9, starting transfers between devices, padded_2(): before = lax.ppermute(last, axis, up)  17.3 us
    ppermute x3, waiting for transfers between devices, passed_along(): lax.ppermute(value, axis, [(source, source + steps) for source in range(f...  13 us
    slice x2, local copies, waits for them, and re-layouts, shards(): averaged = (residual[..., 0::2] + residual[..., 1::2]) * 0.5  11.6 us
    ppermute x9, waiting for transfers between devices, padded_2(): after = lax.ppermute(first, axis, down)  10.9 us
    ppermute x3, starting transfers between devices, passed_along(): lax.ppermute(value, axis, [(source, source + steps) for source in range(f...  9.31 us
  transfers between devices with their start and end apart: 21, of which 10 were waited for; matrix products, arithmetic and copies ran while one was open for 12% of the time, Pallas kernels for 0%

commit v1 on v0

v1 whole, which is shorter than its diff:
```python
import functools

import jax
import jax.numpy as jnp
import numpy as np
from jax import lax
from jax.experimental import pallas as pl
from jax.experimental.pallas import tpu as pltpu
from jax.sharding import PartitionSpec as P

SWEEPS = 8
GAMMA = 1.4
COURANT = 0.8
SMOOTHING = 2.0
COMPS = 5
ROWS = 8
HALO = SWEEPS - 1
LATE = ROWS
EARLY = ROWS + HALO - 1
F32 = jnp.float32


def lanes(shape):
    return lax.broadcasted_iota(jnp.int32, shape, len(shape) - 1)


def sublanes(shape):
    return lax.broadcasted_iota(jnp.int32, shape, len(shape) - 2)


def lane_roll(x, shift):
    return pltpu.roll(x, shift, x.ndim - 1)


def exact_dot(x, w):
    high = x.astype(jnp.bfloat16)
    rest = x - high.astype(F32)
    mid = rest.astype(jnp.bfloat16)
    low = (rest - mid.astype(F32)).astype(jnp.bfloat16)
    dot = functools.partial(jnp.dot, preferred_element_type=F32)
    return dot(high, w) + dot(mid, w) + dot(low, w)


def primitives(q):
    inverse = 1.0 / q[0]
    v = [q[1] * inverse, q[2] * inverse, q[3] * inverse]
    pressure = (GAMMA - 1.0) * (q[4] - 0.5 * (q[1] * v[0] + q[2] * v[1] + q[3] * v[2]))
    sound = jnp.sqrt(GAMMA * pressure * inverse)
    return v, pressure, sound


def flux(q, normal, pressure, d):
    out = [q[1 + d], q[1] * normal, q[2] * normal, q[3] * normal, (q[4] + pressure) * normal]
    out[1 + d] = out[1 + d] + pressure
    return out


def face(q_left, f_left, s_left, q_right, f_right, s_right):
    speed = jnp.maximum(s_left, s_right)
    return [
        (f_left[c] + f_right[c]) - speed * (q_right[c] - q_left[c]) for c in range(COMPS)
    ]


def axis_flags():
    level = lax.axis_index("level")
    block = lax.axis_index("block")
    refinement = jnp.left_shift(jnp.int32(1), level).astype(F32)
    return level, block, refinement


def residual_kernel(
    n, upper, first_ref, second_ref, w_ref, res_ref, down_ref, up_ref, x_ref
):
    level, block, refinement = axis_flags()
    half, groups = n // 2, -(-n // 8)
    ny, nz = x_ref.shape[2:]
    if upper:
        x_ref[:, :ROWS] = first_ref[...]
        outside = (block == lax.axis_size("block") - 1).astype(jnp.int32)
        edge = jnp.broadcast_to(first_ref[:, ROWS - 1 :], first_ref.shape)
        x_ref[:, ROWS:] = jnp.where(outside == 1, edge, second_ref[...])
    else:
        x_ref[:, ROWS:] = second_ref[...]
        outside = (block == 0).astype(jnp.int32)
        edge = jnp.broadcast_to(second_ref[:, :1], first_ref.shape)
        x_ref[:, :ROWS] = jnp.where(outside == 1, edge, first_ref[...])
    lane, sub = lanes((ny, nz)), sublanes((ny, nz))
    down_ref[COMPS * half :] = jnp.zeros((2, ny, nz), F32)
    up_ref[...] = jnp.zeros(up_ref.shape, F32)

    def load(i):
        return [x_ref[c, i] for c in range(COMPS)]

    def row(i, carried):
        q, v, pressure, sound, face_low = carried
        qn = load(i + 1)
        vn, pn, sn = primitives(qn)
        face_high = face(
            q, flux(q, v[0], pressure, 0), jnp.abs(v[0]) + sound,
            qn, flux(qn, vn[0], pn, 0), jnp.abs(vn[0]) + sn,
        )
        total = [face_low[c] - face_high[c] for c in range(COMPS)]
        f = flux(q, v[1], pressure, 1)
        speed = jnp.abs(v[1]) + sound

        def below(a):
            return jnp.where(sub == 0, a, pltpu.roll(a, 1, 0))

        qb = [below(a) for a in q]
        fb = flux(qb, below(v[1]), below(pressure), 1)
        low = face(qb, fb, below(speed), q, f, speed)
        for c in range(COMPS):
            high = jnp.where(sub == ny - 1, 2.0 * f[c], pltpu.roll(low[c], ny - 1, 0))
            total[c] = total[c] + (low[c] - high)
        f = flux(q, v[2], pressure, 2)
        speed = jnp.abs(v[2]) + sound
        qb = [lane_roll(a, 1) for a in q]
        fb = flux(qb, lane_roll(v[2], 1), lane_roll(pressure, 1), 2)
        low = face(qb, fb, lane_roll(speed, 1), q, f, speed)
        rate = (
            jnp.abs(v[0]) + sound + (jnp.abs(v[1]) + sound) + (jnp.abs(v[2]) + sound) * refinement
        )
        scale = (0.5 * COURANT) / rate
        r = i - 1
        slot = lax.rem(r, 8)
        for c in range(COMPS):
            inner = jnp.where(lane == 0, 0.0, low[c])
            difference = inner - lane_roll(inner, nz - 1)
            value = (total[c] + refinement * difference) * scale
            res_ref[c, r] = value
            strip = jnp.where(lane < 96, lane_roll(value, 64), value)
            strip = lane_roll(strip, lax.rem(slot * 16 + (nz - 88), nz))
            place = up_ref.at[c * groups + r // 8]
            place[...] = jnp.where((lane >= slot * 16) & (lane < slot * 16 + 16), strip, place[...])
            at = 32 * (c % 4) + 2 * r
            ends = down_ref.at[COMPS * half + c // 4]
            moved = lane_roll(q[c], lax.rem(at + 1, nz))
            ends[...] = jnp.where((lane == at) | (lane == at + 1), moved, ends[...])
            planes = up_ref.at[COMPS * groups + c // 4]
            above = lane_roll(q[c], lax.rem(at + 32, nz))
            beneath = lane_roll(q[c], lax.rem(at + 98, nz))
            planes[...] = jnp.where(
                lane == at, above, jnp.where(lane == at + 1, beneath, planes[...])
            )
        return qn, vn, pn, sn, face_high

    q0, q1 = load(0), load(1)
    v0, p0, s0 = primitives(q0)
    v1, p1, s1 = primitives(q1)
    low = face(
        q0, flux(q0, v0[0], p0, 0), jnp.abs(v0[0]) + s0, q1, flux(q1, v1[0], p1, 0), jnp.abs(v1[0]) + s1
    )
    lax.fori_loop(1, n + 1, row, (q1, v1, p1, s1, low))
    for c in range(COMPS):
        a = res_ref[c, :half].reshape(half * ny, nz)
        b = res_ref[c, half:].reshape(half * ny, nz)
        packed = exact_dot(a, w_ref[0]) + exact_dot(b, w_ref[1])
        down_ref[c * half : (c + 1) * half] = packed.reshape(half, ny, nz)


def residuals(n, upper, first, second, weights):
    ny, nz = first.shape[2:]
    half, groups = n // 2, -(-n // 8)
    return pl.pallas_call(
        functools.partial(residual_kernel, n, upper),
        out_shape=(
            jax.ShapeDtypeStruct((COMPS, n, ny, nz), F32),
            jax.ShapeDtypeStruct((COMPS * half + 2, ny, nz), F32),
            jax.ShapeDtypeStruct((COMPS * groups + 2, ny, nz), F32),
        ),
        in_specs=[pl.BlockSpec(memory_space=pltpu.VMEM)] * 3,
        out_specs=(pl.BlockSpec(memory_space=pltpu.VMEM),) * 3,
        scratch_shapes=[pltpu.VMEM((COMPS, 2 * ROWS, ny, nz), F32)],
        name="residual_upper" if upper else "residual_lower",
    )(first, second, weights)


def end_faces(ends, planes, refinement):
    shape = ends[0].shape
    upper = lax.rem(lanes(shape), 2) == 0

    def parts(pack):
        return [pack[0]] + [lane_roll(pack[0], 128 - 32 * c) for c in (1, 2, 3)] + [pack[1]]

    q, g = parts(ends), parts(planes)
    v, pressure, sound = primitives(q)
    vg, pg, sg = primitives(g)
    f, fg = flux(q, v[2], pressure, 2), flux(g, vg[2], pg, 2)
    speed = jnp.maximum(jnp.abs(v[2]) + sound, jnp.abs(vg[2]) + sg)
    rate = jnp.abs(v[0]) + sound + (jnp.abs(v[1]) + sound) + (jnp.abs(v[2]) + sound) * refinement
    scale = (0.5 * COURANT) * refinement / rate
    out = []
    for c in range(COMPS):
        jump = speed * (q[c] - g[c])
        mean = f[c] + fg[c]
        out.append(jnp.where(upper, -(mean + jump), mean - jump) * scale)
    return out


def target_rows(n, offset, flags, res_ref, down_own, up_own, down_got, up_got, t_ref, mask):
    level, refinement, top = flags
    half, groups = n // 2, -(-n // 8)
    ny, nz = t_ref.shape[2:]
    lane = lanes((ny, nz))
    covered = (lane >= 32) & (lane < 96)
    replaced = covered & (jnp.full((ny, nz), top, jnp.int32) == 0)
    ends = [down_own[COMPS * half + k] for k in range(2)]
    planes = [up_own[COMPS * groups + k] for k in range(2)]
    ends_finer = [jnp.where(top == 1, ends[k], down_got[COMPS * half + k]) for k in range(2)]
    planes_coarser = [
        jnp.where(level == 0, ends[k], up_got[COMPS * groups + k]) for k in range(2)
    ]
    fix_own = end_faces(ends, planes_coarser, refinement)
    fix_finer = end_faces(ends_finer, planes, 2.0 * refinement)
    scale = mask * (1.0 / (1.0 + 6.0 * SMOOTHING))

    def one(r, c, average_own, average_got):
        moved = lane_roll(fix_own[c], 127 - 2 * r)
        own = res_ref[c, r] + jnp.where((lane == 0) | (lane == 127), moved, 0.0)
        at32 = lax.rem(32 + 127 - 2 * r, nz)
        at95 = 95 - 2 * r
        got = average_got + jnp.where(
            lane == 32,
            0.5 * lane_roll(fix_finer[c], at32),
            jnp.where(lane == 95, 0.5 * lane_roll(fix_finer[c], at95), 0.0),
        )
        t_ref[c, offset + r] = jnp.where(replaced, got, own) * scale
        inside = average_own + jnp.where(
            lane == 32,
            0.5 * lane_roll(fix_own[c], at32),
            jnp.where(lane == 95, 0.5 * lane_roll(fix_own[c], at95), 0.0),
        )
        strip = lane_roll(up_got[c * groups + r // 8], lax.rem(216 - 16 * lax.rem(r, 8), nz))
        strip = jnp.where(lane < 64, lane_roll(strip, 64), strip)
        t_ref[COMPS + c, offset + r] = jnp.where(covered, inside, strip) * scale

    def pair(r, carried):
        for c in range(COMPS):
            mine, got = down_own[c * half + r], down_got[c * half + r]
            one(r, c, mine, got)
            one(r + half, c, lane_roll(mine, 64), lane_roll(got, 64))
        return carried

    lax.fori_loop(0, half, pair, 0)


def sweep_kernel(
    u_ref, res0, down0, up0, got_down0, got_up0, res1, down1, up1, got_down1, got_up1, w_ref,
    out_ref, t_ref, a_ref, b_ref,
):
    level, block, refinement = axis_flags()
    top = (level == lax.axis_size("level") - 1).astype(jnp.int32)
    keep_low = (block > 0).astype(F32)
    keep_high = (block < lax.axis_size("block") - 1).astype(F32)
    ny, nz = t_ref.shape[2:]
    flags = (level, refinement, top)
    total = 2 * HALO + ROWS
    target_rows(LATE, 0, flags, res0, down0, up0, got_down0, got_up0, t_ref, 1.0)
    target_rows(EARLY, LATE, flags, res1, down1, up1, got_down1, got_up1, t_ref, 1.0)

    def clear(i, carried):
        t_ref[:, i] = t_ref[:, i] * keep_low
        t_ref[:, i + HALO + ROWS] = t_ref[:, i + HALO + ROWS] * keep_high
        return carried

    lax.fori_loop(0, HALO, clear, 0)
    half_shape = (2 * COMPS, ny // 2, nz)
    lane = lanes((1, 1, nz))
    sub = sublanes((1, ny // 2, 1))
    weight = SMOOTHING / (1.0 + 6.0 * SMOOTHING)

    def shifted(x):
        left = jnp.where(lane == 0, 0.0, lane_roll(x, 1))
        right = jnp.where(lane == nz - 1, 0.0, lane_roll(x, nz - 1))
        return left + right

    def sweep(source, dest, s):
        def row(i, carried):
            scale = weight * jnp.where(
                i < HALO, keep_low, jnp.where(i >= HALO + ROWS, keep_high, 1.0)
            )
            low, high = source[:, i, : ny // 2], source[:, i, ny // 2 :]
            low_up, high_up = pltpu.roll(low, 1, 1), pltpu.roll(high, 1, 1)
            low_dn, high_dn = pltpu.roll(low, ny // 2 - 1, 1), pltpu.roll(high, ny // 2 - 1, 1)
            n_low = jnp.where(sub == 0, 0.0, low_up) + jnp.where(sub == ny // 2 - 1, high_dn, low_dn)
            n_high = jnp.where(sub == 0, low_up, high_up) + jnp.where(sub == ny // 2 - 1, 0.0, high_dn)
            n_low = n_low + shifted(low) + (source[:, i - 1, : ny // 2] + source[:, i + 1, : ny // 2])
            n_high = n_high + shifted(high) + (source[:, i - 1, ny // 2 :] + source[:, i + 1, ny // 2 :])
            dest[:, i, : ny // 2] = t_ref[:, i, : ny // 2] + scale * n_low
            dest[:, i, ny // 2 :] = t_ref[:, i, ny // 2 :] + scale * n_high
            return carried

        lax.fori_loop(s - 1, total - s + 1, row, 0)

    buffers = (a_ref, b_ref)
    source = t_ref
    for s in range(2, SWEEPS + 1):
        dest = buffers[s % 2]
        sweep(source, dest, s)
        source = dest
    has_coarser = (level > 0).astype(F32)
    for c in range(COMPS):
        coarse = source[COMPS + c, HALO : HALO + ROWS].reshape(ROWS * ny, nz)
        lifted = exact_dot(coarse, w_ref[2]).reshape(ROWS, ny, nz)
        out_ref[c] = u_ref[c] + source[c, HALO : HALO + ROWS] + lifted * has_coarser


def matrices(nz):
    k = np.arange(nz)
    w = np.zeros((3, nz, nz), np.float32)
    w[0, k, nz // 4 + k // 2] = 0.5
    w[1, k, (3 * nz // 4 + k // 2) % nz] = 0.5
    w[2, nz // 4 + k // 2, k] = 1.0
    return jnp.asarray(w, jnp.bfloat16)


def shards(flow_state):
    fields = flow_state[0]
    ny, nz = fields.shape[2:]
    levels, blocks = lax.axis_size("level"), lax.axis_size("block")
    weights = matrices(nz)
    rise = [(i, i + 1) for i in range(blocks - 1)]
    fall = [(i + 1, i) for i in range(blocks - 1)]
    finer = [(i, i + 1) for i in range(levels - 1)]
    coarser = [(i + 1, i) for i in range(levels - 1)]
    below = lax.ppermute(fields, "block", rise)
    above = lax.ppermute(fields, "block", fall)
    res1, down1, up1 = residuals(EARLY, True, fields, above, weights)
    got_down1 = lax.ppermute(down1, "level", coarser)
    got_up1 = lax.ppermute(up1, "level", finer)
    below, res1 = lax.optimization_barrier((below, res1))
    res0, down0, up0 = residuals(LATE, False, below, fields, weights)
    got_down0 = lax.ppermute(down0, "level", coarser)
    got_up0 = lax.ppermute(up0, "level", finer)
    total = 2 * HALO + ROWS
    out = pl.pallas_call(
        sweep_kernel,
        out_shape=jax.ShapeDtypeStruct(fields.shape, F32),
        in_specs=[pl.BlockSpec(memory_space=pltpu.VMEM)] * 12,
        out_specs=pl.BlockSpec(memory_space=pltpu.VMEM),
        scratch_shapes=[pltpu.VMEM((2 * COMPS, total, ny, nz), F32)] * 3,
        name="sweeps",
    )(fields, res0, down0, up0, got_down0, got_up0, res1, down1, up1, got_down1, got_up1, weights)
    return out[None]


def solution(mesh):
    spec = P("level", None, "block", None, None)
    return jax.shard_map(shards, mesh=mesh, in_specs=(spec,), out_specs=spec, check_vma=False)
```

time: 169 us -> 77.9 us (0.46)
  the two profiles are of different devices: /device:TPU:40 before, /device:TPU:56 now
where the time goes in v1:
time: 77.9 us; the launch traced here: 77.6 us
  starting transfers between devices  33 us (42%)
  Pallas kernels  32.2 us (41%)
  waiting for transfers between devices  10 us (13%)
  local copies, waits for them, and re-layouts  2.26 us (3%)
    ppermute x1, starting transfers between devices, shards(): above = lax.ppermute(fields, 'block', fall)  21.2 us
    pallas_call x1, Pallas kernels, shards(): pl.pallas_call(sweep_kernel, out_shape=jax.ShapeDtypeStruct(fields.shape,...  19.4 us
    pallas_call x2, Pallas kernels, residuals(): pl.pallas_call(functools.partial(residual_kernel, n, upper), out_shape=(j...  12.8 us
    ppermute x1, waiting for transfers between devices, shards(): above = lax.ppermute(fields, 'block', fall)  5.33 us
    ppermute x1, waiting for transfers between devices, shards(): got_up0 = lax.ppermute(up0, 'level', finer)  4.68 us
    ppermute x1, starting transfers between devices, shards(): got_down0 = lax.ppermute(down0, 'level', coarser)  3.45 us
    ppermute x1, starting transfers between devices, shards(): got_down1 = lax.ppermute(down1, 'level', coarser)  2.6 us
    unnamed x14, local copies, waits for them, and re-layouts  2.26 us
  transfers between devices with their start and end apart: 6, of which 2 were waited for; matrix products, arithmetic and copies ran while one was open for 0% of the time, Pallas kernels for 17%

profile of v1, /device:TPU:56, one launch (start us, length us, event | category | flops | bytes accessed | tf_op | source)
XLA Modules:
  0.0 77.6 jit_solution(9502398019319723934)
XLA Ops:
  0.0 21.2 %collective-permute-start.1 = (f32[5,8,16,128]{3,2,1,0:T(8,128)}, f32[5,8,16,128]{3,2,1,0:T(8,128)S(1)}, u32[]{:S(2)}, u32[]{:S(2)}) collective-permute-start(f32[5,8,16,128]{3,2,1,0:T(8,128)} %bitcast.2), channel_id=1, source_target_pairs={{1,0},{2,1},{3,2},{4,3},{5,4},{6,5},{7,6},{8,7},{9,8},{10,9},{11,1... | collective-permute-start | bytes 983048 | tf_op jit(solution)/shard_map/ppermute | solution.py:328
  21.2 1.9 %collective-permute-start = (f32[5,8,16,128]{3,2,1,0:T(8,128)}, f32[5,8,16,128]{3,2,1,0:T(8,128)S(1)}, u32[]{:S(2)}, u32[]{:S(2)}) collective-permute-start(f32[5,8,16,128]{3,2,1,0:T(8,128)} %bitcast.3), channel_id=1, source_target_pairs={{0,1},{1,2},{2,3},{3,4},{4,5},{5,6},{6,7},{7,8},{8,9},{9,10},{10,1... | collective-permute-start | bytes 983048 | tf_op jit(solution)/shard_map/ppermute | solution.py:327
  23.1 5.3 %collective-permute-done.1.second_ref = f32[5,8,16,128]{3,2,1,0:T(8,128)S(1)} collective-permute-done((f32[5,8,16,128]{3,2,1,0:T(8,128)}, f32[5,8,16,128]{3,2,1,0:T(8,128)S(1)}, u32[]{:S(2)}, u32[]{:S(2)}) %collective-permute-start.1) | collective-permute-done | bytes 327712 | tf_op jit(solution)/shard_map/ppermute | solution.py:328
  28.5 0.0 copy-start.1
  28.5 0.7 copy-done.1
  29.2 7.6 %residual_upper.1 = (f32[5,14,16,128]{3,2,1,0:T(8,128)}, f32[37,16,128]{2,1,0:T(8,128)}, f32[12,16,128]{2,1,0:T(8,128)}) custom-call(f32[5,8,16,128]{3,2,1,0:T(8,128)} %bitcast.4, f32[5,8,16,128]{3,2,1,0:T(8,128)} %copy-done.1, bf16[3,128,128]{2,1,0:T(8,128)(2,1)} %constant.2.clone.w_ref), custom_call_target="tpu_custom_call" | custom-call | tf_op jit(solution)/shard_map/residual_upper/pallas_call | solution.py:165
  36.8 2.6 %collective-permute-start.4 = (f32[37,16,128]{2,1,0:T(8,128)}, f32[37,16,128]{2,1,0:T(8,128)S(1)}, u32[]{:S(2)}, u32[]{:S(2)}) collective-permute-start(f32[37,16,128]{2,1,0:T(8,128)} %get-tuple-element.19.down1), channel_id=1, source_target_pairs={{128,0},{256,128},{384,256},{512,384},{640,512},{768,640},{896,768... | collective-permute-start | bytes 909320 | tf_op jit(solution)/shard_map/ppermute | solution.py:330
  39.4 0.0 collective-permute-done.first_ref
  39.4 0.0 copy-start
  39.4 0.7 copy-done
  40.2 0.0 copy-start.4
  40.2 5.2 %residual_lower.1 = (f32[5,8,16,128]{3,2,1,0:T(8,128)}, f32[22,16,128]{2,1,0:T(8,128)}, f32[7,16,128]{2,1,0:T(8,128)}) custom-call(f32[5,8,16,128]{3,2,1,0:T(8,128)} %copy-done, f32[5,8,16,128]{3,2,1,0:T(8,128)} %bitcast.5, bf16[3,128,128]{2,1,0:T(8,128)(2,1)} %constant.2.clone.w_ref), custom_call_target="tpu_custom_call" | custom-call | tf_op jit(solution)/shard_map/residual_lower/pallas_call | solution.py:165
  45.4 3.4 %collective-permute-start.2 = (f32[22,16,128]{2,1,0:T(8,128)}, f32[22,16,128]{2,1,0:T(8,128)S(1)}, u32[]{:S(2)}, u32[]{:S(2)}) collective-permute-start(f32[22,16,128]{2,1,0:T(8,128)} %get-tuple-element.16.down0), channel_id=1, source_target_pairs={{128,0},{256,128},{384,256},{512,384},{640,512},{768,640},{896,768... | collective-permute-start | bytes 540680 | tf_op jit(solution)/shard_map/ppermute | solution.py:334
  48.8 0.0 copy-done.4
  48.8 1.9 %collective-permute-start.5 = (f32[12,16,128]{2,1,0:T(8,128)S(1)}, f32[12,16,128]{2,1,0:T(8,128)S(1)}, u32[]{:S(2)}, u32[]{:S(2)}) collective-permute-start(f32[12,16,128]{2,1,0:T(8,128)S(1)} %copy-done.4), channel_id=1, source_target_pairs={{0,128},{128,256},{256,384},{384,512},{512,640},{640,768},{768,896... | collective-permute-start | bytes 294920 | tf_op jit(solution)/shard_map/ppermute | solution.py:331
  50.8 1.9 %collective-permute-start.3 = (f32[7,16,128]{2,1,0:T(8,128)}, f32[7,16,128]{2,1,0:T(8,128)S(1)}, u32[]{:S(2)}, u32[]{:S(2)}) collective-permute-start(f32[7,16,128]{2,1,0:T(8,128)} %get-tuple-element.17.up0), channel_id=1, source_target_pairs={{0,128},{128,256},{256,384},{384,512},{512,640},{640,768},{768,896... | collective-permute-start | bytes 172040 | tf_op jit(solution)/shard_map/ppermute | solution.py:335
  52.7 4.7 %collective-permute-done.3.got_up0 = f32[7,16,128]{2,1,0:T(8,128)S(1)} collective-permute-done((f32[7,16,128]{2,1,0:T(8,128)}, f32[7,16,128]{2,1,0:T(8,128)S(1)}, u32[]{:S(2)}, u32[]{:S(2)}) %collective-permute-start.3) | collective-permute-done | bytes 57376 | tf_op jit(solution)/shard_map/ppermute | solution.py:335
  57.4 0.0 copy-start.6
  57.4 0.0 collective-permute-done.5.got_up1
  57.4 0.0 copy-start.5
  57.4 0.0 collective-permute-done.2.got_down0
  57.4 0.0 copy-start.3
  57.4 0.0 collective-permute-done.4.got_down1
  57.4 0.0 copy-start.2
  57.4 0.6 copy-done.6
  58.0 0.0 copy-done.5
  58.0 0.1 copy-done.3
  58.1 0.1 copy-done.2
  58.2 19.4 %sweeps.1 = f32[5,8,16,128]{3,2,1,0:T(8,128)} custom-call(f32[5,8,16,128]{3,2,1,0:T(8,128)} %bitcast.6, f32[5,8,16,128]{3,2,1,0:T(8,128)} %get-tuple-element.15.res0, f32[22,16,128]{2,1,0:T(8,128)} %get-tuple-element.16.down0, f32[7,16,128]{2,1,0:T(8,128)} %get-tuple-element.17.up0, f32[22,16,128]{2,1,0:T(8,128)} %copy-done.3, f32[7,16,128]{2,1,0:T(8,128)} %copy-done.6, ...), custom_call_target="tpu_custom_call" | custom-call | tf_op jit(solution)/shard_map/sweeps/pallas_call | solution.py:337
Async XLA Ops:
  0.0 28.5 %collective-permute-start.1 = (f32[5,8,16,128]{3,2,1,0:T(8,128)}, f32[5,8,16,128]{3,2,1,0:T(8,128)S(1)}, u32[]{:S(2)}, u32[]{:S(2)}) collective-permute-start(f32[5,8,16,128]{3,2,1,0:T(8,128)} %bitcast.2), channel_id=1, source_target_pairs={{1,0},{2,1},{3,2},{4,3},{5,4},{6,5},{7,6},{8,7},{9,8},{10,9},{11,1... | collective-permute-start | bytes 983048 | tf_op jit(solution)/shard_map/ppermute | solution.py:328
  21.2 18.2 %collective-permute-start = (f32[5,8,16,128]{3,2,1,0:T(8,128)}, f32[5,8,16,128]{3,2,1,0:T(8,128)S(1)}, u32[]{:S(2)}, u32[]{:S(2)}) collective-permute-start(f32[5,8,16,128]{3,2,1,0:T(8,128)} %bitcast.3), channel_id=1, source_target_pairs={{0,1},{1,2},{2,3},{3,4},{4,5},{5,6},{6,7},{7,8},{8,9},{9,10},{10,1... | collective-permute-start | bytes 983048 | tf_op jit(solution)/shard_map/ppermute | solution.py:327
  28.5 0.7 copy-start.1
  36.8 20.6 %collective-permute-start.4 = (f32[37,16,128]{2,1,0:T(8,128)}, f32[37,16,128]{2,1,0:T(8,128)S(1)}, u32[]{:S(2)}, u32[]{:S(2)}) collective-permute-start(f32[37,16,128]{2,1,0:T(8,128)} %get-tuple-element.19.down1), channel_id=1, source_target_pairs={{128,0},{256,128},{384,256},{512,384},{640,512},{768,640},{896,768... | collective-permute-start | bytes 909320 | tf_op jit(solution)/shard_map/ppermute | solution.py:330
  39.4 0.7 copy-start
  40.2 8.6 %copy-start.4 = (f32[12,16,128]{2,1,0:T(8,128)S(1)}, f32[12,16,128]{2,1,0:T(8,128)}, u32[]{:S(2)}) copy-start(f32[12,16,128]{2,1,0:T(8,128)} %get-tuple-element.20.up1) | copy-start | bytes 294916
  45.4 12.0 %collective-permute-start.2 = (f32[22,16,128]{2,1,0:T(8,128)}, f32[22,16,128]{2,1,0:T(8,128)S(1)}, u32[]{:S(2)}, u32[]{:S(2)}) collective-permute-start(f32[22,16,128]{2,1,0:T(8,128)} %get-tuple-element.16.down0), channel_id=1, source_target_pairs={{128,0},{256,128},{384,256},{512,384},{640,512},{768,640},{896,768... | collective-permute-start | bytes 540680 | tf_op jit(solution)/shard_map/ppermute | solution.py:334
  48.8 8.5 %collective-permute-start.5 = (f32[12,16,128]{2,1,0:T(8,128)S(1)}, f32[12,16,128]{2,1,0:T(8,128)S(1)}, u32[]{:S(2)}, u32[]{:S(2)}) collective-permute-start(f32[12,16,128]{2,1,0:T(8,128)S(1)} %copy-done.4), channel_id=1, source_target_pairs={{0,128},{128,256},{256,384},{384,512},{512,640},{640,768},{768,896... | collective-permute-start | bytes 294920 | tf_op jit(solution)/shard_map/ppermute | solution.py:331
  50.8 6.6 %collective-permute-start.3 = (f32[7,16,128]{2,1,0:T(8,128)}, f32[7,16,128]{2,1,0:T(8,128)S(1)}, u32[]{:S(2)}, u32[]{:S(2)}) collective-permute-start(f32[7,16,128]{2,1,0:T(8,128)} %get-tuple-element.17.up0), channel_id=1, source_target_pairs={{0,128},{128,256},{256,384},{384,512},{512,640},{640,768},{768,896... | collective-permute-start | bytes 172040 | tf_op jit(solution)/shard_map/ppermute | solution.py:335
  57.4 0.6 copy-start.6
  57.4 0.7 copy-start.5
  57.4 0.7 copy-start.3
  57.4 0.8 %copy-start.2 = (f32[37,16,128]{2,1,0:T(8,128)}, f32[37,16,128]{2,1,0:T(8,128)S(1)}, u32[]{:S(2)}) copy-start(f32[37,16,128]{2,1,0:T(8,128)S(1)} %collective-permute-done.4.got_down1) | copy-start | bytes 909316

commit v2 on v1

--- a/solution.py
+++ b/solution.py
@@ -15,6 +15,7 @@
 COMPS = 5
 ROWS = 8
 HALO = SWEEPS - 1
+LINE = 16
 LATE = ROWS
 EARLY = ROWS + HALO - 1
 F32 = jnp.float32
@@ -69,37 +70,66 @@
     return level, block, refinement
 
 
-def residual_kernel(
-    n, upper, first_ref, second_ref, w_ref, res_ref, down_ref, up_ref, x_ref
-):
+def orientation():
+    block = lax.axis_index("block")
+    place = lax.rem(block, LINE)
+    mirrored = (place == LINE - 1).astype(jnp.int32)
+    far = jnp.maximum(mirrored, (place == 0).astype(jnp.int32))
+    lowest = (block == 0).astype(jnp.int32)
+    highest = (block == lax.axis_size("block") - 1).astype(jnp.int32)
+    first_outside = jnp.where(mirrored == 1, lowest, highest)
+    second_outside = jnp.where(mirrored == 1, highest, lowest)
+    return mirrored, far, first_outside, second_outside
+
+
+def oriented(mirrored, j):
+    return jnp.where(mirrored == 1, ROWS - 1 - j, j)
+
+
+def residual_kernel(n, own_ref, near_ref, other_ref, w_ref, *refs):
     level, block, refinement = axis_flags()
+    mirrored, far, first_outside, second_outside = orientation()
+    first = n == EARLY
+    if first:
+        res_ref, down_ref, up_ref, x_ref = refs
+    else:
+        earlier_ref, res_ref, down_ref, sent_ref, x_ref = refs
+        up_ref = sent_ref.at[earlier_ref.shape[0] :]
+        sent_ref[: earlier_ref.shape[0]] = earlier_ref[...]
     half, groups = n // 2, -(-n // 8)
     ny, nz = x_ref.shape[2:]
-    if upper:
-        x_ref[:, :ROWS] = first_ref[...]
-        outside = (block == lax.axis_size("block") - 1).astype(jnp.int32)
-        edge = jnp.broadcast_to(first_ref[:, ROWS - 1 :], first_ref.shape)
-        x_ref[:, ROWS:] = jnp.where(outside == 1, edge, second_ref[...])
-    else:
-        x_ref[:, ROWS:] = second_ref[...]
-        outside = (block == 0).astype(jnp.int32)
-        edge = jnp.broadcast_to(second_ref[:, :1], first_ref.shape)
-        x_ref[:, :ROWS] = jnp.where(outside == 1, edge, first_ref[...])
+    other = mirrored if first else far
+    outside = first_outside if first else second_outside
+    sign = jnp.where(mirrored == 1, -1.0, 1.0).astype(F32)
+    edge = own_ref[:, oriented(mirrored, ROWS - 1 if first else 0)]
+
+    def fetch(j, carried):
+        at = oriented(mirrored, j)
+        halo = jnp.where(other == 1, other_ref[:, at], near_ref[:, at])
+        halo = jnp.where(outside == 1, edge, halo)
+        x_ref[:, j] = own_ref[:, at] if first else halo
+        x_ref[:, ROWS + j] = halo if first else own_ref[:, at]
+        return carried
+
+    lax.fori_loop(0, ROWS, fetch, 0, unroll=4)
     lane, sub = lanes((ny, nz)), sublanes((ny, nz))
     down_ref[COMPS * half :] = jnp.zeros((2, ny, nz), F32)
     up_ref[...] = jnp.zeros(up_ref.shape, F32)
 
     def load(i):
         return [x_ref[c, i] for c in range(COMPS)]
+
+    def along(q, v, pressure):
+        normal = sign * v[0]
+        return [
+            sign * q[1], q[1] * normal + sign * pressure, q[2] * normal, q[3] * normal, (q[4] + pressure) * normal
+        ]
 
     def row(i, carried):
         q, v, pressure, sound, face_low = carried
         qn = load(i + 1)
         vn, pn, sn = primitives(qn)
-        face_high = face(
-            q, flux(q, v[0], pressure, 0), jnp.abs(v[0]) + sound,
-            qn, flux(qn, vn[0], pn, 0), jnp.abs(vn[0]) + sn,
-        )
+        face_high = face(q, along(q, v, pressure), jnp.abs(v[0]) + sound, qn, along(qn, vn, pn), jnp.abs(vn[0]) + sn)
         total = [face_low[c] - face_high[c] for c in range(COMPS)]
         f = flux(q, v[1], pressure, 1)
         speed = jnp.abs(v[1]) + sound
@@ -148,10 +178,8 @@
     q0, q1 = load(0), load(1)
     v0, p0, s0 = primitives(q0)
     v1, p1, s1 = primitives(q1)
-    low = face(
-        q0, flux(q0, v0[0], p0, 0), jnp.abs(v0[0]) + s0, q1, flux(q1, v1[0], p1, 0), jnp.abs(v1[0]) + s1
-    )
-    lax.fori_loop(1, n + 1, row, (q1, v1, p1, s1, low))
+    low = face(q0, along(q0, v0, p0), jnp.abs(v0[0]) + s0, q1, along(q1, v1, p1), jnp.abs(v1[0]) + s1)
+    lax.fori_loop(1, n + 1, row, (q1, v1, p1, s1, low), unroll=2)
     for c in range(COMPS):
         a = res_ref[c, :half].reshape(half * ny, nz)
         b = res_ref[c, half:].reshape(half * ny, nz)
@@ -159,21 +187,23 @@
         down_ref[c * half : (c + 1) * half] = packed.reshape(half, ny, nz)
 
 
-def residuals(n, upper, first, second, weights):
-    ny, nz = first.shape[2:]
+def residuals(n, own, near, other, weights, *earlier):
+    ny, nz = own.shape[2:]
     half, groups = n // 2, -(-n // 8)
+    sent = COMPS * groups + 2 + sum(a.shape[0] for a in earlier)
     return pl.pallas_call(
-        functools.partial(residual_kernel, n, upper),
+        functools.partial(residual_kernel, n),
         out_shape=(
             jax.ShapeDtypeStruct((COMPS, n, ny, nz), F32),
             jax.ShapeDtypeStruct((COMPS * half + 2, ny, nz), F32),
-            jax.ShapeDtypeStruct((COMPS * groups + 2, ny, nz), F32),
+            jax.ShapeDtypeStruct((sent, ny, nz), F32),
         ),
-        in_specs=[pl.BlockSpec(memory_space=pltpu.VMEM)] * 3,
+        in_specs=[pl.BlockSpec(memory_space=pltpu.VMEM)] * (4 + len(earlier)),
         out_specs=(pl.BlockSpec(memory_space=pltpu.VMEM),) * 3,
         scratch_shapes=[pltpu.VMEM((COMPS, 2 * ROWS, ny, nz), F32)],
-        name="residual_upper" if upper else "residual_lower",
-    )(first, second, weights)
+        compiler_params=pltpu.CompilerParams(vmem_limit_bytes=8 * 2**20),
+        name="residual_first" if n == EARLY else "residual_second",
+    )(own, near, other, weights, *earlier)
 
 
 def end_faces(ends, planes, refinement):
@@ -246,18 +276,19 @@
 
 
 def sweep_kernel(
-    u_ref, res0, down0, up0, got_down0, got_up0, res1, down1, up1, got_down1, got_up1, w_ref,
-    out_ref, t_ref, a_ref, b_ref,
+    u_ref, res0, down0, got_down0, res1, down1, got_down1, up, got_up, w_ref, out_ref, t_ref, a_ref, b_ref,
 ):
     level, block, refinement = axis_flags()
     top = (level == lax.axis_size("level") - 1).astype(jnp.int32)
-    keep_low = (block > 0).astype(F32)
-    keep_high = (block < lax.axis_size("block") - 1).astype(F32)
+    mirrored, _, first_outside, second_outside = orientation()
+    keep_low = (second_outside == 0).astype(F32)
+    keep_high = (first_outside == 0).astype(F32)
     ny, nz = t_ref.shape[2:]
     flags = (level, refinement, top)
     total = 2 * HALO + ROWS
-    target_rows(LATE, 0, flags, res0, down0, up0, got_down0, got_up0, t_ref, 1.0)
-    target_rows(EARLY, LATE, flags, res1, down1, up1, got_down1, got_up1, t_ref, 1.0)
+    split = COMPS * -(-EARLY // 8) + 2
+    target_rows(LATE, 0, flags, res0, down0, up.at[split:], got_down0, got_up.at[split:], t_ref, 1.0)
+    target_rows(EARLY, LATE, flags, res1, down1, up, got_down1, got_up, t_ref, 1.0)
 
     def clear(i, carried):
         t_ref[:, i] = t_ref[:, i] * keep_low
@@ -291,7 +322,7 @@
             dest[:, i, ny // 2 :] = t_ref[:, i, ny // 2 :] + scale * n_high
             return carried
 
-        lax.fori_loop(s - 1, total - s + 1, row, 0)
+        lax.fori_loop(s - 1, total - s + 1, row, 0, unroll=4)
 
     buffers = (a_ref, b_ref)
     source = t_ref
@@ -303,7 +334,10 @@
     for c in range(COMPS):
         coarse = source[COMPS + c, HALO : HALO + ROWS].reshape(ROWS * ny, nz)
         lifted = exact_dot(coarse, w_ref[2]).reshape(ROWS, ny, nz)
-        out_ref[c] = u_ref[c] + source[c, HALO : HALO + ROWS] + lifted * has_coarser
+        added = source[c, HALO : HALO + ROWS] + lifted * has_coarser
+        for j in range(ROWS):
+            at = oriented(mirrored, j)
+            out_ref[c, at] = u_ref[c, at] + added[j]
 
 
 def matrices(nz):
@@ -320,28 +354,32 @@
     ny, nz = fields.shape[2:]
     levels, blocks = lax.axis_size("level"), lax.axis_size("block")
     weights = matrices(nz)
-    rise = [(i, i + 1) for i in range(blocks - 1)]
-    fall = [(i + 1, i) for i in range(blocks - 1)]
+    inner = [i for i in range(blocks - 1) if i % LINE != LINE - 1]
+    ends = [i for i in range(blocks - 1) if i % LINE == LINE - 1]
+    rise = [(i, i + 1) for i in inner]
+    fall = [(i + 1, i) for i in inner]
+    swap = [(i, i + 1) for i in ends] + [(i + 1, i) for i in ends]
     finer = [(i, i + 1) for i in range(levels - 1)]
     coarser = [(i + 1, i) for i in range(levels - 1)]
     below = lax.ppermute(fields, "block", rise)
     above = lax.ppermute(fields, "block", fall)
-    res1, down1, up1 = residuals(EARLY, True, fields, above, weights)
+    beyond = lax.ppermute(fields, "block", swap)
+    res1, down1, up1 = residuals(EARLY, fields, above, below, weights)
     got_down1 = lax.ppermute(down1, "level", coarser)
-    got_up1 = lax.ppermute(up1, "level", finer)
-    below, res1 = lax.optimization_barrier((below, res1))
-    res0, down0, up0 = residuals(LATE, False, below, fields, weights)
+    beyond, res1 = lax.optimization_barrier((beyond, res1))
+    res0, down0, up = residuals(LATE, fields, below, beyond, weights, up1)
     got_down0 = lax.ppermute(down0, "level", coarser)
-    got_up0 = lax.ppermute(up0, "level", finer)
+    got_up = lax.ppermute(up, "level", finer)
     total = 2 * HALO + ROWS
     out = pl.pallas_call(
         sweep_kernel,
         out_shape=jax.ShapeDtypeStruct(fields.shape, F32),
-        in_specs=[pl.BlockSpec(memory_space=pltpu.VMEM)] * 12,
+        in_specs=[pl.BlockSpec(memory_space=pltpu.VMEM)] * 10,
         out_specs=pl.BlockSpec(memory_space=pltpu.VMEM),
         scratch_shapes=[pltpu.VMEM((2 * COMPS, total, ny, nz), F32)] * 3,
+        compiler_params=pltpu.CompilerParams(vmem_limit_bytes=16 * 2**20),
         name="sweeps",
-    )(fields, res0, down0, up0, got_down0, got_up0, res1, down1, up1, got_down1, got_up1, weights)
+    )(fields, res0, down0, got_down0, res1, down1, got_down1, up, got_up, weights)
     return out[None]
 
 

time: 77.9 us -> 59.2 us (0.76)
  Pallas kernels: 32.2 us -> 18.4 us
  waiting for transfers between devices: 10 us -> 5.53 us
    ppermute x1, starting transfers between devices: 21.2 us -> 1.28 us  [shards(): above = lax.ppermute(fields, 'block', fall)]
    ppermute x2, starting transfers between devices: 3.84 us -> 20.7 us  [the longest x1 18.8 us: shards(): beyond = lax.ppermute(fields, 'block', swap)]
    pallas_call x1, Pallas kernels: 19.4 us -> 12.3 us  [shards(): pl.pallas_call(sweep_kernel, out_shape=jax.ShapeDtypeStruct(fields.shape,...]
    pallas_call x2, Pallas kernels: 12.8 us -> 6.15 us  [residuals(): pl.pallas_call(functools.partial(residual_kernel, n), out_shape=(jax.Shap...]
    ppermute x1, waiting for transfers between devices: 5.33 us -> 0.01 us  [shards(): above = lax.ppermute(fields, 'block', fall)]
    ppermute x1, starting transfers between devices: 1.92 us -> 4.93 us  [shards(): below = lax.ppermute(fields, 'block', rise)]
    ppermute x2, waiting for transfers between devices: 4.68 us -> 5.52 us  [the longest x1 5.52 us: shards(): got_up = lax.ppermute(up, 'level', finer)]
    unnamed x14 -> x8, local copies, waits for them, and re-layouts: 2.26 us -> 1.9 us
  transfers between devices with their start and end apart: 6 -> 6, of which waited for: 2 -> 1; matrix products, arithmetic and copies ran while one was open for 0% -> 0% of each run, Pallas kernels for 17% -> 10%
where the time goes in v2:
time: 59.2 us; the launch traced here: 58.9 us
  starting transfers between devices  32.9 us (56%)
  Pallas kernels  18.4 us (31%)
  waiting for transfers between devices  5.53 us (9%)
  local copies, waits for them, and re-layouts  1.9 us (3%)
    ppermute x1, starting transfers between devices, shards(): beyond = lax.ppermute(fields, 'block', swap)  18.8 us
    pallas_call x1, Pallas kernels, shards(): pl.pallas_call(sweep_kernel, out_shape=jax.ShapeDtypeStruct(fields.shape,...  12.3 us
    pallas_call x2, Pallas kernels, residuals(): pl.pallas_call(functools.partial(residual_kernel, n), out_shape=(jax.Shap...  6.15 us
    ppermute x1, waiting for transfers between devices, shards(): got_up = lax.ppermute(up, 'level', finer)  5.52 us
    ppermute x1, starting transfers between devices, shards(): below = lax.ppermute(fields, 'block', rise)  4.93 us
    ppermute x1, starting transfers between devices, shards(): got_down0 = lax.ppermute(down0, 'level', coarser)  3.14 us
    ppermute x1, starting transfers between devices, shards(): got_down1 = lax.ppermute(down1, 'level', coarser)  2.92 us
    ppermute x1, starting transfers between devices, shards(): got_up = lax.ppermute(up, 'level', finer)  1.92 us
  transfers between devices with their start and end apart: 6, of which 1 were waited for; matrix products, arithmetic and copies ran while one was open for 0% of the time, Pallas kernels for 10%

profile of v2, /device:TPU:56, one launch (start us, length us, event | category | flops | bytes accessed | tf_op | source)
XLA Modules:
  0.0 58.9 jit_solution(15154318907629688007)
XLA Ops:
  0.0 1.3 %collective-permute-start.2 = (f32[5,8,16,128]{3,2,1,0:T(8,128)}, f32[5,8,16,128]{3,2,1,0:T(8,128)S(1)}, u32[]{:S(2)}, u32[]{:S(2)}) collective-permute-start(f32[5,8,16,128]{3,2,1,0:T(8,128)} %bitcast.2), channel_id=1, source_target_pairs={{1,0},{2,1},{3,2},{4,3},{5,4},{6,5},{7,6},{8,7},{9,8},{10,9},{11,1... | collective-permute-start | bytes 983048 | tf_op jit(solution)/shard_map/ppermute | solution.py:365
  1.3 4.9 %collective-permute-start = (f32[5,8,16,128]{3,2,1,0:T(8,128)}, f32[5,8,16,128]{3,2,1,0:T(8,128)S(1)}, u32[]{:S(2)}, u32[]{:S(2)}) collective-permute-start(f32[5,8,16,128]{3,2,1,0:T(8,128)} %bitcast.3), channel_id=1, source_target_pairs={{0,1},{1,2},{2,3},{3,4},{4,5},{5,6},{6,7},{7,8},{8,9},{9,10},{10,1... | collective-permute-start | bytes 983048 | tf_op jit(solution)/shard_map/ppermute | solution.py:364
  6.2 18.8 %collective-permute-start.1 = (f32[5,8,16,128]{3,2,1,0:T(8,128)}, f32[5,8,16,128]{3,2,1,0:T(8,128)S(1)}, u32[]{:S(2)}, u32[]{:S(2)}) collective-permute-start(f32[5,8,16,128]{3,2,1,0:T(8,128)} %bitcast.4), channel_id=1, source_target_pairs={{15,16},{31,32},{47,48},{63,64},{79,80},{95,96},{111,112},{16,15},... | collective-permute-start | bytes 983048 | tf_op jit(solution)/shard_map/ppermute | solution.py:366
  25.0 0.0 collective-permute-done.2.near_ref
  25.0 0.0 collective-permute-done.other_ref.near_ref
  25.0 0.0 copy-start
  25.0 1.0 %copy-done = f32[1,5,8,16,128]{4,3,2,1,0:T(8,128)S(1)} copy-done((f32[1,5,8,16,128]{4,3,2,1,0:T(8,128)S(1)}, f32[1,5,8,16,128]{4,3,2,1,0:T(8,128)}, u32[]{:S(2)}) %copy-start) | copy-done | bytes 327704
  26.0 0.0 copy-start.2
  26.0 0.9 %copy-done.2 = bf16[3,128,128]{2,1,0:T(8,128)(2,1)S(1)} copy-done((bf16[3,128,128]{2,1,0:T(8,128)(2,1)S(1)}, bf16[3,128,128]{2,1,0:T(8,128)(2,1)}, u32[]{:S(2)}) %copy-start.2) | copy-done | bytes 98328
  26.9 3.8 %residual_first.1 = (f32[5,14,16,128]{3,2,1,0:T(8,128)S(1)}, f32[37,16,128]{2,1,0:T(8,128)S(1)}, f32[12,16,128]{2,1,0:T(8,128)S(1)}) custom-call(f32[5,8,16,128]{3,2,1,0:T(8,128)S(1)} %bitcast.5, f32[5,8,16,128]{3,2,1,0:T(8,128)S(1)} %collective-permute-done.2.near_ref, f32[5,8,16,128]{3,2,1,0:T(8,128)S(1)} %collective-permute-done.other_ref.near_ref, ...), custom_call_target="tpu_custom_call" | custom-call | tf_op jit(solution)/shard_map/residual_first/pallas_call | solution.py:194
  30.8 2.9 %collective-permute-start.4 = (f32[37,16,128]{2,1,0:T(8,128)S(1)}, f32[37,16,128]{2,1,0:T(8,128)S(1)}, u32[]{:S(2)}, u32[]{:S(2)}) collective-permute-start(f32[37,16,128]{2,1,0:T(8,128)S(1)} %get-tuple-element.19.down1), channel_id=1, source_target_pairs={{128,0},{256,128},{384,256},{512,384},{640,512},{768,640},{896,768... | collective-permute-start | bytes 909320 | tf_op jit(solution)/shard_map/ppermute | solution.py:368
  33.7 0.0 collective-permute-done.1.other_ref
  33.7 0.0 copy-start.1
  33.7 0.0 copy-start.3
  33.7 2.3 %residual_second.1 = (f32[5,8,16,128]{3,2,1,0:T(8,128)S(1)}, f32[22,16,128]{2,1,0:T(8,128)S(1)}, f32[19,16,128]{2,1,0:T(8,128)S(1)}) custom-call(f32[5,8,16,128]{3,2,1,0:T(8,128)S(1)} %bitcast.6, f32[5,8,16,128]{3,2,1,0:T(8,128)S(1)} %collective-permute-done.other_ref.near_ref, f32[5,8,16,128]{3,2,1,0:T(8,128)S(1)} %collective-permute-done.1.other_ref, ...), custom_call_target="tpu_custom_call" | custom-call | tf_op jit(solution)/shard_map/residual_second/pallas_call | solution.py:194
  36.0 3.1 %collective-permute-start.3 = (f32[22,16,128]{2,1,0:T(8,128)S(1)}, f32[22,16,128]{2,1,0:T(8,128)S(1)}, u32[]{:S(2)}, u32[]{:S(2)}) collective-permute-start(f32[22,16,128]{2,1,0:T(8,128)S(1)} %get-tuple-element.17.down0), channel_id=1, source_target_pairs={{128,0},{256,128},{384,256},{512,384},{640,512},{768,640},{896,768... | collective-permute-start | bytes 540680 | tf_op jit(solution)/shard_map/ppermute | solution.py:371
  39.2 1.9 %collective-permute-start.5 = (f32[19,16,128]{2,1,0:T(8,128)S(1)}, f32[19,16,128]{2,1,0:T(8,128)S(1)}, u32[]{:S(2)}, u32[]{:S(2)}) collective-permute-start(f32[19,16,128]{2,1,0:T(8,128)S(1)} %get-tuple-element.20.up), channel_id=1, source_target_pairs={{0,128},{128,256},{256,384},{384,512},{512,640},{640,768},{768,896... | collective-permute-start | bytes 466952 | tf_op jit(solution)/shard_map/ppermute | solution.py:372
  41.1 5.5 %collective-permute-done.5.got_up = f32[19,16,128]{2,1,0:T(8,128)S(1)} collective-permute-done((f32[19,16,128]{2,1,0:T(8,128)S(1)}, f32[19,16,128]{2,1,0:T(8,128)S(1)}, u32[]{:S(2)}, u32[]{:S(2)}) %collective-permute-start.5) | collective-permute-done | bytes 155680 | tf_op jit(solution)/shard_map/ppermute | solution.py:372
  46.6 0.0 collective-permute-done.3.got_down0
  46.6 0.0 collective-permute-done.4.got_down1
  46.6 0.0 copy-done.1
  46.6 0.0 copy-done.3
  46.6 12.3 %sweeps.1 = f32[5,8,16,128]{3,2,1,0:T(8,128)} custom-call(f32[5,8,16,128]{3,2,1,0:T(8,128)S(1)} %bitcast.7, f32[5,8,16,128]{3,2,1,0:T(8,128)S(1)} %get-tuple-element.16.res0, f32[22,16,128]{2,1,0:T(8,128)S(1)} %get-tuple-element.17.down0, f32[22,16,128]{2,1,0:T(8,128)S(1)} %collective-permute-done.3.got_down0, ...), custom_call_target="tpu_custom_call" | custom-call | tf_op jit(solution)/shard_map/sweeps/pallas_call | solution.py:374
Async XLA Ops:
  0.0 25.0 %collective-permute-start.2 = (f32[5,8,16,128]{3,2,1,0:T(8,128)}, f32[5,8,16,128]{3,2,1,0:T(8,128)S(1)}, u32[]{:S(2)}, u32[]{:S(2)}) collective-permute-start(f32[5,8,16,128]{3,2,1,0:T(8,128)} %bitcast.2), channel_id=1, source_target_pairs={{1,0},{2,1},{3,2},{4,3},{5,4},{6,5},{7,6},{8,7},{9,8},{10,9},{11,1... | collective-permute-start | bytes 983048 | tf_op jit(solution)/shard_map/ppermute | solution.py:365
  1.3 23.7 %collective-permute-start = (f32[5,8,16,128]{3,2,1,0:T(8,128)}, f32[5,8,16,128]{3,2,1,0:T(8,128)S(1)}, u32[]{:S(2)}, u32[]{:S(2)}) collective-permute-start(f32[5,8,16,128]{3,2,1,0:T(8,128)} %bitcast.3), channel_id=1, source_target_pairs={{0,1},{1,2},{2,3},{3,4},{4,5},{5,6},{6,7},{7,8},{8,9},{9,10},{10,1... | collective-permute-start | bytes 983048 | tf_op jit(solution)/shard_map/ppermute | solution.py:364
  6.2 27.5 %collective-permute-start.1 = (f32[5,8,16,128]{3,2,1,0:T(8,128)}, f32[5,8,16,128]{3,2,1,0:T(8,128)S(1)}, u32[]{:S(2)}, u32[]{:S(2)}) collective-permute-start(f32[5,8,16,128]{3,2,1,0:T(8,128)} %bitcast.4), channel_id=1, source_target_pairs={{15,16},{31,32},{47,48},{63,64},{79,80},{95,96},{111,112},{16,15},... | collective-permute-start | bytes 983048 | tf_op jit(solution)/shard_map/ppermute | solution.py:366
  25.0 1.0 %copy-start = (f32[1,5,8,16,128]{4,3,2,1,0:T(8,128)S(1)}, f32[1,5,8,16,128]{4,3,2,1,0:T(8,128)}, u32[]{:S(2)}) copy-start(f32[1,5,8,16,128]{4,3,2,1,0:T(8,128)} %param.2) | copy-start | bytes 983044
  26.0 0.9 %copy-start.2 = (bf16[3,128,128]{2,1,0:T(8,128)(2,1)S(1)}, bf16[3,128,128]{2,1,0:T(8,128)(2,1)}, u32[]{:S(2)}) copy-start(bf16[3,128,128]{2,1,0:T(8,128)(2,1)} %constant.2.clone.w_ref) | copy-start | bytes 294916
  30.8 15.9 %collective-permute-start.4 = (f32[37,16,128]{2,1,0:T(8,128)S(1)}, f32[37,16,128]{2,1,0:T(8,128)S(1)}, u32[]{:S(2)}, u32[]{:S(2)}) collective-permute-start(f32[37,16,128]{2,1,0:T(8,128)S(1)} %get-tuple-element.19.down1), channel_id=1, source_target_pairs={{128,0},{256,128},{384,256},{512,384},{640,512},{768,640},{896,768... | collective-permute-start | bytes 909320 | tf_op jit(solution)/shard_map/ppermute | solution.py:368
  33.7 12.9 %copy-start.1 = (f32[1,5,8,16,128]{4,3,2,1,0:T(8,128)S(1)}, f32[1,5,8,16,128]{4,3,2,1,0:T(8,128)}, u32[]{:S(2)}) copy-start(f32[1,5,8,16,128]{4,3,2,1,0:T(8,128)} %param.2) | copy-start | bytes 983044
  33.7 12.9 %copy-start.3 = (bf16[3,128,128]{2,1,0:T(8,128)(2,1)S(1)}, bf16[3,128,128]{2,1,0:T(8,128)(2,1)}, u32[]{:S(2)}) copy-start(bf16[3,128,128]{2,1,0:T(8,128)(2,1)} %constant.2.clone.w_ref) | copy-start | bytes 294916
  36.0 10.6 %collective-permute-start.3 = (f32[22,16,128]{2,1,0:T(8,128)S(1)}, f32[22,16,128]{2,1,0:T(8,128)S(1)}, u32[]{:S(2)}, u32[]{:S(2)}) collective-permute-start(f32[22,16,128]{2,1,0:T(8,128)S(1)} %get-tuple-element.17.down0), channel_id=1, source_target_pairs={{128,0},{256,128},{384,256},{512,384},{640,512},{768,640},{896,768... | collective-permute-start | bytes 540680 | tf_op jit(solution)/shard_map/ppermute | solution.py:371
  39.2 7.4 %collective-permute-start.5 = (f32[19,16,128]{2,1,0:T(8,128)S(1)}, f32[19,16,128]{2,1,0:T(8,128)S(1)}, u32[]{:S(2)}, u32[]{:S(2)}) collective-permute-start(f32[19,16,128]{2,1,0:T(8,128)S(1)} %get-tuple-element.20.up), channel_id=1, source_target_pairs={{0,128},{128,256},{256,384},{384,512},{512,640},{640,768},{768,896... | collective-permute-start | bytes 466952 | tf_op jit(solution)/shard_map/ppermute | solution.py:372

commit v3 on v2

v3 whole, which is shorter than its diff:
```python
import functools

import jax
import jax.numpy as jnp
import numpy as np
from jax import lax
from jax.experimental import pallas as pl
from jax.experimental.pallas import tpu as pltpu
from jax.sharding import PartitionSpec as P

SWEEPS = 8
GAMMA = 1.4
COURANT = 0.8
SMOOTHING = 2.0
COMPS = 5
ROWS = 8
HALO = SWEEPS - 1
LINE = 16
LATE = ROWS
EARLY = ROWS + HALO - 1
F32 = jnp.float32
UNROLL = 4


def lanes(shape):
    return lax.broadcasted_iota(jnp.int32, shape, len(shape) - 1)


def sublanes(shape):
    return lax.broadcasted_iota(jnp.int32, shape, len(shape) - 2)


def lane_roll(x, shift):
    return pltpu.roll(x, shift, x.ndim - 1)


def split_dot(x, w):
    high = x.astype(jnp.bfloat16)
    low = (x - high.astype(F32)).astype(jnp.bfloat16)
    dot = functools.partial(jnp.dot, preferred_element_type=F32)
    return dot(high, w) + dot(low, w)


def primitives(q):
    inverse = 1.0 / q[0]
    v = [q[1] * inverse, q[2] * inverse, q[3] * inverse]
    pressure = (GAMMA - 1.0) * (q[4] - 0.5 * (q[1] * v[0] + q[2] * v[1] + q[3] * v[2]))
    sound = jnp.sqrt(GAMMA * pressure * inverse)
    return v, pressure, sound


def flux(q, normal, pressure, d):
    out = [q[1 + d], q[1] * normal, q[2] * normal, q[3] * normal, (q[4] + pressure) * normal]
    out[1 + d] = out[1 + d] + pressure
    return out


def face(q_left, f_left, s_left, q_right, f_right, s_right):
    speed = jnp.maximum(s_left, s_right)
    return [
        (f_left[c] + f_right[c]) - speed * (q_right[c] - q_left[c]) for c in range(COMPS)
    ]


def axis_flags():
    level = lax.axis_index("level")
    block = lax.axis_index("block")
    refinement = jnp.left_shift(jnp.int32(1), level).astype(F32)
    return level, block, refinement


def orientation():
    block = lax.axis_index("block")
    place = lax.rem(block, LINE)
    mirrored = (place == LINE - 1).astype(jnp.int32)
    far = jnp.maximum(mirrored, (place == 0).astype(jnp.int32))
    lowest = (block == 0).astype(jnp.int32)
    highest = (block == lax.axis_size("block") - 1).astype(jnp.int32)
    first_outside = jnp.where(mirrored == 1, lowest, highest)
    second_outside = jnp.where(mirrored == 1, highest, lowest)
    return mirrored, far, first_outside, second_outside


def oriented(mirrored, j):
    return jnp.where(mirrored == 1, ROWS - 1 - j, j)


def residual_kernel(n, own_ref, near_ref, other_ref, w_ref, *refs):
    level, block, refinement = axis_flags()
    mirrored, far, first_outside, second_outside = orientation()
    first = n == EARLY
    if first:
        res_ref, down_ref, up_ref, x_ref, pack_ref = refs
    else:
        earlier_ref, res_ref, down_ref, sent_ref, far_ref, near_chip_ref, x_ref, pack_ref = refs
        up_ref = sent_ref.at[earlier_ref.shape[0] :]
        sent_ref[: earlier_ref.shape[0]] = earlier_ref[...]
    half, groups = n // 2, -(-n // 8)
    ny, nz = x_ref.shape[2:]
    other = mirrored if first else far
    outside = first_outside if first else second_outside
    sign = jnp.where(mirrored == 1, -1.0, 1.0).astype(F32)
    edge = own_ref[:, oriented(mirrored, ROWS - 1 if first else 0)]

    def fetch(j, carried):
        at = oriented(mirrored, j)
        halo = jnp.where(other == 1, other_ref[:, at], near_ref[:, at])
        halo = jnp.where(outside == 1, edge, halo)
        x_ref[:, j] = own_ref[:, at] if first else halo
        x_ref[:, ROWS + j] = halo if first else own_ref[:, at]
        return carried

    lax.fori_loop(0, ROWS, fetch, 0, unroll=4)
    lane, sub = lanes((ny, nz)), sublanes((ny, nz))
    up_ref[: COMPS * groups] = jnp.zeros((COMPS * groups, ny, nz), F32)
    pack_ref[...] = jnp.zeros(pack_ref.shape, F32)

    def load(i):
        return [x_ref[c, i] for c in range(COMPS)]

    def along(q, v, pressure):
        normal = sign * v[0]
        return [
            sign * q[1], q[1] * normal + sign * pressure, q[2] * normal, q[3] * normal, (q[4] + pressure) * normal
        ]

    def row(i, carried):
        q, v, pressure, sound, face_low = carried
        qn = load(i + 1)
        vn, pn, sn = primitives(qn)
        face_high = face(q, along(q, v, pressure), jnp.abs(v[0]) + sound, qn, along(qn, vn, pn), jnp.abs(vn[0]) + sn)
        total = [face_low[c] - face_high[c] for c in range(COMPS)]
        f = flux(q, v[1], pressure, 1)
        speed = jnp.abs(v[1]) + sound

        def below(a):
            return jnp.where(sub == 0, a, pltpu.roll(a, 1, 0))

        qb = [below(a) for a in q]
        fb = flux(qb, below(v[1]), below(pressure), 1)
        low = face(qb, fb, below(speed), q, f, speed)
        for c in range(COMPS):
            high = jnp.where(sub == ny - 1, 2.0 * f[c], pltpu.roll(low[c], ny - 1, 0))
            total[c] = total[c] + (low[c] - high)
        f = flux(q, v[2], pressure, 2)
        speed = jnp.abs(v[2]) + sound
        qb = [lane_roll(a, 1) for a in q]
        fb = flux(qb, lane_roll(v[2], 1), lane_roll(pressure, 1), 2)
        low = face(qb, fb, lane_roll(speed, 1), q, f, speed)
        rate = (
            jnp.abs(v[0]) + sound + (jnp.abs(v[1]) + sound) + (jnp.abs(v[2]) + sound) * refinement
        )
        scale = (0.5 * COURANT) / rate
        r = i - 1
        slot = lax.rem(r, 8)
        in_slot = ((lane >= slot * 7) & (lane < slot * 7 + 7)) | ((lane >= slot * 7 + 71) & (lane < slot * 7 + 78))
        picked = (lane == lax.rem(2 * r + nz - 1, nz)) | (lane == 2 * r) | (lane == 2 * r + 31) | (lane == 2 * r + 96)
        for c in range(COMPS):
            inner = jnp.where(lane == 0, 0.0, low[c])
            difference = inner - lane_roll(inner, nz - 1)
            value = (total[c] + refinement * difference) * scale
            res_ref[c, r] = value
            strip = lane_roll(value, lax.rem(slot * 7 + (nz - 25), nz))
            place = up_ref.at[c * groups + r // 8]
            place[...] = jnp.where(in_slot, strip, place[...])
            pack_ref[c] = jnp.where(picked, lane_roll(q[c], 2 * r), pack_ref[c])
        return qn, vn, pn, sn, face_high

    q0, q1 = load(0), load(1)
    v0, p0, s0 = primitives(q0)
    v1, p1, s1 = primitives(q1)
    low = face(q0, along(q0, v0, p0), jnp.abs(v0[0]) + s0, q1, along(q1, v1, p1), jnp.abs(v1[0]) + s1)
    lax.fori_loop(1, n + 1, row, (q1, v1, p1, s1, low), unroll=UNROLL)
    odd = lax.rem(lane, 2) == 1
    ends, planes = [None, None], [None, None]
    for c in range(COMPS):
        pack = pack_ref[c]
        plane = jnp.where(odd, lane_roll(pack, 31), lane_roll(pack, 97))
        k, shift = c // 4, 32 * (c % 4)
        if shift == 0:
            ends[k], planes[k] = pack, plane
        else:
            here = (lane >= shift - 1) & (lane < shift + 31)
            ends[k] = jnp.where(here, lane_roll(pack, shift), ends[k])
            planes[k] = jnp.where(here, lane_roll(plane, shift), planes[k])
    for k in range(2):
        down_ref[COMPS * half + k] = ends[k]
        up_ref[COMPS * groups + k] = planes[k]
    for c in range(COMPS):
        a = res_ref[c, :half].reshape(half * ny, nz)
        b = res_ref[c, half:].reshape(half * ny, nz)
        packed = split_dot(a, w_ref[0]) + split_dot(b, w_ref[1])
        down_ref[c * half : (c + 1) * half] = packed.reshape(half, ny, nz)
    if not first:
        odd_level = lax.rem(level, 2) == 1
        to_odd = (far_ref, near_chip_ref)
        for is_odd in (True, False):
            up_to, down_to = to_odd if is_odd else to_odd[::-1]

            @pl.when(odd_level if is_odd else jnp.logical_not(odd_level))
            def _(up_to=up_to, down_to=down_to):
                up_to[: sent_ref.shape[0]] = sent_ref[...]
                up_to[sent_ref.shape[0] :] = jnp.zeros((up_to.shape[0] - sent_ref.shape[0], ny, nz), F32)
                down_to[...] = down_ref[...]


def residuals(n, own, near, other, weights, *earlier):
    ny, nz = own.shape[2:]
    half, groups = n // 2, -(-n // 8)
    down = COMPS * half + 2
    up = COMPS * groups + 2 + sum(a.shape[0] for a in earlier)
    tiles = [down, up] + ([max(down, up)] * 2 if earlier else [])
    return pl.pallas_call(
        functools.partial(residual_kernel, n),
        out_shape=(jax.ShapeDtypeStruct((COMPS, n, ny, nz), F32),)
        + tuple(jax.ShapeDtypeStruct((k, ny, nz), F32) for k in tiles),
        in_specs=[pl.BlockSpec(memory_space=pltpu.VMEM)] * (4 + len(earlier)),
        out_specs=(pl.BlockSpec(memory_space=pltpu.VMEM),) * (1 + len(tiles)),
        scratch_shapes=[pltpu.VMEM((COMPS, 2 * ROWS, ny, nz), F32), pltpu.VMEM((COMPS, ny, nz), F32)],
        compiler_params=pltpu.CompilerParams(vmem_limit_bytes=8 * 2**20),
        name="residual_second" if earlier else "residual_first",
    )(own, near, other, weights, *earlier)


def end_faces(ends, planes, refinement):
    shape = ends[0].shape
    upper = lax.rem(lanes(shape), 2) == 1

    def parts(pack):
        return [pack[0]] + [lane_roll(pack[0], 128 - 32 * c) for c in (1, 2, 3)] + [pack[1]]

    q, g = parts(ends), parts(planes)
    v, pressure, sound = primitives(q)
    vg, pg, sg = primitives(g)
    f, fg = flux(q, v[2], pressure, 2), flux(g, vg[2], pg, 2)
    speed = jnp.maximum(jnp.abs(v[2]) + sound, jnp.abs(vg[2]) + sg)
    rate = jnp.abs(v[0]) + sound + (jnp.abs(v[1]) + sound) + (jnp.abs(v[2]) + sound) * refinement
    scale = (0.5 * COURANT) * refinement / rate
    out = []
    for c in range(COMPS):
        jump = speed * (q[c] - g[c])
        mean = f[c] + fg[c]
        out.append(jnp.where(upper, -(mean + jump), mean - jump) * scale)
    return out


def end_terms(n, flags, down_own, up_own, down_got, up_got, own_ref, finer_ref):
    level, refinement, top = flags
    half, groups = n // 2, -(-n // 8)
    ends = [down_own[COMPS * half + k] for k in range(2)]
    planes = [up_own[COMPS * groups + k] for k in range(2)]
    ends_finer = [jnp.where(top == 1, ends[k], down_got[COMPS * half + k]) for k in range(2)]
    planes_coarser = [jnp.where(level == 0, ends[k], up_got[COMPS * groups + k]) for k in range(2)]
    lane = lanes(ends[0].shape)
    near = (lane < 30) | (lane == lane.shape[-1] - 1)

    def halves(a):
        return 0.5 * jnp.where(lane < 64, lane_roll(a, 32), lane_roll(a, 96))

    for c, a in enumerate(end_faces(ends, planes_coarser, refinement)):
        own_ref[c] = jnp.where(near, a, halves(a))
    for c, a in enumerate(end_faces(ends_finer, planes, 2.0 * refinement)):
        finer_ref[c] = halves(a)


def sweep_kernel(
    u_ref, res0, down0, res1, down1, up, got_down1, got_far, got_near_chip, w_ref,
    out_ref, got_down0, got_up, t_ref, own0, own1, finer0, finer1,
):
    level, block, refinement = axis_flags()
    top = (level == lax.axis_size("level") - 1).astype(jnp.int32)
    mirrored, _, first_outside, second_outside = orientation()
    keep_low = (second_outside == 0).astype(F32)
    keep_high = (first_outside == 0).astype(F32)
    ny, nz = t_ref.shape[2:]
    flags = (level, refinement, top)
    total = 2 * HALO + ROWS
    odd_level = lax.rem(level, 2) == 1

    @pl.when(odd_level)
    def _():
        got_down0[...] = got_far[: got_down0.shape[0]]
        got_up[...] = got_near_chip[: got_up.shape[0]]

    @pl.when(jnp.logical_not(odd_level))
    def _():
        got_down0[...] = got_near_chip[: got_down0.shape[0]]
        got_up[...] = got_far[: got_up.shape[0]]

    split = COMPS * -(-EARLY // 8) + 2
    late = (LATE, res0, down0, got_down0, got_up.at[split:], own0, finer0)
    early = (EARLY, res1, down1, got_down1, got_up, own1, finer1)
    end_terms(LATE, flags, down0, up.at[split:], got_down0, got_up.at[split:], own0, finer0)
    end_terms(EARLY, flags, down1, up, got_down1, got_up, own1, finer1)

    lane = lanes((ny, nz))
    covered = (lane >= 32) & (lane < 96)
    replaced = covered & (jnp.full((ny, nz), top, jnp.int32) == 0)
    outer = (lane == 0) | (lane == nz - 1)
    brink = (lane == 32) | (lane == 95)
    share = 1.0 / (1.0 + 6.0 * SMOOTHING)
    h = ny // 2
    lane1, sub1 = lanes((h, nz)), sublanes((h, nz))
    weights = [SMOOTHING * share * k for k in (keep_low, 1.0, keep_high)]
    has_coarser = (level > 0).astype(F32)

    def zone(i):
        return 0 if i < HALO else 1 if i < HALO + ROWS else 2

    def sides(x):
        left = jnp.where(lane1 == 0, 0.0, lane_roll(x, 1))
        right = jnp.where(lane1 == nz - 1, 0.0, lane_roll(x, nz - 1))
        return left + right

    def smooth(which):
        def target(i):
            return t_ref[which, i, :h], t_ref[which, i, h:]

        rows = {i: target(i) for i in range(total)}
        for s in range(2, SWEEPS + 1):
            fresh = {}
            for i in range(s - 1, total - s + 1):
                low, high = rows[i]
                low_up, high_up = pltpu.roll(low, 1, 0), pltpu.roll(high, 1, 0)
                low_dn, high_dn = pltpu.roll(low, h - 1, 0), pltpu.roll(high, h - 1, 0)
                n_low = jnp.where(sub1 == 0, 0.0, low_up) + jnp.where(sub1 == h - 1, high_dn, low_dn)
                n_high = jnp.where(sub1 == 0, low_up, high_up) + jnp.where(sub1 == h - 1, 0.0, high_dn)
                n_low = (n_low + sides(low)) + (rows[i - 1][0] + rows[i + 1][0])
                n_high = (n_high + sides(high)) + (rows[i - 1][1] + rows[i + 1][1])
                t_low, t_high = target(i)
                w = weights[zone(i)]
                fresh[i] = (t_low + w * n_low, t_high + w * n_high)
            rows = fresh
        return [jnp.concatenate(rows[HALO + j], axis=0) for j in range(ROWS)]

    def component(c, carried):
        for n, res, down_own, down_got, up_got, own, finer in (late, early):
            half, groups = n // 2, -(-n // 8)
            offset = 0 if n == LATE else LATE
            own_c, finer_c = own[c], finer[c]
            for r in range(n):
                i = offset + r
                scale = share * (keep_low, 1.0, keep_high)[zone(i)]
                average = down_own[c * half + r % half]
                got = down_got[c * half + r % half]
                if r >= half:
                    average, got = lane_roll(average, 64), lane_roll(got, 64)
                back = (nz - 2 * r) % nz
                term = lane_roll(own_c, back) if back else own_c
                term_finer = lane_roll(finer_c, back) if back else finer_c
                mine = res[c, r] + jnp.where(outer, term, 0.0)
                got = got + jnp.where(brink, term_finer, 0.0)
                t_ref[0, i] = jnp.where(replaced, got, mine) * scale
                inside = average + jnp.where(brink, term, 0.0)
                shift = (25 - 7 * (r % 8)) % nz
                strip = lane_roll(up_got[c * groups + r // 8], shift)
                t_ref[1, i] = jnp.where(covered, inside, strip) * scale
        fine, coarse = smooth(0), smooth(1)
        lifted = split_dot(jnp.concatenate(coarse, axis=0), w_ref[2]).reshape(ROWS, ny, nz)
        for j in range(ROWS):
            at = oriented(mirrored, j)
            out_ref[c, at] = u_ref[c, at] + (fine[j] + lifted[j] * has_coarser)
        return carried

    lax.fori_loop(0, COMPS, component, 0)


def matrices(nz):
    k = np.arange(nz)
    w = np.zeros((3, nz, nz), np.float32)
    w[0, k, nz // 4 + k // 2] = 0.5
    w[1, k, (3 * nz // 4 + k // 2) % nz] = 0.5
    w[2, nz // 4 + k // 2, k] = 1.0
    return jnp.asarray(w, jnp.bfloat16)


def shards(flow_state):
    fields = flow_state[0]
    ny, nz = fields.shape[2:]
    levels, blocks = lax.axis_size("level"), lax.axis_size("block")
    weights = matrices(nz)
    inner = [i for i in range(blocks - 1) if i % LINE != LINE - 1]
    ends = [i for i in range(blocks - 1) if i % LINE == LINE - 1]
    rise = [(i, i + 1) for i in inner]
    fall = [(i + 1, i) for i in inner]
    swap = [(i, i + 1) for i in ends] + [(i + 1, i) for i in ends]
    finer = [(i, i + 1) for i in range(levels - 1)]
    coarser = [(i + 1, i) for i in range(levels - 1)]
    below = lax.ppermute(fields, "block", rise)
    above = lax.ppermute(fields, "block", fall)
    beyond = lax.ppermute(fields, "block", swap)
    res1, down1, up1 = residuals(EARLY, fields, above, below, weights)
    got_down1 = lax.ppermute(down1, "level", coarser)
    beyond, res1 = lax.optimization_barrier((beyond, res1))
    res0, down0, up, far, near_chip = residuals(LATE, fields, below, beyond, weights, up1)
    across = [(i, i + 1) for i in range(1, levels - 1, 2)] + [(i + 1, i) for i in range(1, levels - 1, 2)]
    within = [(i, i + 1) for i in range(0, levels - 1, 2)] + [(i + 1, i) for i in range(0, levels - 1, 2)]
    got_far = lax.ppermute(far, "level", across)
    got_near_chip = lax.ppermute(near_chip, "level", within)
    total = 2 * HALO + ROWS
    pair = pltpu.VMEM((COMPS, ny, nz), F32)
    out = pl.pallas_call(
        sweep_kernel,
        out_shape=jax.ShapeDtypeStruct(fields.shape, F32),
        in_specs=[pl.BlockSpec(memory_space=pltpu.VMEM)] * 10,
        out_specs=pl.BlockSpec(memory_space=pltpu.VMEM),
        scratch_shapes=[
            pltpu.VMEM(down0.shape, F32), pltpu.VMEM(up.shape, F32), pltpu.VMEM((2, total, ny, nz), F32),
            pair, pair, pair, pair,
        ],
        compiler_params=pltpu.CompilerParams(vmem_limit_bytes=16 * 2**20),
        name="sweeps",
    )(fields, res0, down0, res1, down1, up, got_down1, got_far, got_near_chip, weights)
    return out[None]


def solution(mesh):
    spec = P("level", None, "block", None, None)
    return jax.shard_map(shards, mesh=mesh, in_specs=(spec,), out_specs=spec, check_vma=False)
```

time: 59.2 us -> 52.2 us (0.88)
  the two profiles are of different devices: /device:TPU:56 before, /device:TPU:23 now
where the time goes in v3:
time: 52.2 us; the launch traced here: 51.9 us
  starting transfers between devices  33.6 us (64%)
  Pallas kernels  11.2 us (21%)
  waiting for transfers between devices  5.03 us (10%)
  local copies, waits for them, and re-layouts  1.89 us (4%)
    ppermute x1, starting transfers between devices, shards(): beyond = lax.ppermute(fields, 'block', swap)  15.8 us
    pallas_call x1, Pallas kernels, shards(): pl.pallas_call(sweep_kernel, out_shape=jax.ShapeDtypeStruct(fields.shape,...  7.99 us
    ppermute x1, starting transfers between devices, shards(): got_far = lax.ppermute(far, 'level', across)  6.88 us
    ppermute x1, waiting for transfers between devices, shards(): got_far = lax.ppermute(far, 'level', across)  4.88 us
    ppermute x1, starting transfers between devices, shards(): below = lax.ppermute(fields, 'block', rise)  4.65 us
    pallas_call x2, Pallas kernels, residuals(): pl.pallas_call(functools.partial(residual_kernel, n), out_shape=(jax.Shap...  3.25 us
    ppermute x1, starting transfers between devices, shards(): got_down1 = lax.ppermute(down1, 'level', coarser)  3.14 us
    ppermute x1, starting transfers between devices, shards(): got_near_chip = lax.ppermute(near_chip, 'level', within)  1.92 us
  transfers between devices with their start and end apart: 6, of which 2 were waited for; matrix products, arithmetic and copies ran while one was open for 0% of the time, Pallas kernels for 6%

profile of v3, /device:TPU:23, one launch (start us, length us, event | category | flops | bytes accessed | tf_op | source)
XLA Modules:
  0.0 51.9 jit_solution(18101540829527837247)
XLA Ops:
  0.0 1.3 %collective-permute-start.2 = (f32[5,8,16,128]{3,2,1,0:T(8,128)}, f32[5,8,16,128]{3,2,1,0:T(8,128)S(1)}, u32[]{:S(2)}, u32[]{:S(2)}) collective-permute-start(f32[5,8,16,128]{3,2,1,0:T(8,128)} %bitcast.2), channel_id=1, source_target_pairs={{1,0},{2,1},{3,2},{4,3},{5,4},{6,5},{7,6},{8,7},{9,8},{10,9},{11,1... | collective-permute-start | bytes 983048 | tf_op jit(solution)/shard_map/ppermute | solution.py:390
  1.3 4.6 %collective-permute-start = (f32[5,8,16,128]{3,2,1,0:T(8,128)}, f32[5,8,16,128]{3,2,1,0:T(8,128)S(1)}, u32[]{:S(2)}, u32[]{:S(2)}) collective-permute-start(f32[5,8,16,128]{3,2,1,0:T(8,128)} %bitcast.3), channel_id=1, source_target_pairs={{0,1},{1,2},{2,3},{3,4},{4,5},{5,6},{6,7},{7,8},{8,9},{9,10},{10,1... | collective-permute-start | bytes 983048 | tf_op jit(solution)/shard_map/ppermute | solution.py:389
  5.9 15.8 %collective-permute-start.1 = (f32[5,8,16,128]{3,2,1,0:T(8,128)}, f32[5,8,16,128]{3,2,1,0:T(8,128)S(1)}, u32[]{:S(2)}, u32[]{:S(2)}) collective-permute-start(f32[5,8,16,128]{3,2,1,0:T(8,128)} %bitcast.4), channel_id=1, source_target_pairs={{15,16},{31,32},{47,48},{63,64},{79,80},{95,96},{111,112},{16,15},... | collective-permute-start | bytes 983048 | tf_op jit(solution)/shard_map/ppermute | solution.py:391
  21.7 0.0 collective-permute-done.2.near_ref
  21.7 0.0 collective-permute-done.other_ref.near_ref
  21.7 0.0 copy-start
  21.7 1.0 %copy-done = f32[1,5,8,16,128]{4,3,2,1,0:T(8,128)S(1)} copy-done((f32[1,5,8,16,128]{4,3,2,1,0:T(8,128)S(1)}, f32[1,5,8,16,128]{4,3,2,1,0:T(8,128)}, u32[]{:S(2)}) %copy-start) | copy-done | bytes 327704
  22.7 0.0 copy-start.2
  22.7 0.9 %copy-done.2 = bf16[3,128,128]{2,1,0:T(8,128)(2,1)S(1)} copy-done((bf16[3,128,128]{2,1,0:T(8,128)(2,1)S(1)}, bf16[3,128,128]{2,1,0:T(8,128)(2,1)}, u32[]{:S(2)}) %copy-start.2) | copy-done | bytes 98328
  23.6 0.0 copy-start.3
  23.6 2.1 %residual_first.1 = (f32[5,14,16,128]{3,2,1,0:T(8,128)S(1)}, f32[37,16,128]{2,1,0:T(8,128)S(1)}, f32[12,16,128]{2,1,0:T(8,128)S(1)}) custom-call(f32[5,8,16,128]{3,2,1,0:T(8,128)S(1)} %bitcast.5, f32[5,8,16,128]{3,2,1,0:T(8,128)S(1)} %collective-permute-done.2.near_ref, f32[5,8,16,128]{3,2,1,0:T(8,128)S(1)} %collective-permute-done.other_ref.near_ref, ...), custom_call_target="tpu_custom_call" | custom-call | tf_op jit(solution)/shard_map/residual_first/pallas_call | solution.py:213
  25.7 3.1 %collective-permute-start.3 = (f32[37,16,128]{2,1,0:T(8,128)S(1)}, f32[37,16,128]{2,1,0:T(8,128)S(1)}, u32[]{:S(2)}, u32[]{:S(2)}) collective-permute-start(f32[37,16,128]{2,1,0:T(8,128)S(1)} %get-tuple-element.21.down1), channel_id=1, source_target_pairs={{128,0},{256,128},{384,256},{512,384},{640,512},{768,640},{896,768... | collective-permute-start | bytes 909320 | tf_op jit(solution)/shard_map/ppermute | solution.py:393
  28.9 0.1 collective-permute-done.1.other_ref
  29.0 0.0 copy-done.3
  29.0 0.0 copy-start.1
  29.0 1.1 %residual_second.1 = (f32[5,8,16,128]{3,2,1,0:T(8,128)S(1)}, f32[22,16,128]{2,1,0:T(8,128)S(1)}, f32[19,16,128]{2,1,0:T(8,128)S(1)}, f32[22,16,128]{2,1,0:T(8,128)S(1)}, f32[22,16,128]{2,1,0:T(8,128)S(1)}) custom-call(f32[5,8,16,128]{3,2,1,0:T(8,128)S(1)} %bitcast.6, f32[5,8,16,128]{3,2,1,0:T(8,128)S(1)} %collective-permute-done.other_ref.near_ref, ...), custom_call_target="tpu_custom_call" | custom-call | tf_op jit(solution)/shard_map/residual_second/pallas_call | solution.py:213
  30.2 6.9 %collective-permute-start.4 = (f32[22,16,128]{2,1,0:T(8,128)S(1)}, f32[22,16,128]{2,1,0:T(8,128)S(1)}, u32[]{:S(2)}, u32[]{:S(2)}) collective-permute-start(f32[22,16,128]{2,1,0:T(8,128)S(1)} %get-tuple-element.23), channel_id=1, source_target_pairs={{128,256},{384,512},{640,768},{256,128},{512,384},{768,640},{129,2... | collective-permute-start | bytes 540680 | tf_op jit(solution)/shard_map/ppermute | solution.py:398
  37.1 1.9 %collective-permute-start.5 = (f32[22,16,128]{2,1,0:T(8,128)S(1)}, f32[22,16,128]{2,1,0:T(8,128)S(1)}, u32[]{:S(2)}, u32[]{:S(2)}) collective-permute-start(f32[22,16,128]{2,1,0:T(8,128)S(1)} %get-tuple-element.24), channel_id=1, source_target_pairs={{0,128},{256,384},{512,640},{768,896},{128,0},{384,256},{640,512},... | collective-permute-start | bytes 540680 | tf_op jit(solution)/shard_map/ppermute | solution.py:399
  39.0 4.9 %collective-permute-done.4.got_far = f32[22,16,128]{2,1,0:T(8,128)S(1)} collective-permute-done((f32[22,16,128]{2,1,0:T(8,128)S(1)}, f32[22,16,128]{2,1,0:T(8,128)S(1)}, u32[]{:S(2)}, u32[]{:S(2)}) %collective-permute-start.4) | collective-permute-done | bytes 180256 | tf_op jit(solution)/shard_map/ppermute | solution.py:398
  43.9 0.0 collective-permute-done.5.got_near_chip
  43.9 0.0 collective-permute-done.3.got_down1
  43.9 0.0 copy-done.1
  43.9 8.0 %sweeps.1 = f32[5,8,16,128]{3,2,1,0:T(8,128)} custom-call(f32[5,8,16,128]{3,2,1,0:T(8,128)S(1)} %bitcast.7, f32[5,8,16,128]{3,2,1,0:T(8,128)S(1)} %get-tuple-element.18.res0, f32[22,16,128]{2,1,0:T(8,128)S(1)} %get-tuple-element.19.down0, f32[5,14,16,128]{3,2,1,0:T(8,128)S(1)} %get-tuple-element.20.res1, f32[37,16,128]{2,1,0:T(8,128)S(1)} %get-tuple-element.21.down1, ...), custom_call_target="tpu_custom_call" | custom-call | tf_op jit(solution)/shard_map/sweeps/pallas_call | solution.py:402
Async XLA Ops:
  0.0 21.7 %collective-permute-start.2 = (f32[5,8,16,128]{3,2,1,0:T(8,128)}, f32[5,8,16,128]{3,2,1,0:T(8,128)S(1)}, u32[]{:S(2)}, u32[]{:S(2)}) collective-permute-start(f32[5,8,16,128]{3,2,1,0:T(8,128)} %bitcast.2), channel_id=1, source_target_pairs={{1,0},{2,1},{3,2},{4,3},{5,4},{6,5},{7,6},{8,7},{9,8},{10,9},{11,1... | collective-permute-start | bytes 983048 | tf_op jit(solution)/shard_map/ppermute | solution.py:390
  1.3 20.4 %collective-permute-start = (f32[5,8,16,128]{3,2,1,0:T(8,128)}, f32[5,8,16,128]{3,2,1,0:T(8,128)S(1)}, u32[]{:S(2)}, u32[]{:S(2)}) collective-permute-start(f32[5,8,16,128]{3,2,1,0:T(8,128)} %bitcast.3), channel_id=1, source_target_pairs={{0,1},{1,2},{2,3},{3,4},{4,5},{5,6},{6,7},{7,8},{8,9},{9,10},{10,1... | collective-permute-start | bytes 983048 | tf_op jit(solution)/shard_map/ppermute | solution.py:389
  5.9 23.1 %collective-permute-start.1 = (f32[5,8,16,128]{3,2,1,0:T(8,128)}, f32[5,8,16,128]{3,2,1,0:T(8,128)S(1)}, u32[]{:S(2)}, u32[]{:S(2)}) collective-permute-start(f32[5,8,16,128]{3,2,1,0:T(8,128)} %bitcast.4), channel_id=1, source_target_pairs={{15,16},{31,32},{47,48},{63,64},{79,80},{95,96},{111,112},{16,15},... | collective-permute-start | bytes 983048 | tf_op jit(solution)/shard_map/ppermute | solution.py:391
  21.7 1.0 %copy-start = (f32[1,5,8,16,128]{4,3,2,1,0:T(8,128)S(1)}, f32[1,5,8,16,128]{4,3,2,1,0:T(8,128)}, u32[]{:S(2)}) copy-start(f32[1,5,8,16,128]{4,3,2,1,0:T(8,128)} %param.2) | copy-start | bytes 983044
  22.7 0.9 %copy-start.2 = (bf16[3,128,128]{2,1,0:T(8,128)(2,1)S(1)}, bf16[3,128,128]{2,1,0:T(8,128)(2,1)}, u32[]{:S(2)}) copy-start(bf16[3,128,128]{2,1,0:T(8,128)(2,1)} %constant.2.clone.w_ref) | copy-start | bytes 294916
  23.6 5.4 %copy-start.3 = (bf16[3,128,128]{2,1,0:T(8,128)(2,1)S(1)}, bf16[3,128,128]{2,1,0:T(8,128)(2,1)}, u32[]{:S(2)}) copy-start(bf16[3,128,128]{2,1,0:T(8,128)(2,1)} %constant.2.clone.w_ref) | copy-start | bytes 294916
  25.7 18.2 %collective-permute-start.3 = (f32[37,16,128]{2,1,0:T(8,128)S(1)}, f32[37,16,128]{2,1,0:T(8,128)S(1)}, u32[]{:S(2)}, u32[]{:S(2)}) collective-permute-start(f32[37,16,128]{2,1,0:T(8,128)S(1)} %get-tuple-element.21.down1), channel_id=1, source_target_pairs={{128,0},{256,128},{384,256},{512,384},{640,512},{768,640},{896,768... | collective-permute-start | bytes 909320 | tf_op jit(solution)/shard_map/ppermute | solution.py:393
  29.0 14.9 %copy-start.1 = (f32[1,5,8,16,128]{4,3,2,1,0:T(8,128)S(1)}, f32[1,5,8,16,128]{4,3,2,1,0:T(8,128)}, u32[]{:S(2)}) copy-start(f32[1,5,8,16,128]{4,3,2,1,0:T(8,128)} %param.2) | copy-start | bytes 983044
  30.2 13.7 %collective-permute-start.4 = (f32[22,16,128]{2,1,0:T(8,128)S(1)}, f32[22,16,128]{2,1,0:T(8,128)S(1)}, u32[]{:S(2)}, u32[]{:S(2)}) collective-permute-start(f32[22,16,128]{2,1,0:T(8,128)S(1)} %get-tuple-element.23), channel_id=1, source_target_pairs={{128,256},{384,512},{640,768},{256,128},{512,384},{768,640},{129,2... | collective-permute-start | bytes 540680 | tf_op jit(solution)/shard_map/ppermute | solution.py:398
  37.1 6.8 %collective-permute-start.5 = (f32[22,16,128]{2,1,0:T(8,128)S(1)}, f32[22,16,128]{2,1,0:T(8,128)S(1)}, u32[]{:S(2)}, u32[]{:S(2)}) collective-permute-start(f32[22,16,128]{2,1,0:T(8,128)S(1)} %get-tuple-element.24), channel_id=1, source_target_pairs={{0,128},{256,384},{512,640},{768,896},{128,0},{384,256},{640,512},... | collective-permute-start | bytes 540680 | tf_op jit(solution)/shard_map/ppermute | solution.py:399

commit v4 on v3

v4 whole, which is shorter than its diff:
```python
import functools

import jax
import jax.numpy as jnp
import ml_dtypes
import numpy as np
from jax import lax
from jax.experimental import pallas as pl
from jax.experimental.pallas import tpu as pltpu
from jax.sharding import PartitionSpec as P

SWEEPS = 8
GAMMA = 1.4
COURANT = 0.8
SMOOTHING = 2.0
COMPS = 5
ROWS = 8
HALO = SWEEPS - 1
LINE = 16
LATE = ROWS
EARLY = ROWS + HALO - 1
F32 = jnp.float32
UNROLL = 4
FIRST_UP_TILES = 22


def lanes(shape):
    return lax.broadcasted_iota(jnp.int32, shape, len(shape) - 1)


def sublanes(shape):
    return lax.broadcasted_iota(jnp.int32, shape, len(shape) - 2)


def lane_roll(x, shift):
    return pltpu.roll(x, shift, x.ndim - 1)


def split_dot(x, w):
    high = x.astype(jnp.bfloat16)
    low = (x - high.astype(F32)).astype(jnp.bfloat16)
    dot = functools.partial(jnp.dot, preferred_element_type=F32)
    return dot(high, w) + dot(low, w)


def pairing(nz, base):
    k = lax.broadcasted_iota(jnp.int32, (nz, nz), 0)
    to = lax.broadcasted_iota(jnp.int32, (nz, nz), 1)
    return jnp.where(to == lax.rem(base + k // 2, nz), 0.5, 0.0).astype(jnp.bfloat16)


def transforms(nz):
    k = np.arange(1, nz + 1)
    sine = np.sqrt(2.0 / (nz + 1)) * np.sin(np.pi * np.outer(k, k) / (nz + 1))
    back = sine[:, nz // 4 + np.arange(nz) // 2]

    def parts(a):
        high = a.astype(ml_dtypes.bfloat16)
        low = (a - high.astype(np.float64)).astype(ml_dtypes.bfloat16)
        row = np.concatenate([high, low], axis=1)
        return np.concatenate([row, row], axis=0)

    factor = 2.0 * np.cos(np.pi * k / (nz + 1))
    return jnp.asarray(np.stack([parts(sine), parts(back)])), jnp.asarray(np.tile(factor, (8, 1)), F32)


def halved(x):
    high = x.astype(jnp.bfloat16)
    return jnp.concatenate([high, (x - high.astype(F32)).astype(jnp.bfloat16)], axis=1)


def transformed(parts, w):
    out = jnp.dot(parts, w, preferred_element_type=F32)
    nz = out.shape[1] // 2
    return out[:, :nz] + out[:, nz:]


def primitives(q):
    inverse = 1.0 / q[0]
    v = [q[1] * inverse, q[2] * inverse, q[3] * inverse]
    pressure = (GAMMA - 1.0) * (q[4] - 0.5 * (q[1] * v[0] + q[2] * v[1] + q[3] * v[2]))
    sound = jnp.sqrt(GAMMA * pressure * inverse)
    return v, pressure, sound


def flux(q, normal, pressure, d):
    out = [q[1 + d], q[1] * normal, q[2] * normal, q[3] * normal, (q[4] + pressure) * normal]
    out[1 + d] = out[1 + d] + pressure
    return out


def face(q_left, f_left, s_left, q_right, f_right, s_right):
    speed = jnp.maximum(s_left, s_right)
    return [
        (f_left[c] + f_right[c]) - speed * (q_right[c] - q_left[c]) for c in range(COMPS)
    ]


def axis_flags():
    level = lax.axis_index("level")
    block = lax.axis_index("block")
    refinement = jnp.left_shift(jnp.int32(1), level).astype(F32)
    return level, block, refinement


def orientation():
    block = lax.axis_index("block")
    place = lax.rem(block, LINE)
    mirrored = (place >= LINE - 2).astype(jnp.int32)
    source = jnp.where(place == LINE - 2, 2, jnp.where((place == 0) | (place == LINE - 1), 1, 0))
    lowest = (block == 0).astype(jnp.int32)
    highest = (block == lax.axis_size("block") - 1).astype(jnp.int32)
    first_outside = jnp.where(mirrored == 1, lowest, highest)
    second_outside = jnp.where(mirrored == 1, highest, lowest)
    return mirrored, source, first_outside, second_outside


def oriented(mirrored, j):
    return jnp.where(mirrored == 1, ROWS - 1 - j, j)


def residual_kernel(n, own_ref, *refs):
    level, block, refinement = axis_flags()
    mirrored, source, first_outside, second_outside = orientation()
    first = n == EARLY
    if first:
        *halos, res_ref, down_ref, up_ref, x_ref, pack_ref = refs
    else:
        *halos, res_ref, down_ref, up_ref, far_ref, near_chip_ref, x_ref, pack_ref = refs
    half, groups = n // 2, -(-n // 8)
    ny, nz = x_ref.shape[2:]
    choice = mirrored if first else source
    outside = first_outside if first else second_outside
    sign = jnp.where(mirrored == 1, -1.0, 1.0).astype(F32)
    up_ref[...] = jnp.zeros(up_ref.shape, F32)
    pack_ref[...] = jnp.zeros(pack_ref.shape, F32)
    edge = own_ref[:, oriented(mirrored, ROWS - 1 if first else 0)]

    def fetch(j, carried):
        at = oriented(mirrored, j)
        halo = halos[0][:, at]
        for k, ref in enumerate(halos[1:], 1):
            halo = jnp.where(choice == k, ref[:, at], halo)
        halo = jnp.where(outside == 1, edge, halo)
        x_ref[:, j] = own_ref[:, at] if first else halo
        x_ref[:, ROWS + j] = halo if first else own_ref[:, at]
        return carried

    lax.fori_loop(0, ROWS, fetch, 0, unroll=4)
    lane, sub = lanes((ny, nz)), sublanes((ny, nz))

    def load(i):
        return [x_ref[c, i] for c in range(COMPS)]

    def along(q, v, pressure):
        normal = sign * v[0]
        return [
            sign * q[1], q[1] * normal + sign * pressure, q[2] * normal, q[3] * normal, (q[4] + pressure) * normal
        ]

    def row(i, carried):
        q, v, pressure, sound, face_low = carried
        qn = load(i + 1)
        vn, pn, sn = primitives(qn)
        face_high = face(q, along(q, v, pressure), jnp.abs(v[0]) + sound, qn, along(qn, vn, pn), jnp.abs(vn[0]) + sn)
        total = [face_low[c] - face_high[c] for c in range(COMPS)]
        f = flux(q, v[1], pressure, 1)
        speed = jnp.abs(v[1]) + sound

        def below(a):
            return jnp.where(sub == 0, a, pltpu.roll(a, 1, 0))

        qb = [below(a) for a in q]
        fb = flux(qb, below(v[1]), below(pressure), 1)
        low = face(qb, fb, below(speed), q, f, speed)
        for c in range(COMPS):
            high = jnp.where(sub == ny - 1, 2.0 * f[c], pltpu.roll(low[c], ny - 1, 0))
            total[c] = total[c] + (low[c] - high)
        f = flux(q, v[2], pressure, 2)
        speed = jnp.abs(v[2]) + sound
        qb = [lane_roll(a, 1) for a in q]
        fb = flux(qb, lane_roll(v[2], 1), lane_roll(pressure, 1), 2)
        low = face(qb, fb, lane_roll(speed, 1), q, f, speed)
        rate = (
            jnp.abs(v[0]) + sound + (jnp.abs(v[1]) + sound) + (jnp.abs(v[2]) + sound) * refinement
        )
        scale = (0.5 * COURANT) / rate
        r = i - 1
        slot = lax.rem(r, 8)
        in_slot = ((lane >= slot * 7) & (lane < slot * 7 + 7)) | ((lane >= slot * 7 + 71) & (lane < slot * 7 + 78))
        picked = (lane == lax.rem(2 * r + nz - 1, nz)) | (lane == 2 * r) | (lane == 2 * r + 31) | (lane == 2 * r + 96)
        for c in range(COMPS):
            inner = jnp.where(lane == 0, 0.0, low[c])
            difference = inner - lane_roll(inner, nz - 1)
            value = (total[c] + refinement * difference) * scale
            res_ref[c, r] = value
            strip = lane_roll(value, lax.rem(slot * 7 + (nz - 25), nz))
            place = up_ref.at[c * groups + r // 8]
            place[...] = jnp.where(in_slot, strip, place[...])
            pack_ref[c] = jnp.where(picked, lane_roll(q[c], 2 * r), pack_ref[c])
        return qn, vn, pn, sn, face_high

    q0, q1 = load(0), load(1)
    v0, p0, s0 = primitives(q0)
    v1, p1, s1 = primitives(q1)
    low = face(q0, along(q0, v0, p0), jnp.abs(v0[0]) + s0, q1, along(q1, v1, p1), jnp.abs(v1[0]) + s1)
    lax.fori_loop(1, n + 1, row, (q1, v1, p1, s1, low), unroll=UNROLL)
    odd = lax.rem(lane, 2) == 1
    ends, planes = [None, None], [None, None]
    for c in range(COMPS):
        pack = pack_ref[c]
        plane = jnp.where(odd, lane_roll(pack, 31), lane_roll(pack, 97))
        k, shift = c // 4, 32 * (c % 4)
        if shift == 0:
            ends[k], planes[k] = pack, plane
        else:
            here = (lane >= shift - 1) & (lane < shift + 31)
            ends[k] = jnp.where(here, lane_roll(pack, shift), ends[k])
            planes[k] = jnp.where(here, lane_roll(plane, shift), planes[k])
    for k in range(2):
        down_ref[COMPS * half + k] = ends[k]
        up_ref[COMPS * groups + k] = planes[k]
    to_first, to_second = pairing(nz, nz // 4), pairing(nz, 3 * nz // 4)
    for c in range(COMPS):
        a = res_ref[c, :half].reshape(half * ny, nz)
        b = res_ref[c, half:].reshape(half * ny, nz)
        packed = split_dot(a, to_first) + split_dot(b, to_second)
        down_ref[c * half : (c + 1) * half] = packed.reshape(half, ny, nz)
    if not first:
        odd_level = lax.rem(level, 2) == 1
        to_odd = (far_ref, near_chip_ref)
        for is_odd in (True, False):
            up_to, down_to = to_odd if is_odd else to_odd[::-1]

            @pl.when(odd_level if is_odd else jnp.logical_not(odd_level))
            def _(up_to=up_to, down_to=down_to):
                up_to[: up_ref.shape[0]] = up_ref[...]
                up_to[up_ref.shape[0] :] = jnp.zeros((up_to.shape[0] - up_ref.shape[0], ny, nz), F32)
                down_to[...] = down_ref[...]


def residuals(n, own, *halos):
    ny, nz = own.shape[2:]
    first = n == EARLY
    half, groups = n // 2, -(-n // 8)
    down, up = COMPS * half + 2, COMPS * groups + 2
    tiles = (down, FIRST_UP_TILES) if first else (down, up, down, down)
    shapes = [(COMPS, n, ny, nz)] + [(k, ny, nz) for k in tiles]
    scratch = [pltpu.VMEM((COMPS, 2 * ROWS, ny, nz), F32), pltpu.VMEM((COMPS, ny, nz), F32)]
    vmem = pl.BlockSpec(memory_space=pltpu.VMEM)
    return pl.pallas_call(
        functools.partial(residual_kernel, n),
        out_shape=tuple(jax.ShapeDtypeStruct(k, F32) for k in shapes),
        in_specs=[vmem] * (1 + len(halos)),
        out_specs=(vmem,) * len(shapes),
        scratch_shapes=scratch,
        compiler_params=pltpu.CompilerParams(vmem_limit_bytes=8 * 2**20),
        cost_estimate=pl.CostEstimate(flops=2_000_000, bytes_accessed=2_000_000, transcendentals=0),
        name="residual_first" if first else "residual_second",
    )(own, *halos)


def end_faces(ends, planes, refinement):
    shape = ends[0].shape
    upper = lax.rem(lanes(shape), 2) == 1

    def parts(pack):
        return [pack[0]] + [lane_roll(pack[0], 128 - 32 * c) for c in (1, 2, 3)] + [pack[1]]

    q, g = parts(ends), parts(planes)
    v, pressure, sound = primitives(q)
    vg, pg, sg = primitives(g)
    f, fg = flux(q, v[2], pressure, 2), flux(g, vg[2], pg, 2)
    speed = jnp.maximum(jnp.abs(v[2]) + sound, jnp.abs(vg[2]) + sg)
    rate = jnp.abs(v[0]) + sound + (jnp.abs(v[1]) + sound) + (jnp.abs(v[2]) + sound) * refinement
    scale = (0.5 * COURANT) * refinement / rate
    out = []
    for c in range(COMPS):
        jump = speed * (q[c] - g[c])
        mean = f[c] + fg[c]
        out.append(jnp.where(upper, -(mean + jump), mean - jump) * scale)
    return out


def end_terms(n, flags, down_own, up_own, down_got, up_got, own_ref, finer_ref):
    level, refinement, top = flags
    half, groups = n // 2, -(-n // 8)
    ends = [down_own[COMPS * half + k] for k in range(2)]
    planes = [up_own[COMPS * groups + k] for k in range(2)]
    ends_finer = [jnp.where(top == 1, ends[k], down_got[COMPS * half + k]) for k in range(2)]
    planes_coarser = [jnp.where(level == 0, ends[k], up_got[COMPS * groups + k]) for k in range(2)]
    lane = lanes(ends[0].shape)
    near = (lane < 30) | (lane == lane.shape[-1] - 1)

    def halves(a):
        return 0.5 * jnp.where(lane < 64, lane_roll(a, 32), lane_roll(a, 96))

    for c, a in enumerate(end_faces(ends, planes_coarser, refinement)):
        own_ref[c] = jnp.where(near, a, halves(a))
    for c, a in enumerate(end_faces(ends_finer, planes, 2.0 * refinement)):
        finer_ref[c] = halves(a)


def sweep_kernel(
    n, w_ref, factor_ref, res, down_own, up_own, *refs
):
    first = n == EARLY
    if first:
        down_got, up_got, part_ref, t_ref, lhs_ref, own_ends, finer_ends = refs
    else:
        got_far, got_near_chip, u_ref, earlier_ref, out_ref, t_ref, lhs_ref, own_ends, finer_ends, down_got, up_got = refs
    level, block, refinement = axis_flags()
    top = (level == lax.axis_size("level") - 1).astype(jnp.int32)
    mirrored, _, first_outside, second_outside = orientation()
    keep_low = (second_outside == 0).astype(F32)
    keep_high = (first_outside == 0).astype(F32)
    ny, nz = t_ref.shape[2:]
    half, groups = n // 2, -(-n // 8)
    total = 2 * HALO + ROWS
    offset = LATE if first else 0
    if not first:
        odd_level = lax.rem(level, 2) == 1
        for is_odd in (True, False):
            down_from, up_from = (got_far, got_near_chip) if is_odd else (got_near_chip, got_far)

            @pl.when(odd_level if is_odd else jnp.logical_not(odd_level))
            def _(down_from=down_from, up_from=up_from):
                down_got[...] = down_from[...]
                up_got[...] = up_from[: up_got.shape[0]]

    end_terms(n, (level, refinement, top), down_own, up_own, down_got, up_got, own_ends, finer_ends)

    lane = lanes((ny, nz))
    covered = (lane >= 32) & (lane < 96)
    replaced = covered & (jnp.full((ny, nz), top, jnp.int32) == 0)
    outer = (lane == 0) | (lane == nz - 1)
    brink = (lane == 32) | (lane == 95)
    share = 1.0 / (1.0 + 6.0 * SMOOTHING)
    h = ny // 2
    sub1 = sublanes((h, nz))
    factor = factor_ref[...]
    weights = [SMOOTHING * share * k for k in (keep_low, 1.0, keep_high)]
    has_coarser = (level > 0).astype(F32)

    def zone(i):
        return 0 if i < HALO else 1 if i < HALO + ROWS else 2

    def add(terms):
        out = terms[0]
        for term in terms[1:]:
            out = out + term
        return out

    def smooth(which):
        def target(i):
            return t_ref[which, i, :h], t_ref[which, i, h:]

        rows = {offset + r: target(offset + r) for r in range(n)}
        for s in range(2, SWEEPS + 1):
            fresh = {}
            for i in range(s - 1, total - s + 1):
                if i in rows:
                    low, high = rows[i]
                    low_up, high_up = pltpu.roll(low, 1, 0), pltpu.roll(high, 1, 0)
                    low_dn, high_dn = pltpu.roll(low, h - 1, 0), pltpu.roll(high, h - 1, 0)
                    n_low = jnp.where(sub1 == 0, 0.0, low_up) + jnp.where(sub1 == h - 1, high_dn, low_dn)
                    n_high = jnp.where(sub1 == 0, low_up, high_up) + jnp.where(sub1 == h - 1, 0.0, high_dn)
                    around = [(n_low + factor * low, n_high + factor * high)]
                else:
                    around = []
                beside = [rows[k] for k in (i - 1, i + 1) if k in rows]
                if not around and not beside:
                    continue
                w = weights[zone(i)]
                new = [w * add([a[k] for a in around + beside]) for k in range(2)]
                if offset <= i < offset + n:
                    new = [a + b for a, b in zip(target(i), new)]
                fresh[i] = tuple(new)
            rows = fresh
        return [jnp.concatenate(rows[HALO + j], axis=0) for j in range(ROWS)]

    def component(c, carried):
        own_c, finer_c = own_ends[c], finer_ends[c]
        for r in range(n):
            i = offset + r
            scale = share * (keep_low, 1.0, keep_high)[zone(i)]
            average = down_own[c * half + r % half]
            got = down_got[c * half + r % half]
            if r >= half:
                average, got = lane_roll(average, 64), lane_roll(got, 64)
            back = (nz - 2 * r) % nz
            term = lane_roll(own_c, back) if back else own_c
            term_finer = lane_roll(finer_c, back) if back else finer_c
            mine = res[c, r] + jnp.where(outer, term, 0.0)
            got = got + jnp.where(brink, term_finer, 0.0)
            lhs_ref[r * ny : (r + 1) * ny] = halved(jnp.where(replaced, got, mine) * scale)
            inside = average + jnp.where(brink, term, 0.0)
            shift = (25 - 7 * (r % 8)) % nz
            strip = lane_roll(up_got[c * groups + r // 8], shift)
            lhs_ref[(n + r) * ny : (n + r + 1) * ny] = halved(jnp.where(covered, inside, strip) * scale)
        t_ref[:, offset : offset + n] = transformed(lhs_ref[...], w_ref[0]).reshape(2, n, ny, nz)
        fine, coarse = smooth(0), smooth(1)
        if first:
            for j in range(ROWS):
                part_ref[c, j] = fine[j]
                part_ref[COMPS + c, j] = coarse[j]
            return carried
        for j in range(ROWS):
            lhs_ref[j * ny : (j + 1) * ny] = halved(fine[j] + earlier_ref[c, j])
            lhs_ref[(ROWS + j) * ny : (ROWS + j + 1) * ny] = halved(coarse[j] + earlier_ref[COMPS + c, j])
        own = transformed(lhs_ref[: ROWS * ny], w_ref[0]).reshape(ROWS, ny, nz)
        lifted = transformed(lhs_ref[ROWS * ny : 2 * ROWS * ny], w_ref[1]).reshape(ROWS, ny, nz)
        for j in range(ROWS):
            at = oriented(mirrored, j)
            out_ref[c, at] = u_ref[c, at] + (own[j] + lifted[j] * has_coarser)
        return carried

    lax.fori_loop(0, COMPS, component, 0)


def sweeps(n, shape, *args):
    ny, nz = shape[2:]
    first = n == EARLY
    half, groups = n // 2, -(-n // 8)
    ends = pltpu.VMEM((COMPS, ny, nz), F32)
    out = (2 * COMPS, ROWS, ny, nz) if first else shape
    return pl.pallas_call(
        functools.partial(sweep_kernel, n),
        out_shape=jax.ShapeDtypeStruct(out, F32),
        in_specs=[pl.BlockSpec(memory_space=pltpu.VMEM)] * (2 + len(args)),
        out_specs=pl.BlockSpec(memory_space=pltpu.VMEM),
        scratch_shapes=[
            pltpu.VMEM((2, 2 * HALO + ROWS, ny, nz), F32), pltpu.VMEM((2 * n * ny, 2 * nz), jnp.bfloat16), ends, ends
        ]
        + ([] if first else [pltpu.VMEM((k, ny, nz), F32) for k in (COMPS * half + 2, COMPS * groups + 2)]),
        compiler_params=pltpu.CompilerParams(vmem_limit_bytes=16 * 2**20),
        cost_estimate=pl.CostEstimate(flops=10_000_000, bytes_accessed=10_000_000, transcendentals=0),
        name="sweeps_first" if first else "sweeps_second",
    )(*transforms(nz), *args)


def staged(x):
    def kernel(x_ref, out_ref):
        out_ref[...] = x_ref[...]

    vmem = pl.BlockSpec(memory_space=pltpu.VMEM)
    return pl.pallas_call(
        kernel,
        out_shape=jax.ShapeDtypeStruct(x.shape, F32),
        in_specs=[vmem],
        out_specs=vmem,
        compiler_params=pltpu.CompilerParams(vmem_limit_bytes=2 * 2**20),
        name="staged",
    )(x)


def shards(flow_state):
    fields = flow_state[0]
    ny, nz = fields.shape[2:]
    levels, blocks = lax.axis_size("level"), lax.axis_size("block")
    inner = [i for i in range(blocks - 1) if i % LINE != LINE - 1]
    ends = [i for i in range(blocks - 1) if i % LINE == LINE - 1]
    rise = [(i, i + 1) for i in inner]
    fall = [(i + 1, i) for i in inner if i % LINE != LINE - 2]
    last = [(i + 1, i) for i in inner if i % LINE == LINE - 2]
    swap = [(i, i + 1) for i in ends] + [(i + 1, i) for i in ends]
    finer = [(i, i + 1) for i in range(levels - 1)]
    coarser = [(i + 1, i) for i in range(levels - 1)]
    across = [(i, i + 1) for i in range(1, levels - 1, 2)] + [(i + 1, i) for i in range(1, levels - 1, 2)]
    within = [(i, i + 1) for i in range(0, levels - 1, 2)] + [(i + 1, i) for i in range(0, levels - 1, 2)]
    above = lax.ppermute(fields, "block", fall)
    below = lax.ppermute(fields, "block", rise)
    own = staged(fields)
    beyond = lax.ppermute(own, "block", swap)
    res1, down1, up1 = residuals(EARLY, own, above, below)
    got_down1 = lax.ppermute(down1, "level", coarser)
    got_up1 = lax.ppermute(up1, "level", finer)
    own, down1 = lax.optimization_barrier((own, down1))
    edge = lax.ppermute(own, "block", last)
    res0, down0, up0, far0, near0 = residuals(LATE, own, below, beyond, edge)
    got_far0 = lax.ppermute(far0, "level", across)
    got_near0 = lax.ppermute(near0, "level", within)
    res1, res0 = lax.optimization_barrier((res1, res0))
    part = sweeps(EARLY, fields.shape, res1, down1, up1, got_down1, got_up1)
    out = sweeps(LATE, fields.shape, res0, down0, up0, got_far0, got_near0, own, part)
    return out[None]


def solution(mesh):
    spec = P("level", None, "block", None, None)
    return jax.shard_map(shards, mesh=mesh, in_specs=(spec,), out_specs=spec, check_vma=False)
```

time: 52.2 us -> 49.1 us (0.941)
  the two profiles are of different devices: /device:TPU:23 before, /device:TPU:57 now
where the time goes in v4:
time: 49.1 us; the launch traced here: 48.8 us
  starting transfers between devices  36 us (73%)
  Pallas kernels  11.3 us (23%)
  local copies, waits for them, and re-layouts  1.01 us (2%)
    ppermute x1, starting transfers between devices, shards(): beyond = lax.ppermute(own, 'block', swap)  16.9 us
    pallas_call x2, Pallas kernels, sweeps(): pl.pallas_call(functools.partial(sweep_kernel, n), out_shape=jax.ShapeDty...  8.01 us
    ppermute x1, starting transfers between devices, shards(): got_near0 = lax.ppermute(near0, 'level', within)  7.46 us
    ppermute x1, starting transfers between devices, shards(): below = lax.ppermute(fields, 'block', rise)  4.64 us
    pallas_call x2, Pallas kernels, residuals(): pl.pallas_call(functools.partial(residual_kernel, n), out_shape=tuple((ja...  3.3 us
    ppermute x1, starting transfers between devices, shards(): got_down1 = lax.ppermute(down1, 'level', coarser)  2.88 us
    ppermute x1, starting transfers between devices, shards(): got_up1 = lax.ppermute(up1, 'level', finer)  1.42 us
    ppermute x1, starting transfers between devices, shards(): above = lax.ppermute(fields, 'block', fall)  1.28 us
  transfers between devices with their start and end apart: 8, of which 1 were waited for; matrix products, arithmetic and copies ran while one was open for 0% of the time, Pallas kernels for 15%

profile of v4, /device:TPU:57, one launch (start us, length us, event | category | flops | bytes accessed | tf_op | source)
XLA Modules:
  0.0 48.8 jit_solution(2069643454065592220)
XLA Ops:
  0.0 1.3 %collective-permute-start = (f32[5,8,16,128]{3,2,1,0:T(8,128)}, f32[5,8,16,128]{3,2,1,0:T(8,128)S(1)}, u32[]{:S(2)}, u32[]{:S(2)}) collective-permute-start(f32[5,8,16,128]{3,2,1,0:T(8,128)} %bitcast.2), channel_id=1, source_target_pairs={{1,0},{2,1},{3,2},{4,3},{5,4},{6,5},{7,6},{8,7},{9,8},{10,9},{11,1... | collective-permute-start | bytes 983048 | tf_op jit(solution)/shard_map/ppermute | solution.py:471
  1.3 4.6 %collective-permute-start.1 = (f32[5,8,16,128]{3,2,1,0:T(8,128)}, f32[5,8,16,128]{3,2,1,0:T(8,128)S(1)}, u32[]{:S(2)}, u32[]{:S(2)}) collective-permute-start(f32[5,8,16,128]{3,2,1,0:T(8,128)} %bitcast.3), channel_id=1, source_target_pairs={{0,1},{1,2},{2,3},{3,4},{4,5},{5,6},{6,7},{7,8},{8,9},{9,10},{10,1... | collective-permute-start | bytes 983048 | tf_op jit(solution)/shard_map/ppermute | solution.py:472
  5.9 0.0 copy-start.1
  6.0 1.0 %copy-done.1 = f32[1,5,8,16,128]{4,3,2,1,0:T(8,128)S(1)} copy-done((f32[1,5,8,16,128]{4,3,2,1,0:T(8,128)S(1)}, f32[1,5,8,16,128]{4,3,2,1,0:T(8,128)}, u32[]{:S(2)}) %copy-start.1) | copy-done | bytes 327704
  7.0 16.9 %collective-permute-start.2 = (f32[5,8,16,128]{3,2,1,0:T(8,128)S(1)}, f32[5,8,16,128]{3,2,1,0:T(8,128)S(1)}, u32[]{:S(2)}, u32[]{:S(2)}) collective-permute-start(f32[5,8,16,128]{3,2,1,0:T(8,128)S(1)} %staged.1.own_ref.refs_2_), channel_id=1, source_target_pairs={{15,16},{31,32},{47,48},{63,64},{79,80},{95,96},{111,112},{16,15},... | collective-permute-start | bytes 983048 | tf_op jit(solution)/shard_map/ppermute | solution.py:474
  23.9 0.0 collective-permute-done.refs_0_
  23.9 0.0 collective-permute-done.1.refs_1_.refs_0_
  23.9 2.1 %residual_first.1 = (f32[5,14,16,128]{3,2,1,0:T(8,128)S(1)}, f32[37,16,128]{2,1,0:T(8,128)S(1)}, f32[22,16,128]{2,1,0:T(8,128)S(1)}) custom-call(f32[5,8,16,128]{3,2,1,0:T(8,128)S(1)} %staged.1.own_ref.refs_2_, f32[5,8,16,128]{3,2,1,0:T(8,128)S(1)} %collective-permute-done.refs_0_, f32[5,8,16,128]{3,2,1,0:T(8,128)S(1)} %collective-permute-done.1.refs_1_.refs_0_), custom_call_target="tpu_custom_call" | custom-call | flops 2000000 | bytes 2000000 | tf_op jit(solution)/shard_map/residual_first/pallas_call | solution.py:251
  26.1 0.7 %collective-permute-start.3 = (f32[5,8,16,128]{3,2,1,0:T(8,128)S(1)}, f32[5,8,16,128]{3,2,1,0:T(8,128)S(1)}, u32[]{:S(2)}, u32[]{:S(2)}) collective-permute-start(f32[5,8,16,128]{3,2,1,0:T(8,128)S(1)} %staged.1.own_ref.refs_2_), channel_id=1, source_target_pairs={{15,14},{31,30},{47,46},{63,62},{79,78},{95,94},{111,110},{127,126... | collective-permute-start | bytes 983048 | tf_op jit(solution)/shard_map/ppermute | solution.py:479
  26.7 2.9 %collective-permute-start.6 = (f32[37,16,128]{2,1,0:T(8,128)S(1)}, f32[37,16,128]{2,1,0:T(8,128)S(1)}, u32[]{:S(2)}, u32[]{:S(2)}) collective-permute-start(f32[37,16,128]{2,1,0:T(8,128)S(1)} %get-tuple-element.27.down_own), channel_id=1, source_target_pairs={{128,0},{256,128},{384,256},{512,384},{640,512},{768,640},{896,768... | collective-permute-start | bytes 909320 | tf_op jit(solution)/shard_map/ppermute | solution.py:476
  29.6 0.0 copy-start
  29.6 1.4 %collective-permute-start.7 = (f32[22,16,128]{2,1,0:T(8,128)S(1)}, f32[22,16,128]{2,1,0:T(8,128)S(1)}, u32[]{:S(2)}, u32[]{:S(2)}) collective-permute-start(f32[22,16,128]{2,1,0:T(8,128)S(1)} %get-tuple-element.28.up_own), channel_id=1, source_target_pairs={{0,128},{128,256},{256,384},{384,512},{512,640},{640,768},{768,896... | collective-permute-start | bytes 540680 | tf_op jit(solution)/shard_map/ppermute | solution.py:477
  31.1 0.3 collective-permute-done.2.refs_1_
  31.3 0.0 collective-permute-done.3.refs_2_
  31.3 1.2 %residual_second.1 = (f32[5,8,16,128]{3,2,1,0:T(8,128)S(1)}, f32[22,16,128]{2,1,0:T(8,128)S(1)}, f32[7,16,128]{2,1,0:T(8,128)S(1)}, f32[22,16,128]{2,1,0:T(8,128)S(1)}, f32[22,16,128]{2,1,0:T(8,128)S(1)}) custom-call(f32[5,8,16,128]{3,2,1,0:T(8,128)S(1)} %staged.1.own_ref.refs_2_, f32[5,8,16,128]{3,2,1,0:T(8,128)S(1)} %collective-permute-done.1.refs_1_.refs_0_, ...), custom_call_target="tpu_custom_call" | custom-call | flops 2000000 | bytes 2000000 | tf_op jit(solution)/shard_map/residual_second/pallas_call | solution.py:251
  32.5 0.0 copy-start.2
  32.5 0.7 %collective-permute-start.4 = (f32[22,16,128]{2,1,0:T(8,128)S(1)}, f32[22,16,128]{2,1,0:T(8,128)S(1)}, u32[]{:S(2)}, u32[]{:S(2)}) collective-permute-start(f32[22,16,128]{2,1,0:T(8,128)S(1)} %get-tuple-element.24), channel_id=1, source_target_pairs={{128,256},{384,512},{640,768},{256,128},{512,384},{768,640},{129,2... | collective-permute-start | bytes 540680 | tf_op jit(solution)/shard_map/ppermute | solution.py:481
  33.2 7.5 %collective-permute-start.5 = (f32[22,16,128]{2,1,0:T(8,128)S(1)}, f32[22,16,128]{2,1,0:T(8,128)S(1)}, u32[]{:S(2)}, u32[]{:S(2)}) collective-permute-start(f32[22,16,128]{2,1,0:T(8,128)S(1)} %get-tuple-element.25), channel_id=1, source_target_pairs={{0,128},{256,384},{512,640},{768,896},{128,0},{384,256},{640,512},... | collective-permute-start | bytes 540680 | tf_op jit(solution)/shard_map/ppermute | solution.py:482
  40.7 0.0 collective-permute-done.7.refs_1_
  40.7 0.0 collective-permute-done.6.refs_0_
  40.7 0.0 copy-done
  40.7 0.0 copy-done.2
  40.7 3.8 %sweeps_first.1.refs_3_ = f32[10,8,16,128]{3,2,1,0:T(8,128)S(1)} custom-call(bf16[2,256,256]{2,1,0:T(8,128)(2,1)S(1)} %copy-done, f32[8,128]{1,0:T(8,128)S(1)} %copy-done.2, f32[5,14,16,128]{3,2,1,0:T(8,128)S(1)} %get-tuple-element.26.res, f32[37,16,128]{2,1,0:T(8,128)S(1)} %get-tuple-element.27.down_own, f32[22,16,128]{2,1,0:T(8,128)S(1)} %get-tuple-element.28.up_own, ...), custom_call_target="tpu_custom_call" | custom-call | flops 10000000 | bytes 10000000 | tf_op jit(solution)/shard_map/sweeps_first/pallas_call | solution.py:427
  44.5 0.0 collective-permute-done.4.refs_0_
  44.5 0.0 collective-permute-done.5.refs_1_
  44.6 4.2 %sweeps_second.1 = f32[5,8,16,128]{3,2,1,0:T(8,128)} custom-call(bf16[2,256,256]{2,1,0:T(8,128)(2,1)S(1)} %copy-done, f32[8,128]{1,0:T(8,128)S(1)} %copy-done.2, f32[5,8,16,128]{3,2,1,0:T(8,128)S(1)} %get-tuple-element.21.res, f32[22,16,128]{2,1,0:T(8,128)S(1)} %get-tuple-element.22.down_own, f32[7,16,128]{2,1,0:T(8,128)S(1)} %get-tuple-element.23.up_own, ...), custom_call_target="tpu_custom_call" | custom-call | flops 10000000 | bytes 10000000 | tf_op jit(solution)/shard_map/sweeps_second/pallas_call | solution.py:427
  (1 shorter events, 0.0 us)
Async XLA Ops:
  0.0 23.9 %collective-permute-start = (f32[5,8,16,128]{3,2,1,0:T(8,128)}, f32[5,8,16,128]{3,2,1,0:T(8,128)S(1)}, u32[]{:S(2)}, u32[]{:S(2)}) collective-permute-start(f32[5,8,16,128]{3,2,1,0:T(8,128)} %bitcast.2), channel_id=1, source_target_pairs={{1,0},{2,1},{3,2},{4,3},{5,4},{6,5},{7,6},{8,7},{9,8},{10,9},{11,1... | collective-permute-start | bytes 983048 | tf_op jit(solution)/shard_map/ppermute | solution.py:471
  1.3 22.6 %collective-permute-start.1 = (f32[5,8,16,128]{3,2,1,0:T(8,128)}, f32[5,8,16,128]{3,2,1,0:T(8,128)S(1)}, u32[]{:S(2)}, u32[]{:S(2)}) collective-permute-start(f32[5,8,16,128]{3,2,1,0:T(8,128)} %bitcast.3), channel_id=1, source_target_pairs={{0,1},{1,2},{2,3},{3,4},{4,5},{5,6},{6,7},{7,8},{8,9},{9,10},{10,1... | collective-permute-start | bytes 983048 | tf_op jit(solution)/shard_map/ppermute | solution.py:472
  5.9 1.0 %copy-start.1 = (f32[1,5,8,16,128]{4,3,2,1,0:T(8,128)S(1)}, f32[1,5,8,16,128]{4,3,2,1,0:T(8,128)}, u32[]{:S(2)}) copy-start(f32[1,5,8,16,128]{4,3,2,1,0:T(8,128)} %param.5) | copy-start | bytes 983044
  7.0 24.4 %collective-permute-start.2 = (f32[5,8,16,128]{3,2,1,0:T(8,128)S(1)}, f32[5,8,16,128]{3,2,1,0:T(8,128)S(1)}, u32[]{:S(2)}, u32[]{:S(2)}) collective-permute-start(f32[5,8,16,128]{3,2,1,0:T(8,128)S(1)} %staged.1.own_ref.refs_2_), channel_id=1, source_target_pairs={{15,16},{31,32},{47,48},{63,64},{79,80},{95,96},{111,112},{16,15},... | collective-permute-start | bytes 983048 | tf_op jit(solution)/shard_map/ppermute | solution.py:474
  26.1 5.3 %collective-permute-start.3 = (f32[5,8,16,128]{3,2,1,0:T(8,128)S(1)}, f32[5,8,16,128]{3,2,1,0:T(8,128)S(1)}, u32[]{:S(2)}, u32[]{:S(2)}) collective-permute-start(f32[5,8,16,128]{3,2,1,0:T(8,128)S(1)} %staged.1.own_ref.refs_2_), channel_id=1, source_target_pairs={{15,14},{31,30},{47,46},{63,62},{79,78},{95,94},{111,110},{127,126... | collective-permute-start | bytes 983048 | tf_op jit(solution)/shard_map/ppermute | solution.py:479
  26.7 13.9 %collective-permute-start.6 = (f32[37,16,128]{2,1,0:T(8,128)S(1)}, f32[37,16,128]{2,1,0:T(8,128)S(1)}, u32[]{:S(2)}, u32[]{:S(2)}) collective-permute-start(f32[37,16,128]{2,1,0:T(8,128)S(1)} %get-tuple-element.27.down_own), channel_id=1, source_target_pairs={{128,0},{256,128},{384,256},{512,384},{640,512},{768,640},{896,768... | collective-permute-start | bytes 909320 | tf_op jit(solution)/shard_map/ppermute | solution.py:476
  29.6 11.1 %copy-start = (bf16[2,256,256]{2,1,0:T(8,128)(2,1)S(1)}, bf16[2,256,256]{2,1,0:T(8,128)(2,1)}, u32[]{:S(2)}) copy-start(bf16[2,256,256]{2,1,0:T(8,128)(2,1)} %constant.4.clone.w_ref) | copy-start | bytes 786436
  29.6 11.0 %collective-permute-start.7 = (f32[22,16,128]{2,1,0:T(8,128)S(1)}, f32[22,16,128]{2,1,0:T(8,128)S(1)}, u32[]{:S(2)}, u32[]{:S(2)}) collective-permute-start(f32[22,16,128]{2,1,0:T(8,128)S(1)} %get-tuple-element.28.up_own), channel_id=1, source_target_pairs={{0,128},{128,256},{256,384},{384,512},{512,640},{640,768},{768,896... | collective-permute-start | bytes 540680 | tf_op jit(solution)/shard_map/ppermute | solution.py:477
  32.5 8.2 %copy-start.2 = (f32[8,128]{1,0:T(8,128)S(1)}, f32[8,128]{1,0:T(8,128)}, u32[]{:S(2)}) copy-start(f32[8,128]{1,0:T(8,128)} %constant.5.clone.factor_ref) | copy-start | bytes 12292
  32.5 12.0 %collective-permute-start.4 = (f32[22,16,128]{2,1,0:T(8,128)S(1)}, f32[22,16,128]{2,1,0:T(8,128)S(1)}, u32[]{:S(2)}, u32[]{:S(2)}) collective-permute-start(f32[22,16,128]{2,1,0:T(8,128)S(1)} %get-tuple-element.24), channel_id=1, source_target_pairs={{128,256},{384,512},{640,768},{256,128},{512,384},{768,640},{129,2... | collective-permute-start | bytes 540680 | tf_op jit(solution)/shard_map/ppermute | solution.py:481
  33.2 11.3 %collective-permute-start.5 = (f32[22,16,128]{2,1,0:T(8,128)S(1)}, f32[22,16,128]{2,1,0:T(8,128)S(1)}, u32[]{:S(2)}, u32[]{:S(2)}) collective-permute-start(f32[22,16,128]{2,1,0:T(8,128)S(1)} %get-tuple-element.25), channel_id=1, source_target_pairs={{0,128},{256,384},{512,640},{768,896},{128,0},{384,256},{640,512},... | collective-permute-start | bytes 540680 | tf_op jit(solution)/shard_map/ppermute | solution.py:482

commit v5 on v4

--- a/solution.py
+++ b/solution.py
@@ -21,7 +21,7 @@
 EARLY = ROWS + HALO - 1
 F32 = jnp.float32
 UNROLL = 4
-FIRST_UP_TILES = 22
+FIRST_UP_TILES = 12
 
 
 def lanes(shape):
@@ -60,8 +60,7 @@
         row = np.concatenate([high, low], axis=1)
         return np.concatenate([row, row], axis=0)
 
-    factor = 2.0 * np.cos(np.pi * k / (nz + 1))
-    return jnp.asarray(np.stack([parts(sine), parts(back)])), jnp.asarray(np.tile(factor, (8, 1)), F32)
+    return jnp.asarray(np.stack([parts(sine), parts(back)]))
 
 
 def halved(x):
@@ -415,7 +414,7 @@
             out_ref[c, at] = u_ref[c, at] + (own[j] + lifted[j] * has_coarser)
         return carried
 
-    lax.fori_loop(0, COMPS, component, 0)
+    lax.fori_loop(0, COMPS, component, 0, unroll=COMPS)
 
 
 def sweeps(n, shape, *args):
@@ -427,31 +426,30 @@
     return pl.pallas_call(
         functools.partial(sweep_kernel, n),
         out_shape=jax.ShapeDtypeStruct(out, F32),
-        in_specs=[pl.BlockSpec(memory_space=pltpu.VMEM)] * (2 + len(args)),
+        in_specs=[pl.BlockSpec(memory_space=pltpu.VMEM)] * (1 + len(args)),
         out_specs=pl.BlockSpec(memory_space=pltpu.VMEM),
         scratch_shapes=[
             pltpu.VMEM((2, 2 * HALO + ROWS, ny, nz), F32), pltpu.VMEM((2 * n * ny, 2 * nz), jnp.bfloat16), ends, ends
         ]
         + ([] if first else [pltpu.VMEM((k, ny, nz), F32) for k in (COMPS * half + 2, COMPS * groups + 2)]),
         compiler_params=pltpu.CompilerParams(vmem_limit_bytes=16 * 2**20),
-        cost_estimate=pl.CostEstimate(flops=10_000_000, bytes_accessed=10_000_000, transcendentals=0),
+        cost_estimate=pl.CostEstimate(flops=10000000000, bytes_accessed=100000000, transcendentals=0),
         name="sweeps_first" if first else "sweeps_second",
-    )(*transforms(nz), *args)
-
-
-def staged(x):
-    def kernel(x_ref, out_ref):
-        out_ref[...] = x_ref[...]
-
-    vmem = pl.BlockSpec(memory_space=pltpu.VMEM)
+    )(transforms(nz), *args)
+
+
+def factors(nz):
+    def kernel(out_ref):
+        out_ref[...] = 2.0 * jnp.cos((np.pi / (nz + 1)) * (lanes((8, nz)) + 1).astype(F32))
+
     return pl.pallas_call(
         kernel,
-        out_shape=jax.ShapeDtypeStruct(x.shape, F32),
-        in_specs=[vmem],
-        out_specs=vmem,
+        out_shape=jax.ShapeDtypeStruct((8, nz), F32),
+        out_specs=pl.BlockSpec(memory_space=pltpu.VMEM),
         compiler_params=pltpu.CompilerParams(vmem_limit_bytes=2 * 2**20),
-        name="staged",
-    )(x)
+        cost_estimate=pl.CostEstimate(flops=10000000000, bytes_accessed=100000000, transcendentals=0),
+        name="factors",
+    )()
 
 
 def shards(flow_state):
@@ -470,19 +468,19 @@
     within = [(i, i + 1) for i in range(0, levels - 1, 2)] + [(i + 1, i) for i in range(0, levels - 1, 2)]
     above = lax.ppermute(fields, "block", fall)
     below = lax.ppermute(fields, "block", rise)
-    own = staged(fields)
-    beyond = lax.ppermute(own, "block", swap)
-    res1, down1, up1 = residuals(EARLY, own, above, below)
+    sent, factor = lax.optimization_barrier((fields, factors(nz)))
+    beyond = lax.ppermute(sent, "block", swap)
+    res1, down1, up1 = residuals(EARLY, fields, above, below)
     got_down1 = lax.ppermute(down1, "level", coarser)
     got_up1 = lax.ppermute(up1, "level", finer)
-    own, down1 = lax.optimization_barrier((own, down1))
+    own, down1 = lax.optimization_barrier((fields, down1))
     edge = lax.ppermute(own, "block", last)
     res0, down0, up0, far0, near0 = residuals(LATE, own, below, beyond, edge)
     got_far0 = lax.ppermute(far0, "level", across)
     got_near0 = lax.ppermute(near0, "level", within)
     res1, res0 = lax.optimization_barrier((res1, res0))
-    part = sweeps(EARLY, fields.shape, res1, down1, up1, got_down1, got_up1)
-    out = sweeps(LATE, fields.shape, res0, down0, up0, got_far0, got_near0, own, part)
+    part = sweeps(EARLY, fields.shape, factor, res1, down1, up1, got_down1, got_up1)
+    out = sweeps(LATE, fields.shape, factor, res0, down0, up0, got_far0, got_near0, own, part)
     return out[None]
 
 

time: 49.1 us -> 47 us (0.957)
  the two profiles are of different devices: /device:TPU:57 before, /device:TPU:23 now
where the time goes in v5:
time: 47 us; the launch traced here: 46.8 us
  starting transfers between devices  34 us (72%)
  Pallas kernels  9.67 us (21%)
  waiting for transfers between devices  2.95 us (6%)
    ppermute x1, starting transfers between devices, shards(): beyond = lax.ppermute(sent, 'block', swap)  14.2 us
    pallas_call x2, Pallas kernels, sweeps(): pl.pallas_call(functools.partial(sweep_kernel, n), out_shape=jax.ShapeDty...  6.31 us
    ppermute x1, starting transfers between devices, shards(): got_up1 = lax.ppermute(up1, 'level', finer)  5.46 us
    ppermute x1, starting transfers between devices, shards(): below = lax.ppermute(fields, 'block', rise)  4.64 us
    pallas_call x2, Pallas kernels, residuals(): pl.pallas_call(functools.partial(residual_kernel, n), out_shape=tuple((ja...  3.31 us
    ppermute x1, waiting for transfers between devices, shards(): got_far0 = lax.ppermute(far0, 'level', across)  2.93 us
    ppermute x1, starting transfers between devices, shards(): got_down1 = lax.ppermute(down1, 'level', coarser)  2.86 us
    ppermute x1, starting transfers between devices, shards(): got_far0 = lax.ppermute(far0, 'level', across)  2.76 us
  transfers between devices with their start and end apart: 8, of which 1 were waited for; matrix products, arithmetic and copies ran while one was open for 0% of the time, Pallas kernels for 14%

profile of v5, /device:TPU:23, one launch (start us, length us, event | category | flops | bytes accessed | tf_op | source)
XLA Modules:
  0.0 46.8 jit_solution(6099824946407056117)
XLA Ops:
  0.0 0.0 copy-start
  0.0 1.4 %collective-permute-start = (f32[5,8,16,128]{3,2,1,0:T(8,128)}, f32[5,8,16,128]{3,2,1,0:T(8,128)S(1)}, u32[]{:S(2)}, u32[]{:S(2)}) collective-permute-start(f32[5,8,16,128]{3,2,1,0:T(8,128)} %bitcast.2), channel_id=1, source_target_pairs={{1,0},{2,1},{3,2},{4,3},{5,4},{6,5},{7,6},{8,7},{9,8},{10,9},{11,1... | collective-permute-start | bytes 983048 | tf_op jit(solution)/shard_map/ppermute | solution.py:469
  1.4 4.6 %collective-permute-start.1 = (f32[5,8,16,128]{3,2,1,0:T(8,128)}, f32[5,8,16,128]{3,2,1,0:T(8,128)S(1)}, u32[]{:S(2)}, u32[]{:S(2)}) collective-permute-start(f32[5,8,16,128]{3,2,1,0:T(8,128)} %bitcast.3), channel_id=1, source_target_pairs={{0,1},{1,2},{2,3},{3,4},{4,5},{5,6},{6,7},{7,8},{8,9},{9,10},{10,1... | collective-permute-start | bytes 983048 | tf_op jit(solution)/shard_map/ppermute | solution.py:470
  6.1 0.0 copy-done
  6.1 14.2 %collective-permute-start.2 = (f32[5,8,16,128]{3,2,1,0:T(8,128)S(1)}, f32[5,8,16,128]{3,2,1,0:T(8,128)S(1)}, u32[]{:S(2)}, u32[]{:S(2)}) collective-permute-start(f32[5,8,16,128]{3,2,1,0:T(8,128)S(1)} %bitcast.4), channel_id=1, source_target_pairs={{15,16},{31,32},{47,48},{63,64},{79,80},{95,96},{111,112},{16,15},... | collective-permute-start | bytes 983048 | tf_op jit(solution)/shard_map/ppermute | solution.py:472
  20.4 0.0 collective-permute-done.refs_0_
  20.4 0.0 collective-permute-done.1.refs_1_.refs_0_
  20.4 2.1 %residual_first.1 = (f32[5,14,16,128]{3,2,1,0:T(8,128)S(1)}, f32[37,16,128]{2,1,0:T(8,128)S(1)}, f32[12,16,128]{2,1,0:T(8,128)S(1)}) custom-call(f32[5,8,16,128]{3,2,1,0:T(8,128)S(1)} %bitcast.5, f32[5,8,16,128]{3,2,1,0:T(8,128)S(1)} %collective-permute-done.refs_0_, f32[5,8,16,128]{3,2,1,0:T(8,128)S(1)} %collective-permute-done.1.refs_1_.refs_0_), custom_call_target="tpu_custom_call" | custom-call | flops 2000000 | bytes 2000000 | tf_op jit(solution)/shard_map/residual_first/pallas_call | solution.py:250
  22.5 0.7 %collective-permute-start.3 = (f32[5,8,16,128]{3,2,1,0:T(8,128)S(1)}, f32[5,8,16,128]{3,2,1,0:T(8,128)S(1)}, u32[]{:S(2)}, u32[]{:S(2)}) collective-permute-start(f32[5,8,16,128]{3,2,1,0:T(8,128)S(1)} %bitcast.6), channel_id=1, source_target_pairs={{15,14},{31,30},{47,46},{63,62},{79,78},{95,94},{111,110},{127,126... | collective-permute-start | bytes 983048 | tf_op jit(solution)/shard_map/ppermute | solution.py:477
  23.2 2.9 %collective-permute-start.6 = (f32[37,16,128]{2,1,0:T(8,128)S(1)}, f32[37,16,128]{2,1,0:T(8,128)S(1)}, u32[]{:S(2)}, u32[]{:S(2)}) collective-permute-start(f32[37,16,128]{2,1,0:T(8,128)S(1)} %get-tuple-element.31.down_own), channel_id=1, source_target_pairs={{128,0},{256,128},{384,256},{512,384},{640,512},{768,640},{896,768... | collective-permute-start | bytes 909320 | tf_op jit(solution)/shard_map/ppermute | solution.py:474
  26.1 0.0 copy-start.1
  26.1 5.5 %collective-permute-start.7 = (f32[12,16,128]{2,1,0:T(8,128)S(1)}, f32[12,16,128]{2,1,0:T(8,128)S(1)}, u32[]{:S(2)}, u32[]{:S(2)}) collective-permute-start(f32[12,16,128]{2,1,0:T(8,128)S(1)} %get-tuple-element.32.up_own), channel_id=1, source_target_pairs={{0,128},{128,256},{256,384},{384,512},{512,640},{640,768},{768,896... | collective-permute-start | bytes 294920 | tf_op jit(solution)/shard_map/ppermute | solution.py:475
  31.6 0.0 collective-permute-done.2.refs_1_
  31.6 0.0 collective-permute-done.3.refs_2_
  31.6 1.2 %residual_second.1 = (f32[5,8,16,128]{3,2,1,0:T(8,128)S(1)}, f32[22,16,128]{2,1,0:T(8,128)S(1)}, f32[7,16,128]{2,1,0:T(8,128)S(1)}, f32[22,16,128]{2,1,0:T(8,128)S(1)}, f32[22,16,128]{2,1,0:T(8,128)S(1)}) custom-call(f32[5,8,16,128]{3,2,1,0:T(8,128)S(1)} %bitcast.7, f32[5,8,16,128]{3,2,1,0:T(8,128)S(1)} %collective-permute-done.1.refs_1_.refs_0_, ...), custom_call_target="tpu_custom_call" | custom-call | flops 2000000 | bytes 2000000 | tf_op jit(solution)/shard_map/residual_second/pallas_call | solution.py:250
  32.8 2.8 %collective-permute-start.4 = (f32[22,16,128]{2,1,0:T(8,128)S(1)}, f32[22,16,128]{2,1,0:T(8,128)S(1)}, u32[]{:S(2)}, u32[]{:S(2)}) collective-permute-start(f32[22,16,128]{2,1,0:T(8,128)S(1)} %get-tuple-element.28), channel_id=1, source_target_pairs={{128,256},{384,512},{640,768},{256,128},{512,384},{768,640},{129,2... | collective-permute-start | bytes 540680 | tf_op jit(solution)/shard_map/ppermute | solution.py:479
  35.6 1.9 %collective-permute-start.5 = (f32[22,16,128]{2,1,0:T(8,128)S(1)}, f32[22,16,128]{2,1,0:T(8,128)S(1)}, u32[]{:S(2)}, u32[]{:S(2)}) collective-permute-start(f32[22,16,128]{2,1,0:T(8,128)S(1)} %get-tuple-element.29), channel_id=1, source_target_pairs={{0,128},{256,384},{512,640},{768,896},{128,0},{384,256},{640,512},... | collective-permute-start | bytes 540680 | tf_op jit(solution)/shard_map/ppermute | solution.py:480
  37.5 0.0 collective-permute-done.7.refs_1_
  37.5 0.0 collective-permute-done.6.refs_0_
  37.5 0.0 copy-done.1
  37.5 3.2 %sweeps_first.1.refs_3_ = f32[10,8,16,128]{3,2,1,0:T(8,128)S(1)} custom-call(bf16[2,256,256]{2,1,0:T(8,128)(2,1)S(1)} %copy-done.1, f32[8,128]{1,0:T(8,128)S(1)} %factors.1.factor_ref, f32[5,14,16,128]{3,2,1,0:T(8,128)S(1)} %get-tuple-element.30.res, f32[37,16,128]{2,1,0:T(8,128)S(1)} %get-tuple-element.31.down_own, ...), custom_call_target="tpu_custom_call" | custom-call | flops 10000000000 | bytes 100000000 | tf_op jit(solution)/shard_map/sweeps_first/pallas_call | solution.py:426
  40.7 2.9 %collective-permute-done.4.refs_0_ = f32[22,16,128]{2,1,0:T(8,128)S(1)} collective-permute-done((f32[22,16,128]{2,1,0:T(8,128)S(1)}, f32[22,16,128]{2,1,0:T(8,128)S(1)}, u32[]{:S(2)}, u32[]{:S(2)}) %collective-permute-start.4) | collective-permute-done | bytes 180256 | tf_op jit(solution)/shard_map/ppermute | solution.py:479
  43.6 0.0 collective-permute-done.5.refs_1_
  43.7 3.1 %sweeps_second.1 = f32[5,8,16,128]{3,2,1,0:T(8,128)} custom-call(bf16[2,256,256]{2,1,0:T(8,128)(2,1)S(1)} %copy-done.1, f32[8,128]{1,0:T(8,128)S(1)} %factors.1.factor_ref, f32[5,8,16,128]{3,2,1,0:T(8,128)S(1)} %get-tuple-element.25.res, f32[22,16,128]{2,1,0:T(8,128)S(1)} %get-tuple-element.26.down_own, f32[7,16,128]{2,1,0:T(8,128)S(1)} %get-tuple-element.27.up_own, ...), custom_call_target="tpu_custom_call" | custom-call | flops 10000000000 | bytes 100000000 | tf_op jit(solution)/shard_map/sweeps_second/pallas_call | solution.py:426
  (1 shorter events, 0.0 us)
Async XLA Ops:
  0.0 6.1 %copy-start = (f32[1,5,8,16,128]{4,3,2,1,0:T(8,128)S(1)}, f32[1,5,8,16,128]{4,3,2,1,0:T(8,128)}, u32[]{:S(2)}) copy-start(f32[1,5,8,16,128]{4,3,2,1,0:T(8,128)} %param.3) | copy-start | bytes 983044
  0.0 20.4 %collective-permute-start = (f32[5,8,16,128]{3,2,1,0:T(8,128)}, f32[5,8,16,128]{3,2,1,0:T(8,128)S(1)}, u32[]{:S(2)}, u32[]{:S(2)}) collective-permute-start(f32[5,8,16,128]{3,2,1,0:T(8,128)} %bitcast.2), channel_id=1, source_target_pairs={{1,0},{2,1},{3,2},{4,3},{5,4},{6,5},{7,6},{8,7},{9,8},{10,9},{11,1... | collective-permute-start | bytes 983048 | tf_op jit(solution)/shard_map/ppermute | solution.py:469
  1.4 19.0 %collective-permute-start.1 = (f32[5,8,16,128]{3,2,1,0:T(8,128)}, f32[5,8,16,128]{3,2,1,0:T(8,128)S(1)}, u32[]{:S(2)}, u32[]{:S(2)}) collective-permute-start(f32[5,8,16,128]{3,2,1,0:T(8,128)} %bitcast.3), channel_id=1, source_target_pairs={{0,1},{1,2},{2,3},{3,4},{4,5},{5,6},{6,7},{7,8},{8,9},{9,10},{10,1... | collective-permute-start | bytes 983048 | tf_op jit(solution)/shard_map/ppermute | solution.py:470
  6.1 25.4 %collective-permute-start.2 = (f32[5,8,16,128]{3,2,1,0:T(8,128)S(1)}, f32[5,8,16,128]{3,2,1,0:T(8,128)S(1)}, u32[]{:S(2)}, u32[]{:S(2)}) collective-permute-start(f32[5,8,16,128]{3,2,1,0:T(8,128)S(1)} %bitcast.4), channel_id=1, source_target_pairs={{15,16},{31,32},{47,48},{63,64},{79,80},{95,96},{111,112},{16,15},... | collective-permute-start | bytes 983048 | tf_op jit(solution)/shard_map/ppermute | solution.py:472
  22.5 9.1 %collective-permute-start.3 = (f32[5,8,16,128]{3,2,1,0:T(8,128)S(1)}, f32[5,8,16,128]{3,2,1,0:T(8,128)S(1)}, u32[]{:S(2)}, u32[]{:S(2)}) collective-permute-start(f32[5,8,16,128]{3,2,1,0:T(8,128)S(1)} %bitcast.6), channel_id=1, source_target_pairs={{15,14},{31,30},{47,46},{63,62},{79,78},{95,94},{111,110},{127,126... | collective-permute-start | bytes 983048 | tf_op jit(solution)/shard_map/ppermute | solution.py:477
  23.2 14.3 %collective-permute-start.6 = (f32[37,16,128]{2,1,0:T(8,128)S(1)}, f32[37,16,128]{2,1,0:T(8,128)S(1)}, u32[]{:S(2)}, u32[]{:S(2)}) collective-permute-start(f32[37,16,128]{2,1,0:T(8,128)S(1)} %get-tuple-element.31.down_own), channel_id=1, source_target_pairs={{128,0},{256,128},{384,256},{512,384},{640,512},{768,640},{896,768... | collective-permute-start | bytes 909320 | tf_op jit(solution)/shard_map/ppermute | solution.py:474
  26.1 11.4 %copy-start.1 = (bf16[2,256,256]{2,1,0:T(8,128)(2,1)S(1)}, bf16[2,256,256]{2,1,0:T(8,128)(2,1)}, u32[]{:S(2)}) copy-start(bf16[2,256,256]{2,1,0:T(8,128)(2,1)} %constant.2.clone.w_ref) | copy-start | bytes 786436
  26.1 11.4 %collective-permute-start.7 = (f32[12,16,128]{2,1,0:T(8,128)S(1)}, f32[12,16,128]{2,1,0:T(8,128)S(1)}, u32[]{:S(2)}, u32[]{:S(2)}) collective-permute-start(f32[12,16,128]{2,1,0:T(8,128)S(1)} %get-tuple-element.32.up_own), channel_id=1, source_target_pairs={{0,128},{128,256},{256,384},{384,512},{512,640},{640,768},{768,896... | collective-permute-start | bytes 294920 | tf_op jit(solution)/shard_map/ppermute | solution.py:475
  32.8 10.9 %collective-permute-start.4 = (f32[22,16,128]{2,1,0:T(8,128)S(1)}, f32[22,16,128]{2,1,0:T(8,128)S(1)}, u32[]{:S(2)}, u32[]{:S(2)}) collective-permute-start(f32[22,16,128]{2,1,0:T(8,128)S(1)} %get-tuple-element.28), channel_id=1, source_target_pairs={{128,256},{384,512},{640,768},{256,128},{512,384},{768,640},{129,2... | collective-permute-start | bytes 540680 | tf_op jit(solution)/shard_map/ppermute | solution.py:479
  35.6 8.1 %collective-permute-start.5 = (f32[22,16,128]{2,1,0:T(8,128)S(1)}, f32[22,16,128]{2,1,0:T(8,128)S(1)}, u32[]{:S(2)}, u32[]{:S(2)}) collective-permute-start(f32[22,16,128]{2,1,0:T(8,128)S(1)} %get-tuple-element.29), channel_id=1, source_target_pairs={{0,128},{256,384},{512,640},{768,896},{128,0},{384,256},{640,512},... | collective-permute-start | bytes 540680 | tf_op jit(solution)/shard_map/ppermute | solution.py:480

commit v6 on v5

--- a/solution.py
+++ b/solution.py
@@ -352,19 +352,17 @@
 
     def smooth(which):
         def target(i):
-            return t_ref[which, i, :h], t_ref[which, i, h:]
+            return tuple(t_ref[which, i, pl.ds(k, h, stride=2)] for k in range(2))
 
         rows = {offset + r: target(offset + r) for r in range(n)}
         for s in range(2, SWEEPS + 1):
             fresh = {}
             for i in range(s - 1, total - s + 1):
                 if i in rows:
-                    low, high = rows[i]
-                    low_up, high_up = pltpu.roll(low, 1, 0), pltpu.roll(high, 1, 0)
-                    low_dn, high_dn = pltpu.roll(low, h - 1, 0), pltpu.roll(high, h - 1, 0)
-                    n_low = jnp.where(sub1 == 0, 0.0, low_up) + jnp.where(sub1 == h - 1, high_dn, low_dn)
-                    n_high = jnp.where(sub1 == 0, low_up, high_up) + jnp.where(sub1 == h - 1, 0.0, high_dn)
-                    around = [(n_low + factor * low, n_high + factor * high)]
+                    even, odd = rows[i]
+                    n_even = odd + jnp.where(sub1 == 0, 0.0, pltpu.roll(odd, 1, 0))
+                    n_odd = even + jnp.where(sub1 == h - 1, 0.0, pltpu.roll(even, h - 1, 0))
+                    around = [(n_even + factor * even, n_odd + factor * odd)]
                 else:
                     around = []
                 beside = [rows[k] for k in (i - 1, i + 1) if k in rows]
@@ -376,7 +374,7 @@
                     new = [a + b for a, b in zip(target(i), new)]
                 fresh[i] = tuple(new)
             rows = fresh
-        return [jnp.concatenate(rows[HALO + j], axis=0) for j in range(ROWS)]
+        return [rows[HALO + j] for j in range(ROWS)]
 
     def component(c, carried):
         own_c, finer_c = own_ends[c], finer_ends[c]
@@ -401,12 +399,17 @@
         fine, coarse = smooth(0), smooth(1)
         if first:
             for j in range(ROWS):
-                part_ref[c, j] = fine[j]
-                part_ref[COMPS + c, j] = coarse[j]
+                for k in range(2):
+                    part_ref[c, j, k * h : (k + 1) * h] = fine[j][k]
+                    part_ref[COMPS + c, j, k * h : (k + 1) * h] = coarse[j][k]
             return carried
-        for j in range(ROWS):
-            lhs_ref[j * ny : (j + 1) * ny] = halved(fine[j] + earlier_ref[c, j])
-            lhs_ref[(ROWS + j) * ny : (ROWS + j + 1) * ny] = halved(coarse[j] + earlier_ref[COMPS + c, j])
+        for which, swept in enumerate((fine, coarse)):
+            for j in range(ROWS):
+                for k in range(2):
+                    before = earlier_ref[which * COMPS + c, j, k * h : (k + 1) * h]
+                    t_ref[which, j, pl.ds(k, h, stride=2)] = swept[j][k] + before
+                at = which * ROWS + j
+                lhs_ref[at * ny : (at + 1) * ny] = halved(t_ref[which, j])
         own = transformed(lhs_ref[: ROWS * ny], w_ref[0]).reshape(ROWS, ny, nz)
         lifted = transformed(lhs_ref[ROWS * ny : 2 * ROWS * ny], w_ref[1]).reshape(ROWS, ny, nz)
         for j in range(ROWS):

time: 47 us -> 46.9 us (level)
  Pallas kernels: 9.67 us -> 9.12 us
    pallas_call x2, Pallas kernels: 6.31 us -> 5.76 us  [sweeps(): pl.pallas_call(functools.partial(sweep_kernel, n), out_shape=jax.ShapeDty...]
  transfers between devices with their start and end apart: 8 -> 8, of which waited for: 1 -> 1; matrix products, arithmetic and copies ran while one was open for 0% -> 0% of each run, Pallas kernels for 14% -> 13%
where the time goes in v6:
time: 46.9 us; the launch traced here: 46.6 us
  starting transfers between devices  34 us (72%)
  Pallas kernels  9.12 us (19%)
  waiting for transfers between devices  3.35 us (7%)
    ppermute x1, starting transfers between devices, shards(): beyond = lax.ppermute(sent, 'block', swap)  14.2 us
    pallas_call x2, Pallas kernels, sweeps(): pl.pallas_call(functools.partial(sweep_kernel, n), out_shape=jax.ShapeDty...  5.76 us
    ppermute x1, starting transfers between devices, shards(): got_up1 = lax.ppermute(up1, 'level', finer)  5.46 us
    ppermute x1, starting transfers between devices, shards(): below = lax.ppermute(fields, 'block', rise)  4.64 us
    ppermute x1, waiting for transfers between devices, shards(): got_far0 = lax.ppermute(far0, 'level', across)  3.33 us
    pallas_call x2, Pallas kernels, residuals(): pl.pallas_call(functools.partial(residual_kernel, n), out_shape=tuple((ja...  3.31 us
    ppermute x1, starting transfers between devices, shards(): got_down1 = lax.ppermute(down1, 'level', coarser)  2.86 us
    ppermute x1, starting transfers between devices, shards(): got_far0 = lax.ppermute(far0, 'level', across)  2.76 us
  transfers between devices with their start and end apart: 8, of which 1 were waited for; matrix products, arithmetic and copies ran while one was open for 0% of the time, Pallas kernels for 13%

profile of v6, /device:TPU:23, one launch (start us, length us, event | category | flops | bytes accessed | tf_op | source)
XLA Modules:
  0.0 46.6 jit_solution(7895106130737816662)
XLA Ops:
  0.0 0.0 copy-start
  0.0 1.4 %collective-permute-start = (f32[5,8,16,128]{3,2,1,0:T(8,128)}, f32[5,8,16,128]{3,2,1,0:T(8,128)S(1)}, u32[]{:S(2)}, u32[]{:S(2)}) collective-permute-start(f32[5,8,16,128]{3,2,1,0:T(8,128)} %bitcast.2), channel_id=1, source_target_pairs={{1,0},{2,1},{3,2},{4,3},{5,4},{6,5},{7,6},{8,7},{9,8},{10,9},{11,1... | collective-permute-start | bytes 983048 | tf_op jit(solution)/shard_map/ppermute | solution.py:472
  1.4 4.6 %collective-permute-start.1 = (f32[5,8,16,128]{3,2,1,0:T(8,128)}, f32[5,8,16,128]{3,2,1,0:T(8,128)S(1)}, u32[]{:S(2)}, u32[]{:S(2)}) collective-permute-start(f32[5,8,16,128]{3,2,1,0:T(8,128)} %bitcast.3), channel_id=1, source_target_pairs={{0,1},{1,2},{2,3},{3,4},{4,5},{5,6},{6,7},{7,8},{8,9},{9,10},{10,1... | collective-permute-start | bytes 983048 | tf_op jit(solution)/shard_map/ppermute | solution.py:473
  6.1 0.0 copy-done
  6.1 14.2 %collective-permute-start.2 = (f32[5,8,16,128]{3,2,1,0:T(8,128)S(1)}, f32[5,8,16,128]{3,2,1,0:T(8,128)S(1)}, u32[]{:S(2)}, u32[]{:S(2)}) collective-permute-start(f32[5,8,16,128]{3,2,1,0:T(8,128)S(1)} %bitcast.4), channel_id=1, source_target_pairs={{15,16},{31,32},{47,48},{63,64},{79,80},{95,96},{111,112},{16,15},... | collective-permute-start | bytes 983048 | tf_op jit(solution)/shard_map/ppermute | solution.py:475
  20.4 0.0 collective-permute-done.refs_0_
  20.4 0.0 collective-permute-done.1.refs_1_.refs_0_
  20.4 2.1 %residual_first.1 = (f32[5,14,16,128]{3,2,1,0:T(8,128)S(1)}, f32[37,16,128]{2,1,0:T(8,128)S(1)}, f32[12,16,128]{2,1,0:T(8,128)S(1)}) custom-call(f32[5,8,16,128]{3,2,1,0:T(8,128)S(1)} %bitcast.5, f32[5,8,16,128]{3,2,1,0:T(8,128)S(1)} %collective-permute-done.refs_0_, f32[5,8,16,128]{3,2,1,0:T(8,128)S(1)} %collective-permute-done.1.refs_1_.refs_0_), custom_call_target="tpu_custom_call" | custom-call | flops 2000000 | bytes 2000000 | tf_op jit(solution)/shard_map/residual_first/pallas_call | solution.py:250
  22.5 0.7 %collective-permute-start.3 = (f32[5,8,16,128]{3,2,1,0:T(8,128)S(1)}, f32[5,8,16,128]{3,2,1,0:T(8,128)S(1)}, u32[]{:S(2)}, u32[]{:S(2)}) collective-permute-start(f32[5,8,16,128]{3,2,1,0:T(8,128)S(1)} %bitcast.6), channel_id=1, source_target_pairs={{15,14},{31,30},{47,46},{63,62},{79,78},{95,94},{111,110},{127,126... | collective-permute-start | bytes 983048 | tf_op jit(solution)/shard_map/ppermute | solution.py:480
  23.2 2.9 %collective-permute-start.6 = (f32[37,16,128]{2,1,0:T(8,128)S(1)}, f32[37,16,128]{2,1,0:T(8,128)S(1)}, u32[]{:S(2)}, u32[]{:S(2)}) collective-permute-start(f32[37,16,128]{2,1,0:T(8,128)S(1)} %get-tuple-element.31.down_own), channel_id=1, source_target_pairs={{128,0},{256,128},{384,256},{512,384},{640,512},{768,640},{896,768... | collective-permute-start | bytes 909320 | tf_op jit(solution)/shard_map/ppermute | solution.py:477
  26.1 0.0 copy-start.1
  26.1 5.5 %collective-permute-start.7 = (f32[12,16,128]{2,1,0:T(8,128)S(1)}, f32[12,16,128]{2,1,0:T(8,128)S(1)}, u32[]{:S(2)}, u32[]{:S(2)}) collective-permute-start(f32[12,16,128]{2,1,0:T(8,128)S(1)} %get-tuple-element.32.up_own), channel_id=1, source_target_pairs={{0,128},{128,256},{256,384},{384,512},{512,640},{640,768},{768,896... | collective-permute-start | bytes 294920 | tf_op jit(solution)/shard_map/ppermute | solution.py:478
  31.6 0.0 collective-permute-done.2.refs_1_
  31.6 0.0 collective-permute-done.3.refs_2_
  31.6 1.2 %residual_second.1 = (f32[5,8,16,128]{3,2,1,0:T(8,128)S(1)}, f32[22,16,128]{2,1,0:T(8,128)S(1)}, f32[7,16,128]{2,1,0:T(8,128)S(1)}, f32[22,16,128]{2,1,0:T(8,128)S(1)}, f32[22,16,128]{2,1,0:T(8,128)S(1)}) custom-call(f32[5,8,16,128]{3,2,1,0:T(8,128)S(1)} %bitcast.7, f32[5,8,16,128]{3,2,1,0:T(8,128)S(1)} %collective-permute-done.1.refs_1_.refs_0_, ...), custom_call_target="tpu_custom_call" | custom-call | flops 2000000 | bytes 2000000 | tf_op jit(solution)/shard_map/residual_second/pallas_call | solution.py:250
  32.8 2.8 %collective-permute-start.4 = (f32[22,16,128]{2,1,0:T(8,128)S(1)}, f32[22,16,128]{2,1,0:T(8,128)S(1)}, u32[]{:S(2)}, u32[]{:S(2)}) collective-permute-start(f32[22,16,128]{2,1,0:T(8,128)S(1)} %get-tuple-element.28), channel_id=1, source_target_pairs={{128,256},{384,512},{640,768},{256,128},{512,384},{768,640},{129,2... | collective-permute-start | bytes 540680 | tf_op jit(solution)/shard_map/ppermute | solution.py:482
  35.6 1.9 %collective-permute-start.5 = (f32[22,16,128]{2,1,0:T(8,128)S(1)}, f32[22,16,128]{2,1,0:T(8,128)S(1)}, u32[]{:S(2)}, u32[]{:S(2)}) collective-permute-start(f32[22,16,128]{2,1,0:T(8,128)S(1)} %get-tuple-element.29), channel_id=1, source_target_pairs={{0,128},{256,384},{512,640},{768,896},{128,0},{384,256},{640,512},... | collective-permute-start | bytes 540680 | tf_op jit(solution)/shard_map/ppermute | solution.py:483
  37.5 0.0 collective-permute-done.7.refs_1_
  37.5 0.0 collective-permute-done.6.refs_0_
  37.5 0.0 copy-done.1
  37.5 2.8 %sweeps_first.1.refs_3_ = f32[10,8,16,128]{3,2,1,0:T(8,128)S(1)} custom-call(bf16[2,256,256]{2,1,0:T(8,128)(2,1)S(1)} %copy-done.1, f32[8,128]{1,0:T(8,128)S(1)} %factors.1.factor_ref, f32[5,14,16,128]{3,2,1,0:T(8,128)S(1)} %get-tuple-element.30.res, f32[37,16,128]{2,1,0:T(8,128)S(1)} %get-tuple-element.31.down_own, ...), custom_call_target="tpu_custom_call" | custom-call | flops 10000000000 | bytes 100000000 | tf_op jit(solution)/shard_map/sweeps_first/pallas_call | solution.py:429
  40.3 3.3 %collective-permute-done.4.refs_0_ = f32[22,16,128]{2,1,0:T(8,128)S(1)} collective-permute-done((f32[22,16,128]{2,1,0:T(8,128)S(1)}, f32[22,16,128]{2,1,0:T(8,128)S(1)}, u32[]{:S(2)}, u32[]{:S(2)}) %collective-permute-start.4) | collective-permute-done | bytes 180256 | tf_op jit(solution)/shard_map/ppermute | solution.py:482
  43.6 0.0 collective-permute-done.5.refs_1_
  43.7 3.0 %sweeps_second.1 = f32[5,8,16,128]{3,2,1,0:T(8,128)} custom-call(bf16[2,256,256]{2,1,0:T(8,128)(2,1)S(1)} %copy-done.1, f32[8,128]{1,0:T(8,128)S(1)} %factors.1.factor_ref, f32[5,8,16,128]{3,2,1,0:T(8,128)S(1)} %get-tuple-element.25.res, f32[22,16,128]{2,1,0:T(8,128)S(1)} %get-tuple-element.26.down_own, f32[7,16,128]{2,1,0:T(8,128)S(1)} %get-tuple-element.27.up_own, ...), custom_call_target="tpu_custom_call" | custom-call | flops 10000000000 | bytes 100000000 | tf_op jit(solution)/shard_map/sweeps_second/pallas_call | solution.py:429
  (1 shorter events, 0.0 us)
Async XLA Ops:
  0.0 6.1 %copy-start = (f32[1,5,8,16,128]{4,3,2,1,0:T(8,128)S(1)}, f32[1,5,8,16,128]{4,3,2,1,0:T(8,128)}, u32[]{:S(2)}) copy-start(f32[1,5,8,16,128]{4,3,2,1,0:T(8,128)} %param.3) | copy-start | bytes 983044
  0.0 20.4 %collective-permute-start = (f32[5,8,16,128]{3,2,1,0:T(8,128)}, f32[5,8,16,128]{3,2,1,0:T(8,128)S(1)}, u32[]{:S(2)}, u32[]{:S(2)}) collective-permute-start(f32[5,8,16,128]{3,2,1,0:T(8,128)} %bitcast.2), channel_id=1, source_target_pairs={{1,0},{2,1},{3,2},{4,3},{5,4},{6,5},{7,6},{8,7},{9,8},{10,9},{11,1... | collective-permute-start | bytes 983048 | tf_op jit(solution)/shard_map/ppermute | solution.py:472
  1.4 19.0 %collective-permute-start.1 = (f32[5,8,16,128]{3,2,1,0:T(8,128)}, f32[5,8,16,128]{3,2,1,0:T(8,128)S(1)}, u32[]{:S(2)}, u32[]{:S(2)}) collective-permute-start(f32[5,8,16,128]{3,2,1,0:T(8,128)} %bitcast.3), channel_id=1, source_target_pairs={{0,1},{1,2},{2,3},{3,4},{4,5},{5,6},{6,7},{7,8},{8,9},{9,10},{10,1... | collective-permute-start | bytes 983048 | tf_op jit(solution)/shard_map/ppermute | solution.py:473
  6.1 25.4 %collective-permute-start.2 = (f32[5,8,16,128]{3,2,1,0:T(8,128)S(1)}, f32[5,8,16,128]{3,2,1,0:T(8,128)S(1)}, u32[]{:S(2)}, u32[]{:S(2)}) collective-permute-start(f32[5,8,16,128]{3,2,1,0:T(8,128)S(1)} %bitcast.4), channel_id=1, source_target_pairs={{15,16},{31,32},{47,48},{63,64},{79,80},{95,96},{111,112},{16,15},... | collective-permute-start | bytes 983048 | tf_op jit(solution)/shard_map/ppermute | solution.py:475
  22.5 9.1 %collective-permute-start.3 = (f32[5,8,16,128]{3,2,1,0:T(8,128)S(1)}, f32[5,8,16,128]{3,2,1,0:T(8,128)S(1)}, u32[]{:S(2)}, u32[]{:S(2)}) collective-permute-start(f32[5,8,16,128]{3,2,1,0:T(8,128)S(1)} %bitcast.6), channel_id=1, source_target_pairs={{15,14},{31,30},{47,46},{63,62},{79,78},{95,94},{111,110},{127,126... | collective-permute-start | bytes 983048 | tf_op jit(solution)/shard_map/ppermute | solution.py:480
  23.2 14.3 %collective-permute-start.6 = (f32[37,16,128]{2,1,0:T(8,128)S(1)}, f32[37,16,128]{2,1,0:T(8,128)S(1)}, u32[]{:S(2)}, u32[]{:S(2)}) collective-permute-start(f32[37,16,128]{2,1,0:T(8,128)S(1)} %get-tuple-element.31.down_own), channel_id=1, source_target_pairs={{128,0},{256,128},{384,256},{512,384},{640,512},{768,640},{896,768... | collective-permute-start | bytes 909320 | tf_op jit(solution)/shard_map/ppermute | solution.py:477
  26.1 11.4 %copy-start.1 = (bf16[2,256,256]{2,1,0:T(8,128)(2,1)S(1)}, bf16[2,256,256]{2,1,0:T(8,128)(2,1)}, u32[]{:S(2)}) copy-start(bf16[2,256,256]{2,1,0:T(8,128)(2,1)} %constant.2.clone.w_ref) | copy-start | bytes 786436
  26.1 11.4 %collective-permute-start.7 = (f32[12,16,128]{2,1,0:T(8,128)S(1)}, f32[12,16,128]{2,1,0:T(8,128)S(1)}, u32[]{:S(2)}, u32[]{:S(2)}) collective-permute-start(f32[12,16,128]{2,1,0:T(8,128)S(1)} %get-tuple-element.32.up_own), channel_id=1, source_target_pairs={{0,128},{128,256},{256,384},{384,512},{512,640},{640,768},{768,896... | collective-permute-start | bytes 294920 | tf_op jit(solution)/shard_map/ppermute | solution.py:478
  32.8 10.9 %collective-permute-start.4 = (f32[22,16,128]{2,1,0:T(8,128)S(1)}, f32[22,16,128]{2,1,0:T(8,128)S(1)}, u32[]{:S(2)}, u32[]{:S(2)}) collective-permute-start(f32[22,16,128]{2,1,0:T(8,128)S(1)} %get-tuple-element.28), channel_id=1, source_target_pairs={{128,256},{384,512},{640,768},{256,128},{512,384},{768,640},{129,2... | collective-permute-start | bytes 540680 | tf_op jit(solution)/shard_map/ppermute | solution.py:482
  35.6 8.1 %collective-permute-start.5 = (f32[22,16,128]{2,1,0:T(8,128)S(1)}, f32[22,16,128]{2,1,0:T(8,128)S(1)}, u32[]{:S(2)}, u32[]{:S(2)}) collective-permute-start(f32[22,16,128]{2,1,0:T(8,128)S(1)} %get-tuple-element.29), channel_id=1, source_target_pairs={{0,128},{256,384},{512,640},{768,896},{128,0},{384,256},{640,512},... | collective-permute-start | bytes 540680 | tf_op jit(solution)/shard_map/ppermute | solution.py:483

commit v7 on v6

--- a/solution.py
+++ b/solution.py
@@ -116,6 +116,11 @@
 
 def oriented(mirrored, j):
     return jnp.where(mirrored == 1, ROWS - 1 - j, j)
+
+
+def end_layout(n):
+    width = 32 if n == EARLY else 16
+    return width, 128 // width, -(-COMPS * width // 128)
 
 
 def residual_kernel(n, own_ref, *refs):
@@ -205,18 +210,19 @@
     low = face(q0, along(q0, v0, p0), jnp.abs(v0[0]) + s0, q1, along(q1, v1, p1), jnp.abs(v1[0]) + s1)
     lax.fori_loop(1, n + 1, row, (q1, v1, p1, s1, low), unroll=UNROLL)
     odd = lax.rem(lane, 2) == 1
-    ends, planes = [None, None], [None, None]
+    width, each, tiles = end_layout(n)
+    ends, planes = [None] * tiles, [None] * tiles
     for c in range(COMPS):
         pack = pack_ref[c]
         plane = jnp.where(odd, lane_roll(pack, 31), lane_roll(pack, 97))
-        k, shift = c // 4, 32 * (c % 4)
+        k, shift = c // each, width * (c % each)
         if shift == 0:
             ends[k], planes[k] = pack, plane
         else:
-            here = (lane >= shift - 1) & (lane < shift + 31)
+            here = (lane >= shift - 1) & (lane < shift + width - 1)
             ends[k] = jnp.where(here, lane_roll(pack, shift), ends[k])
             planes[k] = jnp.where(here, lane_roll(plane, shift), planes[k])
-    for k in range(2):
+    for k in range(tiles):
         down_ref[COMPS * half + k] = ends[k]
         up_ref[COMPS * groups + k] = planes[k]
     to_first, to_second = pairing(nz, nz // 4), pairing(nz, 3 * nz // 4)
@@ -242,7 +248,8 @@
     ny, nz = own.shape[2:]
     first = n == EARLY
     half, groups = n // 2, -(-n // 8)
-    down, up = COMPS * half + 2, COMPS * groups + 2
+    ends = end_layout(n)[2]
+    down, up = COMPS * half + ends, COMPS * groups + ends
     tiles = (down, FIRST_UP_TILES) if first else (down, up, down, down)
     shapes = [(COMPS, n, ny, nz)] + [(k, ny, nz) for k in tiles]
     scratch = [pltpu.VMEM((COMPS, 2 * ROWS, ny, nz), F32), pltpu.VMEM((COMPS, ny, nz), F32)]
@@ -259,12 +266,13 @@
     )(own, *halos)
 
 
-def end_faces(ends, planes, refinement):
+def end_faces(n, ends, planes, refinement):
     shape = ends[0].shape
     upper = lax.rem(lanes(shape), 2) == 1
 
     def parts(pack):
-        return [pack[0]] + [lane_roll(pack[0], 128 - 32 * c) for c in (1, 2, 3)] + [pack[1]]
+        width, each, _ = end_layout(n)
+        return [lane_roll(pack[c // each], 128 - width * (c % each)) if c % each else pack[c // each] for c in range(COMPS)]
 
     q, g = parts(ends), parts(planes)
     v, pressure, sound = primitives(q)
@@ -283,20 +291,21 @@
 
 def end_terms(n, flags, down_own, up_own, down_got, up_got, own_ref, finer_ref):
     level, refinement, top = flags
+    tiles = end_layout(n)[2]
     half, groups = n // 2, -(-n // 8)
-    ends = [down_own[COMPS * half + k] for k in range(2)]
-    planes = [up_own[COMPS * groups + k] for k in range(2)]
-    ends_finer = [jnp.where(top == 1, ends[k], down_got[COMPS * half + k]) for k in range(2)]
-    planes_coarser = [jnp.where(level == 0, ends[k], up_got[COMPS * groups + k]) for k in range(2)]
+    ends = [down_own[COMPS * half + k] for k in range(tiles)]
+    planes = [up_own[COMPS * groups + k] for k in range(tiles)]
+    ends_finer = [jnp.where(top == 1, ends[k], down_got[COMPS * half + k]) for k in range(tiles)]
+    planes_coarser = [jnp.where(level == 0, ends[k], up_got[COMPS * groups + k]) for k in range(tiles)]
     lane = lanes(ends[0].shape)
     near = (lane < 30) | (lane == lane.shape[-1] - 1)
 
     def halves(a):
         return 0.5 * jnp.where(lane < 64, lane_roll(a, 32), lane_roll(a, 96))
 
-    for c, a in enumerate(end_faces(ends, planes_coarser, refinement)):
+    for c, a in enumerate(end_faces(n, ends, planes_coarser, refinement)):
         own_ref[c] = jnp.where(near, a, halves(a))
-    for c, a in enumerate(end_faces(ends_finer, planes, 2.0 * refinement)):
+    for c, a in enumerate(end_faces(n, ends_finer, planes, 2.0 * refinement)):
         finer_ref[c] = halves(a)
 
 
@@ -434,7 +443,7 @@
         scratch_shapes=[
             pltpu.VMEM((2, 2 * HALO + ROWS, ny, nz), F32), pltpu.VMEM((2 * n * ny, 2 * nz), jnp.bfloat16), ends, ends
         ]
-        + ([] if first else [pltpu.VMEM((k, ny, nz), F32) for k in (COMPS * half + 2, COMPS * groups + 2)]),
+        + ([] if first else [pltpu.VMEM((k, ny, nz), F32) for k in (COMPS * half + end_layout(n)[2], COMPS * groups + end_layout(n)[2])]),
         compiler_params=pltpu.CompilerParams(vmem_limit_bytes=16 * 2**20),
         cost_estimate=pl.CostEstimate(flops=10000000000, bytes_accessed=100000000, transcendentals=0),
         name="sweeps_first" if first else "sweeps_second",

time: 46.9 us -> 46.7 us (level)
  no operation moved by 1% of the time
where the time goes in v7:
time: 46.7 us; the launch traced here: 46.4 us
  starting transfers between devices  34 us (73%)
  Pallas kernels  9.11 us (20%)
  waiting for transfers between devices  3.18 us (7%)
    ppermute x1, starting transfers between devices, shards(): beyond = lax.ppermute(sent, 'block', swap)  14.2 us
    pallas_call x2, Pallas kernels, sweeps(): pl.pallas_call(functools.partial(sweep_kernel, n), out_shape=jax.ShapeDty...  5.75 us
    ppermute x1, starting transfers between devices, shards(): got_up1 = lax.ppermute(up1, 'level', finer)  5.46 us
    ppermute x1, starting transfers between devices, shards(): below = lax.ppermute(fields, 'block', rise)  4.64 us
    pallas_call x2, Pallas kernels, residuals(): pl.pallas_call(functools.partial(residual_kernel, n), out_shape=tuple((ja...  3.31 us
    ppermute x1, waiting for transfers between devices, shards(): got_far0 = lax.ppermute(far0, 'level', across)  3.16 us
    ppermute x1, starting transfers between devices, shards(): got_down1 = lax.ppermute(down1, 'level', coarser)  2.86 us
    ppermute x1, starting transfers between devices, shards(): got_far0 = lax.ppermute(far0, 'level', across)  2.76 us
  transfers between devices with their start and end apart: 8, of which 1 were waited for; matrix products, arithmetic and copies ran while one was open for 0% of the time, Pallas kernels for 13%

profile of v7, /device:TPU:23, one launch (start us, length us, event | category | flops | bytes accessed | tf_op | source)
XLA Modules:
  0.0 46.4 jit_solution(8966683960844602579)
XLA Ops:
  0.0 0.0 copy-start
  0.0 1.4 %collective-permute-start = (f32[5,8,16,128]{3,2,1,0:T(8,128)}, f32[5,8,16,128]{3,2,1,0:T(8,128)S(1)}, u32[]{:S(2)}, u32[]{:S(2)}) collective-permute-start(f32[5,8,16,128]{3,2,1,0:T(8,128)} %bitcast.2), channel_id=1, source_target_pairs={{1,0},{2,1},{3,2},{4,3},{5,4},{6,5},{7,6},{8,7},{9,8},{10,9},{11,1... | collective-permute-start | bytes 983048 | tf_op jit(solution)/shard_map/ppermute | solution.py:481
  1.4 4.6 %collective-permute-start.1 = (f32[5,8,16,128]{3,2,1,0:T(8,128)}, f32[5,8,16,128]{3,2,1,0:T(8,128)S(1)}, u32[]{:S(2)}, u32[]{:S(2)}) collective-permute-start(f32[5,8,16,128]{3,2,1,0:T(8,128)} %bitcast.3), channel_id=1, source_target_pairs={{0,1},{1,2},{2,3},{3,4},{4,5},{5,6},{6,7},{7,8},{8,9},{9,10},{10,1... | collective-permute-start | bytes 983048 | tf_op jit(solution)/shard_map/ppermute | solution.py:482
  6.1 0.0 copy-done
  6.1 14.2 %collective-permute-start.2 = (f32[5,8,16,128]{3,2,1,0:T(8,128)S(1)}, f32[5,8,16,128]{3,2,1,0:T(8,128)S(1)}, u32[]{:S(2)}, u32[]{:S(2)}) collective-permute-start(f32[5,8,16,128]{3,2,1,0:T(8,128)S(1)} %bitcast.4), channel_id=1, source_target_pairs={{15,16},{31,32},{47,48},{63,64},{79,80},{95,96},{111,112},{16,15},... | collective-permute-start | bytes 983048 | tf_op jit(solution)/shard_map/ppermute | solution.py:484
  20.4 0.0 collective-permute-done.refs_0_
  20.4 0.0 collective-permute-done.1.refs_1_.refs_0_
  20.4 2.1 %residual_first.1 = (f32[5,14,16,128]{3,2,1,0:T(8,128)S(1)}, f32[37,16,128]{2,1,0:T(8,128)S(1)}, f32[12,16,128]{2,1,0:T(8,128)S(1)}) custom-call(f32[5,8,16,128]{3,2,1,0:T(8,128)S(1)} %bitcast.5, f32[5,8,16,128]{3,2,1,0:T(8,128)S(1)} %collective-permute-done.refs_0_, f32[5,8,16,128]{3,2,1,0:T(8,128)S(1)} %collective-permute-done.1.refs_1_.refs_0_), custom_call_target="tpu_custom_call" | custom-call | flops 2000000 | bytes 2000000 | tf_op jit(solution)/shard_map/residual_first/pallas_call | solution.py:257
  22.5 0.7 %collective-permute-start.3 = (f32[5,8,16,128]{3,2,1,0:T(8,128)S(1)}, f32[5,8,16,128]{3,2,1,0:T(8,128)S(1)}, u32[]{:S(2)}, u32[]{:S(2)}) collective-permute-start(f32[5,8,16,128]{3,2,1,0:T(8,128)S(1)} %bitcast.6), channel_id=1, source_target_pairs={{15,14},{31,30},{47,46},{63,62},{79,78},{95,94},{111,110},{127,126... | collective-permute-start | bytes 983048 | tf_op jit(solution)/shard_map/ppermute | solution.py:489
  23.2 2.9 %collective-permute-start.6 = (f32[37,16,128]{2,1,0:T(8,128)S(1)}, f32[37,16,128]{2,1,0:T(8,128)S(1)}, u32[]{:S(2)}, u32[]{:S(2)}) collective-permute-start(f32[37,16,128]{2,1,0:T(8,128)S(1)} %get-tuple-element.31.down_own), channel_id=1, source_target_pairs={{128,0},{256,128},{384,256},{512,384},{640,512},{768,640},{896,768... | collective-permute-start | bytes 909320 | tf_op jit(solution)/shard_map/ppermute | solution.py:486
  26.1 0.0 copy-start.1
  26.1 5.5 %collective-permute-start.7 = (f32[12,16,128]{2,1,0:T(8,128)S(1)}, f32[12,16,128]{2,1,0:T(8,128)S(1)}, u32[]{:S(2)}, u32[]{:S(2)}) collective-permute-start(f32[12,16,128]{2,1,0:T(8,128)S(1)} %get-tuple-element.32.up_own), channel_id=1, source_target_pairs={{0,128},{128,256},{256,384},{384,512},{512,640},{640,768},{768,896... | collective-permute-start | bytes 294920 | tf_op jit(solution)/shard_map/ppermute | solution.py:487
  31.6 0.0 collective-permute-done.2.refs_1_
  31.6 0.0 collective-permute-done.3.refs_2_
  31.6 1.2 %residual_second.1 = (f32[5,8,16,128]{3,2,1,0:T(8,128)S(1)}, f32[21,16,128]{2,1,0:T(8,128)S(1)}, f32[6,16,128]{2,1,0:T(8,128)S(1)}, f32[21,16,128]{2,1,0:T(8,128)S(1)}, f32[21,16,128]{2,1,0:T(8,128)S(1)}) custom-call(f32[5,8,16,128]{3,2,1,0:T(8,128)S(1)} %bitcast.7, f32[5,8,16,128]{3,2,1,0:T(8,128)S(1)} %collective-permute-done.1.refs_1_.refs_0_, ...), custom_call_target="tpu_custom_call" | custom-call | flops 2000000 | bytes 2000000 | tf_op jit(solution)/shard_map/residual_second/pallas_call | solution.py:257
  32.8 2.8 %collective-permute-start.4 = (f32[21,16,128]{2,1,0:T(8,128)S(1)}, f32[21,16,128]{2,1,0:T(8,128)S(1)}, u32[]{:S(2)}, u32[]{:S(2)}) collective-permute-start(f32[21,16,128]{2,1,0:T(8,128)S(1)} %get-tuple-element.28), channel_id=1, source_target_pairs={{128,256},{384,512},{640,768},{256,128},{512,384},{768,640},{129,2... | collective-permute-start | bytes 516104 | tf_op jit(solution)/shard_map/ppermute | solution.py:491
  35.6 1.9 %collective-permute-start.5 = (f32[21,16,128]{2,1,0:T(8,128)S(1)}, f32[21,16,128]{2,1,0:T(8,128)S(1)}, u32[]{:S(2)}, u32[]{:S(2)}) collective-permute-start(f32[21,16,128]{2,1,0:T(8,128)S(1)} %get-tuple-element.29), channel_id=1, source_target_pairs={{0,128},{256,384},{512,640},{768,896},{128,0},{384,256},{640,512},... | collective-permute-start | bytes 516104 | tf_op jit(solution)/shard_map/ppermute | solution.py:492
  37.5 0.0 collective-permute-done.7.refs_1_
  37.5 0.0 collective-permute-done.6.refs_0_
  37.5 0.0 copy-done.1
  37.5 2.8 %sweeps_first.1.refs_3_ = f32[10,8,16,128]{3,2,1,0:T(8,128)S(1)} custom-call(bf16[2,256,256]{2,1,0:T(8,128)(2,1)S(1)} %copy-done.1, f32[8,128]{1,0:T(8,128)S(1)} %factors.1.factor_ref, f32[5,14,16,128]{3,2,1,0:T(8,128)S(1)} %get-tuple-element.30.res, f32[37,16,128]{2,1,0:T(8,128)S(1)} %get-tuple-element.31.down_own, ...), custom_call_target="tpu_custom_call" | custom-call | flops 10000000000 | bytes 100000000 | tf_op jit(solution)/shard_map/sweeps_first/pallas_call | solution.py:438
  40.3 3.2 %collective-permute-done.4.refs_0_ = f32[21,16,128]{2,1,0:T(8,128)S(1)} collective-permute-done((f32[21,16,128]{2,1,0:T(8,128)S(1)}, f32[21,16,128]{2,1,0:T(8,128)S(1)}, u32[]{:S(2)}, u32[]{:S(2)}) %collective-permute-start.4) | collective-permute-done | bytes 172064 | tf_op jit(solution)/shard_map/ppermute | solution.py:491
  43.5 0.0 collective-permute-done.5.refs_1_
  43.5 3.0 %sweeps_second.1 = f32[5,8,16,128]{3,2,1,0:T(8,128)} custom-call(bf16[2,256,256]{2,1,0:T(8,128)(2,1)S(1)} %copy-done.1, f32[8,128]{1,0:T(8,128)S(1)} %factors.1.factor_ref, f32[5,8,16,128]{3,2,1,0:T(8,128)S(1)} %get-tuple-element.25.res, f32[21,16,128]{2,1,0:T(8,128)S(1)} %get-tuple-element.26.down_own, f32[6,16,128]{2,1,0:T(8,128)S(1)} %get-tuple-element.27.up_own, ...), custom_call_target="tpu_custom_call" | custom-call | flops 10000000000 | bytes 100000000 | tf_op jit(solution)/shard_map/sweeps_second/pallas_call | solution.py:438
  (1 shorter events, 0.0 us)
Async XLA Ops:
  0.0 6.1 %copy-start = (f32[1,5,8,16,128]{4,3,2,1,0:T(8,128)S(1)}, f32[1,5,8,16,128]{4,3,2,1,0:T(8,128)}, u32[]{:S(2)}) copy-start(f32[1,5,8,16,128]{4,3,2,1,0:T(8,128)} %param.3) | copy-start | bytes 983044
  0.0 20.4 %collective-permute-start = (f32[5,8,16,128]{3,2,1,0:T(8,128)}, f32[5,8,16,128]{3,2,1,0:T(8,128)S(1)}, u32[]{:S(2)}, u32[]{:S(2)}) collective-permute-start(f32[5,8,16,128]{3,2,1,0:T(8,128)} %bitcast.2), channel_id=1, source_target_pairs={{1,0},{2,1},{3,2},{4,3},{5,4},{6,5},{7,6},{8,7},{9,8},{10,9},{11,1... | collective-permute-start | bytes 983048 | tf_op jit(solution)/shard_map/ppermute | solution.py:481
  1.4 19.0 %collective-permute-start.1 = (f32[5,8,16,128]{3,2,1,0:T(8,128)}, f32[5,8,16,128]{3,2,1,0:T(8,128)S(1)}, u32[]{:S(2)}, u32[]{:S(2)}) collective-permute-start(f32[5,8,16,128]{3,2,1,0:T(8,128)} %bitcast.3), channel_id=1, source_target_pairs={{0,1},{1,2},{2,3},{3,4},{4,5},{5,6},{6,7},{7,8},{8,9},{9,10},{10,1... | collective-permute-start | bytes 983048 | tf_op jit(solution)/shard_map/ppermute | solution.py:482
  6.1 25.4 %collective-permute-start.2 = (f32[5,8,16,128]{3,2,1,0:T(8,128)S(1)}, f32[5,8,16,128]{3,2,1,0:T(8,128)S(1)}, u32[]{:S(2)}, u32[]{:S(2)}) collective-permute-start(f32[5,8,16,128]{3,2,1,0:T(8,128)S(1)} %bitcast.4), channel_id=1, source_target_pairs={{15,16},{31,32},{47,48},{63,64},{79,80},{95,96},{111,112},{16,15},... | collective-permute-start | bytes 983048 | tf_op jit(solution)/shard_map/ppermute | solution.py:484
  22.5 9.1 %collective-permute-start.3 = (f32[5,8,16,128]{3,2,1,0:T(8,128)S(1)}, f32[5,8,16,128]{3,2,1,0:T(8,128)S(1)}, u32[]{:S(2)}, u32[]{:S(2)}) collective-permute-start(f32[5,8,16,128]{3,2,1,0:T(8,128)S(1)} %bitcast.6), channel_id=1, source_target_pairs={{15,14},{31,30},{47,46},{63,62},{79,78},{95,94},{111,110},{127,126... | collective-permute-start | bytes 983048 | tf_op jit(solution)/shard_map/ppermute | solution.py:489
  23.2 14.3 %collective-permute-start.6 = (f32[37,16,128]{2,1,0:T(8,128)S(1)}, f32[37,16,128]{2,1,0:T(8,128)S(1)}, u32[]{:S(2)}, u32[]{:S(2)}) collective-permute-start(f32[37,16,128]{2,1,0:T(8,128)S(1)} %get-tuple-element.31.down_own), channel_id=1, source_target_pairs={{128,0},{256,128},{384,256},{512,384},{640,512},{768,640},{896,768... | collective-permute-start | bytes 909320 | tf_op jit(solution)/shard_map/ppermute | solution.py:486
  26.1 11.4 %copy-start.1 = (bf16[2,256,256]{2,1,0:T(8,128)(2,1)S(1)}, bf16[2,256,256]{2,1,0:T(8,128)(2,1)}, u32[]{:S(2)}) copy-start(bf16[2,256,256]{2,1,0:T(8,128)(2,1)} %constant.2.clone.w_ref) | copy-start | bytes 786436
  26.1 11.4 %collective-permute-start.7 = (f32[12,16,128]{2,1,0:T(8,128)S(1)}, f32[12,16,128]{2,1,0:T(8,128)S(1)}, u32[]{:S(2)}, u32[]{:S(2)}) collective-permute-start(f32[12,16,128]{2,1,0:T(8,128)S(1)} %get-tuple-element.32.up_own), channel_id=1, source_target_pairs={{0,128},{128,256},{256,384},{384,512},{512,640},{640,768},{768,896... | collective-permute-start | bytes 294920 | tf_op jit(solution)/shard_map/ppermute | solution.py:487
  32.8 10.7 %collective-permute-start.4 = (f32[21,16,128]{2,1,0:T(8,128)S(1)}, f32[21,16,128]{2,1,0:T(8,128)S(1)}, u32[]{:S(2)}, u32[]{:S(2)}) collective-permute-start(f32[21,16,128]{2,1,0:T(8,128)S(1)} %get-tuple-element.28), channel_id=1, source_target_pairs={{128,256},{384,512},{640,768},{256,128},{512,384},{768,640},{129,2... | collective-permute-start | bytes 516104 | tf_op jit(solution)/shard_map/ppermute | solution.py:491
  35.6 7.9 %collective-permute-start.5 = (f32[21,16,128]{2,1,0:T(8,128)S(1)}, f32[21,16,128]{2,1,0:T(8,128)S(1)}, u32[]{:S(2)}, u32[]{:S(2)}) collective-permute-start(f32[21,16,128]{2,1,0:T(8,128)S(1)} %get-tuple-element.29), channel_id=1, source_target_pairs={{0,128},{256,384},{512,640},{768,896},{128,0},{384,256},{640,512},... | collective-permute-start | bytes 516104 | tf_op jit(solution)/shard_map/ppermute | solution.py:492

commit v8 on v7

--- a/solution.py
+++ b/solution.py
@@ -225,11 +225,11 @@
     for k in range(tiles):
         down_ref[COMPS * half + k] = ends[k]
         up_ref[COMPS * groups + k] = planes[k]
-    to_first, to_second = pairing(nz, nz // 4), pairing(nz, 3 * nz // 4)
+    to_pair = jnp.concatenate([pairing(nz, nz // 4), pairing(nz, 3 * nz // 4)], axis=0)
     for c in range(COMPS):
         a = res_ref[c, :half].reshape(half * ny, nz)
         b = res_ref[c, half:].reshape(half * ny, nz)
-        packed = split_dot(a, to_first) + split_dot(b, to_second)
+        packed = split_dot(jnp.concatenate([a, b], axis=1), to_pair)
         down_ref[c * half : (c + 1) * half] = packed.reshape(half, ny, nz)
     if not first:
         odd_level = lax.rem(level, 2) == 1

time: 46.7 us -> 46.5 us (level)
  no operation moved by 1% of the time
where the time goes in v8:
time: 46.5 us; the launch traced here: 46.3 us
  starting transfers between devices  34.1 us (73%)
  Pallas kernels  8.94 us (19%)
  waiting for transfers between devices  3.07 us (7%)
    ppermute x1, starting transfers between devices, shards(): beyond = lax.ppermute(sent, 'block', swap)  14.2 us
    pallas_call x2, Pallas kernels, sweeps(): pl.pallas_call(functools.partial(sweep_kernel, n), out_shape=jax.ShapeDty...  5.75 us
    ppermute x1, starting transfers between devices, shards(): got_up1 = lax.ppermute(up1, 'level', finer)  5.46 us
    ppermute x1, starting transfers between devices, shards(): below = lax.ppermute(fields, 'block', rise)  4.64 us
    pallas_call x2, Pallas kernels, residuals(): pl.pallas_call(functools.partial(residual_kernel, n), out_shape=tuple((ja...  3.14 us
    ppermute x1, waiting for transfers between devices, shards(): got_far0 = lax.ppermute(far0, 'level', across)  3.05 us
    ppermute x1, starting transfers between devices, shards(): got_far0 = lax.ppermute(far0, 'level', across)  2.87 us
    ppermute x1, starting transfers between devices, shards(): got_down1 = lax.ppermute(down1, 'level', coarser)  2.86 us
  transfers between devices with their start and end apart: 8, of which 1 were waited for; matrix products, arithmetic and copies ran while one was open for 0% of the time, Pallas kernels for 13%

profile of v8, /device:TPU:23, one launch (start us, length us, event | category | flops | bytes accessed | tf_op | source)
XLA Modules:
  0.0 46.3 jit_solution(10067093154065544174)
XLA Ops:
  0.0 0.0 copy-start
  0.0 1.4 %collective-permute-start = (f32[5,8,16,128]{3,2,1,0:T(8,128)}, f32[5,8,16,128]{3,2,1,0:T(8,128)S(1)}, u32[]{:S(2)}, u32[]{:S(2)}) collective-permute-start(f32[5,8,16,128]{3,2,1,0:T(8,128)} %bitcast.2), channel_id=1, source_target_pairs={{1,0},{2,1},{3,2},{4,3},{5,4},{6,5},{7,6},{8,7},{9,8},{10,9},{11,1... | collective-permute-start | bytes 983048 | tf_op jit(solution)/shard_map/ppermute | solution.py:481
  1.4 4.6 %collective-permute-start.1 = (f32[5,8,16,128]{3,2,1,0:T(8,128)}, f32[5,8,16,128]{3,2,1,0:T(8,128)S(1)}, u32[]{:S(2)}, u32[]{:S(2)}) collective-permute-start(f32[5,8,16,128]{3,2,1,0:T(8,128)} %bitcast.3), channel_id=1, source_target_pairs={{0,1},{1,2},{2,3},{3,4},{4,5},{5,6},{6,7},{7,8},{8,9},{9,10},{10,1... | collective-permute-start | bytes 983048 | tf_op jit(solution)/shard_map/ppermute | solution.py:482
  6.1 0.0 copy-done
  6.1 14.2 %collective-permute-start.2 = (f32[5,8,16,128]{3,2,1,0:T(8,128)S(1)}, f32[5,8,16,128]{3,2,1,0:T(8,128)S(1)}, u32[]{:S(2)}, u32[]{:S(2)}) collective-permute-start(f32[5,8,16,128]{3,2,1,0:T(8,128)S(1)} %bitcast.4), channel_id=1, source_target_pairs={{15,16},{31,32},{47,48},{63,64},{79,80},{95,96},{111,112},{16,15},... | collective-permute-start | bytes 983048 | tf_op jit(solution)/shard_map/ppermute | solution.py:484
  20.4 0.0 collective-permute-done.refs_0_
  20.4 0.0 collective-permute-done.1.refs_1_.refs_0_
  20.4 2.0 %residual_first.1 = (f32[5,14,16,128]{3,2,1,0:T(8,128)S(1)}, f32[37,16,128]{2,1,0:T(8,128)S(1)}, f32[12,16,128]{2,1,0:T(8,128)S(1)}) custom-call(f32[5,8,16,128]{3,2,1,0:T(8,128)S(1)} %bitcast.5, f32[5,8,16,128]{3,2,1,0:T(8,128)S(1)} %collective-permute-done.refs_0_, f32[5,8,16,128]{3,2,1,0:T(8,128)S(1)} %collective-permute-done.1.refs_1_.refs_0_), custom_call_target="tpu_custom_call" | custom-call | flops 2000000 | bytes 2000000 | tf_op jit(solution)/shard_map/residual_first/pallas_call | solution.py:257
  22.4 0.7 %collective-permute-start.3 = (f32[5,8,16,128]{3,2,1,0:T(8,128)S(1)}, f32[5,8,16,128]{3,2,1,0:T(8,128)S(1)}, u32[]{:S(2)}, u32[]{:S(2)}) collective-permute-start(f32[5,8,16,128]{3,2,1,0:T(8,128)S(1)} %bitcast.6), channel_id=1, source_target_pairs={{15,14},{31,30},{47,46},{63,62},{79,78},{95,94},{111,110},{127,126... | collective-permute-start | bytes 983048 | tf_op jit(solution)/shard_map/ppermute | solution.py:489
  23.1 2.9 %collective-permute-start.6 = (f32[37,16,128]{2,1,0:T(8,128)S(1)}, f32[37,16,128]{2,1,0:T(8,128)S(1)}, u32[]{:S(2)}, u32[]{:S(2)}) collective-permute-start(f32[37,16,128]{2,1,0:T(8,128)S(1)} %get-tuple-element.31.down_own), channel_id=1, source_target_pairs={{128,0},{256,128},{384,256},{512,384},{640,512},{768,640},{896,768... | collective-permute-start | bytes 909320 | tf_op jit(solution)/shard_map/ppermute | solution.py:486
  26.0 0.0 copy-start.1
  26.0 5.5 %collective-permute-start.7 = (f32[12,16,128]{2,1,0:T(8,128)S(1)}, f32[12,16,128]{2,1,0:T(8,128)S(1)}, u32[]{:S(2)}, u32[]{:S(2)}) collective-permute-start(f32[12,16,128]{2,1,0:T(8,128)S(1)} %get-tuple-element.32.up_own), channel_id=1, source_target_pairs={{0,128},{128,256},{256,384},{384,512},{512,640},{640,768},{768,896... | collective-permute-start | bytes 294920 | tf_op jit(solution)/shard_map/ppermute | solution.py:487
  31.5 0.0 collective-permute-done.2.refs_1_
  31.5 0.0 collective-permute-done.3.refs_2_
  31.5 1.1 %residual_second.1 = (f32[5,8,16,128]{3,2,1,0:T(8,128)S(1)}, f32[21,16,128]{2,1,0:T(8,128)S(1)}, f32[6,16,128]{2,1,0:T(8,128)S(1)}, f32[21,16,128]{2,1,0:T(8,128)S(1)}, f32[21,16,128]{2,1,0:T(8,128)S(1)}) custom-call(f32[5,8,16,128]{3,2,1,0:T(8,128)S(1)} %bitcast.7, f32[5,8,16,128]{3,2,1,0:T(8,128)S(1)} %collective-permute-done.1.refs_1_.refs_0_, ...), custom_call_target="tpu_custom_call" | custom-call | flops 2000000 | bytes 2000000 | tf_op jit(solution)/shard_map/residual_second/pallas_call | solution.py:257
  32.6 2.9 %collective-permute-start.4 = (f32[21,16,128]{2,1,0:T(8,128)S(1)}, f32[21,16,128]{2,1,0:T(8,128)S(1)}, u32[]{:S(2)}, u32[]{:S(2)}) collective-permute-start(f32[21,16,128]{2,1,0:T(8,128)S(1)} %get-tuple-element.28), channel_id=1, source_target_pairs={{128,256},{384,512},{640,768},{256,128},{512,384},{768,640},{129,2... | collective-permute-start | bytes 516104 | tf_op jit(solution)/shard_map/ppermute | solution.py:491
  35.5 1.9 %collective-permute-start.5 = (f32[21,16,128]{2,1,0:T(8,128)S(1)}, f32[21,16,128]{2,1,0:T(8,128)S(1)}, u32[]{:S(2)}, u32[]{:S(2)}) collective-permute-start(f32[21,16,128]{2,1,0:T(8,128)S(1)} %get-tuple-element.29), channel_id=1, source_target_pairs={{0,128},{256,384},{512,640},{768,896},{128,0},{384,256},{640,512},... | collective-permute-start | bytes 516104 | tf_op jit(solution)/shard_map/ppermute | solution.py:492
  37.4 0.0 collective-permute-done.7.refs_1_
  37.4 0.0 collective-permute-done.6.refs_0_
  37.5 0.0 copy-done.1
  37.5 2.8 %sweeps_first.1.refs_3_ = f32[10,8,16,128]{3,2,1,0:T(8,128)S(1)} custom-call(bf16[2,256,256]{2,1,0:T(8,128)(2,1)S(1)} %copy-done.1, f32[8,128]{1,0:T(8,128)S(1)} %factors.1.factor_ref, f32[5,14,16,128]{3,2,1,0:T(8,128)S(1)} %get-tuple-element.30.res, f32[37,16,128]{2,1,0:T(8,128)S(1)} %get-tuple-element.31.down_own, ...), custom_call_target="tpu_custom_call" | custom-call | flops 10000000000 | bytes 100000000 | tf_op jit(solution)/shard_map/sweeps_first/pallas_call | solution.py:438
  40.3 3.0 %collective-permute-done.4.refs_0_ = f32[21,16,128]{2,1,0:T(8,128)S(1)} collective-permute-done((f32[21,16,128]{2,1,0:T(8,128)S(1)}, f32[21,16,128]{2,1,0:T(8,128)S(1)}, u32[]{:S(2)}, u32[]{:S(2)}) %collective-permute-start.4) | collective-permute-done | bytes 172064 | tf_op jit(solution)/shard_map/ppermute | solution.py:491
  43.3 0.0 collective-permute-done.5.refs_1_
  43.3 3.0 %sweeps_second.1 = f32[5,8,16,128]{3,2,1,0:T(8,128)} custom-call(bf16[2,256,256]{2,1,0:T(8,128)(2,1)S(1)} %copy-done.1, f32[8,128]{1,0:T(8,128)S(1)} %factors.1.factor_ref, f32[5,8,16,128]{3,2,1,0:T(8,128)S(1)} %get-tuple-element.25.res, f32[21,16,128]{2,1,0:T(8,128)S(1)} %get-tuple-element.26.down_own, f32[6,16,128]{2,1,0:T(8,128)S(1)} %get-tuple-element.27.up_own, ...), custom_call_target="tpu_custom_call" | custom-call | flops 10000000000 | bytes 100000000 | tf_op jit(solution)/shard_map/sweeps_second/pallas_call | solution.py:438
  (1 shorter events, 0.0 us)
Async XLA Ops:
  0.0 6.1 %copy-start = (f32[1,5,8,16,128]{4,3,2,1,0:T(8,128)S(1)}, f32[1,5,8,16,128]{4,3,2,1,0:T(8,128)}, u32[]{:S(2)}) copy-start(f32[1,5,8,16,128]{4,3,2,1,0:T(8,128)} %param.3) | copy-start | bytes 983044
  0.0 20.4 %collective-permute-start = (f32[5,8,16,128]{3,2,1,0:T(8,128)}, f32[5,8,16,128]{3,2,1,0:T(8,128)S(1)}, u32[]{:S(2)}, u32[]{:S(2)}) collective-permute-start(f32[5,8,16,128]{3,2,1,0:T(8,128)} %bitcast.2), channel_id=1, source_target_pairs={{1,0},{2,1},{3,2},{4,3},{5,4},{6,5},{7,6},{8,7},{9,8},{10,9},{11,1... | collective-permute-start | bytes 983048 | tf_op jit(solution)/shard_map/ppermute | solution.py:481
  1.4 19.0 %collective-permute-start.1 = (f32[5,8,16,128]{3,2,1,0:T(8,128)}, f32[5,8,16,128]{3,2,1,0:T(8,128)S(1)}, u32[]{:S(2)}, u32[]{:S(2)}) collective-permute-start(f32[5,8,16,128]{3,2,1,0:T(8,128)} %bitcast.3), channel_id=1, source_target_pairs={{0,1},{1,2},{2,3},{3,4},{4,5},{5,6},{6,7},{7,8},{8,9},{9,10},{10,1... | collective-permute-start | bytes 983048 | tf_op jit(solution)/shard_map/ppermute | solution.py:482
  6.1 25.3 %collective-permute-start.2 = (f32[5,8,16,128]{3,2,1,0:T(8,128)S(1)}, f32[5,8,16,128]{3,2,1,0:T(8,128)S(1)}, u32[]{:S(2)}, u32[]{:S(2)}) collective-permute-start(f32[5,8,16,128]{3,2,1,0:T(8,128)S(1)} %bitcast.4), channel_id=1, source_target_pairs={{15,16},{31,32},{47,48},{63,64},{79,80},{95,96},{111,112},{16,15},... | collective-permute-start | bytes 983048 | tf_op jit(solution)/shard_map/ppermute | solution.py:484
  22.4 9.1 %collective-permute-start.3 = (f32[5,8,16,128]{3,2,1,0:T(8,128)S(1)}, f32[5,8,16,128]{3,2,1,0:T(8,128)S(1)}, u32[]{:S(2)}, u32[]{:S(2)}) collective-permute-start(f32[5,8,16,128]{3,2,1,0:T(8,128)S(1)} %bitcast.6), channel_id=1, source_target_pairs={{15,14},{31,30},{47,46},{63,62},{79,78},{95,94},{111,110},{127,126... | collective-permute-start | bytes 983048 | tf_op jit(solution)/shard_map/ppermute | solution.py:489
  23.1 14.3 %collective-permute-start.6 = (f32[37,16,128]{2,1,0:T(8,128)S(1)}, f32[37,16,128]{2,1,0:T(8,128)S(1)}, u32[]{:S(2)}, u32[]{:S(2)}) collective-permute-start(f32[37,16,128]{2,1,0:T(8,128)S(1)} %get-tuple-element.31.down_own), channel_id=1, source_target_pairs={{128,0},{256,128},{384,256},{512,384},{640,512},{768,640},{896,768... | collective-permute-start | bytes 909320 | tf_op jit(solution)/shard_map/ppermute | solution.py:486
  26.0 11.5 %copy-start.1 = (bf16[2,256,256]{2,1,0:T(8,128)(2,1)S(1)}, bf16[2,256,256]{2,1,0:T(8,128)(2,1)}, u32[]{:S(2)}) copy-start(bf16[2,256,256]{2,1,0:T(8,128)(2,1)} %constant.2.clone.w_ref) | copy-start | bytes 786436
  26.0 11.4 %collective-permute-start.7 = (f32[12,16,128]{2,1,0:T(8,128)S(1)}, f32[12,16,128]{2,1,0:T(8,128)S(1)}, u32[]{:S(2)}, u32[]{:S(2)}) collective-permute-start(f32[12,16,128]{2,1,0:T(8,128)S(1)} %get-tuple-element.32.up_own), channel_id=1, source_target_pairs={{0,128},{128,256},{256,384},{384,512},{512,640},{640,768},{768,896... | collective-permute-start | bytes 294920 | tf_op jit(solution)/shard_map/ppermute | solution.py:487
  32.6 10.7 %collective-permute-start.4 = (f32[21,16,128]{2,1,0:T(8,128)S(1)}, f32[21,16,128]{2,1,0:T(8,128)S(1)}, u32[]{:S(2)}, u32[]{:S(2)}) collective-permute-start(f32[21,16,128]{2,1,0:T(8,128)S(1)} %get-tuple-element.28), channel_id=1, source_target_pairs={{128,256},{384,512},{640,768},{256,128},{512,384},{768,640},{129,2... | collective-permute-start | bytes 516104 | tf_op jit(solution)/shard_map/ppermute | solution.py:491
  35.5 7.8 %collective-permute-start.5 = (f32[21,16,128]{2,1,0:T(8,128)S(1)}, f32[21,16,128]{2,1,0:T(8,128)S(1)}, u32[]{:S(2)}, u32[]{:S(2)}) collective-permute-start(f32[21,16,128]{2,1,0:T(8,128)S(1)} %get-tuple-element.29), channel_id=1, source_target_pairs={{0,128},{256,384},{512,640},{768,896},{128,0},{384,256},{640,512},... | collective-permute-start | bytes 516104 | tf_op jit(solution)/shard_map/ppermute | solution.py:492
